TPU v7x, 256 devices: a whole 4x4x8 slice. The times are simulated.
256 devices in a mesh: ctx: 64 (over x, z_lo, y), dp: 4 (over z_hi, core).
Axes of the slice: x: 4, y: 4, z: 8 (z_hi: 2, z_lo: 4; z = z_hi * 4 + z_lo), core: 2. Of those that a mesh axis runs over, the one named last changes fastest.
Arguments:
- tokens: bfloat16 [4, 8192, 1536], P('dp', 'ctx'), may hold values from -6 to 6
- w_in: bfloat16 [1536, 2880], replicated, may hold values from -0.15625 to 0.15625
- conv_taps: float32 [7, 2880], replicated, may hold values from -2.4 to 2.4
- residues: float32 [960, 16], P('ctx'), may hold values from -1.5 to 1.5
- rates: float32 [960, 16], P('ctx'), may hold values from 3.6621094e-05 to 0.08
- cotangent: bfloat16 [4, 8192, 960], P('dp', 'ctx'), may hold values from -6 to 6
Outputs:
- output: bfloat16 [4, 8192, 960], P('dp', 'ctx')
- grad_tokens: bfloat16 [4, 8192, 1536], P('dp', 'ctx')
- grad_weight: bfloat16 [1536, 2880], P('ctx', 'dp')
- grad_taps: float32 [7, 2880], replicated
- grad_residues: float32 [960, 16], P('ctx')
All inputs are finite; a program needn't handle non-finite values.
Results may differ from a plain program's by a relative error of at most 0.02.
Values may be sent and summed in bfloat16 or wider, within the bound.
No kernel may reach another device: no remote copies, remote signals or barrier semaphores. Data moves between devices by JAX's collectives and lax.ppermute only.
A program may use at most 192 MiB of HBM per device.

v0:
```python
import math

import jax
import jax.numpy as jnp
from jax import lax
from jax.experimental import pallas as pl
from jax.experimental.pallas import tpu as pltpu
from jax.sharding import Mesh, PartitionSpec as P

F32 = jnp.float32
BF16 = jnp.bfloat16
HALO = 16
EXT = 136
SEG = 17
PADC = 1024
MODES = 16
NT = (((1,), (1,)), ((), ()))


def rounded(a):
    return a.astype(BF16).astype(F32)


KBLK = 256


def make_project(part):
    def project(*refs):
        if part == 0:
            tp, nexts, feats, wt, acc, tk, wbuf, tsem, sems = refs
        else:
            tp, nexts, before, feats, wt, zq, zk, zv, tk, wbuf, tsem, sems, acc = refs
        steps, chans, _ = wbuf.shape
        low = part * steps * KBLK
        arrival = pltpu.make_async_copy(feats.at[:, pl.ds(low, steps * KBLK)], tk, tsem)
        arrival.start()
        copies = [
            pltpu.make_async_copy(wt.at[:, pl.ds(low + k * KBLK, KBLK)], wbuf.at[k], sems.at[k])
            for k in range(steps)
        ]
        for copy in copies:
            copy.start()
        arrival.wait()
        for k in range(steps):
            wide = slice(low + k * KBLK, low + (k + 1) * KBLK)
            rows = jnp.concatenate(
                [tp[:, wide], tk[:, k * KBLK : (k + 1) * KBLK], nexts[:, wide]], axis=0
            )
            copies[k].wait()
            total = lax.dot_general(rows, wbuf[k], NT, preferred_element_type=F32)
            if k > 0:
                total = acc[...] + total
            elif part == 1:
                total = before[...] + total
            if part == 0 or k < steps - 1:
                acc[...] = total
            else:
                width = chans // 3
                for g, z in enumerate((zq, zk, zv)):
                    z[:, 0:width] = rounded(total[:, g * width : (g + 1) * width])
                    z[:, width:] = jnp.zeros((z.shape[0], PADC - width), F32)

    return project


def mix_taps(taps, zq, zk, zv, mq, mk, mv):
    def tile(ct, carry):
        lanes = pl.ds(pl.multiple_of(ct * 128, 128), 128)
        for g, (z, m) in enumerate(((zq, mq), (zk, mk), (zv, mv))):
            total = taps[g, 0:1, lanes] * z[pl.ds(HALO, EXT), lanes]
            for j in range(1, 7):
                total = total + taps[g, j : j + 1, lanes] * z[pl.ds(HALO - j, EXT), lanes]
            m[:, lanes] = total
        return carry

    lax.fori_loop(0, PADC // 128, tile, 0)


def one_minus_exp(x):
    series = jnp.ones_like(x)
    for n in range(13, 1, -1):
        series = 1.0 - series * x * (1.0 / n)
    return jnp.where(x < 0.5, x * series, 1.0 - jnp.exp(-x))


def prepare(
    feats, cott, rates, residues, conv, head, tail, block, taps, amp, cots,
    held, turn, cbuf, rbuf, sbuf, vbuf, sems,
):
    count = rates.shape[0]
    width, own = cott.shape
    depth = feats.shape[1]
    copies = [
        pltpu.make_async_copy(rates, rbuf, sems.at[0]),
        pltpu.make_async_copy(residues, sbuf, sems.at[1]),
        pltpu.make_async_copy(cott, cbuf, sems.at[2]),
        pltpu.make_async_copy(conv, vbuf, sems.at[3]),
        pltpu.make_async_copy(feats.at[pl.ds(0, HALO)], head.at[:, pl.ds(0, depth)], sems.at[4]),
        pltpu.make_async_copy(feats.at[pl.ds(own - HALO, HALO)], tail, sems.at[5]),
    ]
    for copy in copies:
        copy.start()
    held[...] = jnp.zeros(held.shape, F32)
    turn[...] = jnp.zeros(turn.shape, F32)
    taps[...] = jnp.zeros(taps.shape, F32)
    copies[0].wait()
    copies[1].wait()
    size = jnp.sqrt(one_minus_exp(2.0 * rbuf[...]))
    amp[...] = size
    held[0:count, 0:MODES] = rbuf[...]
    held[0:count, MODES : 2 * MODES] = sbuf[...] * size
    block[...] = held[...].T[0 : 2 * MODES, 0:count]
    copies[2].wait()
    turn[0:width, :] = cbuf[...].astype(F32)
    for c in range(PADC // 128):
        part = turn[c * 128 : (c + 1) * 128, :].T
        cots[:, c * 128 : (c + 1) * 128] = part
        head[:, depth + c * 128 : depth + (c + 1) * 128] = part[0:HALO].astype(BF16)
    copies[3].wait()
    for g in range(3):
        taps[g, 0:7, 0:width] = vbuf[:, g * width : (g + 1) * width]
    for copy in copies[4:]:
        copy.wait()


def placed(me, refs, held, goal):
    wide = refs[0].shape[1]
    total = None
    for d, ref in enumerate(refs):
        held[...] = jnp.zeros(held.shape, F32)
        held[:, 0:wide] = ref[...]
        part = pltpu.roll(held[...], lax.rem(me + (4 - d), 4) * wide, 1)
        total = part if total is None else total + part
    return total[:, 0:goal]


def join_params(me, r0, r1, r2, r3, out, held):
    out[...] = placed(me[0], (r0, r1, r2, r3), held, out.shape[1])


def end_states(me, r0, r1, r2, r3, mq, mk, mv, cown, nexts, cots, rates, gains, es, ends, endb, ut, dt, held):
    joined = placed(me[0], (r0, r1, r2, r3), held, PADC)
    rates[...] = joined[0:MODES]
    gains[...] = joined[MODES : 2 * MODES]
    sub = lax.broadcasted_iota(jnp.int32, (8, 128), 0)
    subf = sub.astype(F32)
    fdepth = jnp.where(sub == 7, 0.0, (EXT - 8 - SEG) - SEG * subf)
    bdepth = jnp.where(sub == 0, 0.0, SEG * subf - 8.0)

    def tile(ct, carry):
        lanes = pl.ds(pl.multiple_of(ct * 128, 128), 128)
        ut[...] = rounded(mk[:, lanes] * mv[:, lanes])
        lane = pl.multiple_of(nexts.shape[1] - PADC + ct * 128, 128)
        after = nexts[:, pl.ds(lane, 128)].astype(F32)
        cot = jnp.concatenate([cown[:, lanes], after[0 : EXT - 128]], axis=0)
        cots[:, lanes] = cot
        dt[...] = rounded(cot * mq[:, lanes])
        rate = rates[:, lanes]
        decay = jnp.exp(-rate)
        for half in range(2):
            ks = range(half * 8, half * 8 + 8)
            al = [jnp.broadcast_to(decay[k : k + 1, :], (8, 128)) for k in ks]
            rl = [jnp.broadcast_to(rate[k : k + 1, :], (8, 128)) for k in ks]
            st = [jnp.zeros((8, 128), F32)] * 8
            snap = st
            for t in range(SEG):
                uv = ut[pl.ds(t, 8, stride=SEG), :]
                st = [a * s + uv for a, s in zip(al, st)]
                if t == 8:
                    snap = st
            for i, k in enumerate(ks):
                es[0, k, :, lanes] = st[i]
                full = jnp.where(sub == 7, snap[i], st[i]) * jnp.exp(-rl[i] * fdepth)
                ends[k : k + 1, lanes] = jnp.sum(full, axis=0, keepdims=True)
            st = [jnp.zeros((8, 128), F32)] * 8
            for t in range(SEG - 1, -1, -1):
                dv = dt[pl.ds(t, 8, stride=SEG), :]
                st = [a * s + dv for a, s in zip(al, st)]
                if t == 8:
                    snap = st
            for i, k in enumerate(ks):
                es[1, k, :, lanes] = st[i]
                full = jnp.where(sub == 0, snap[i], st[i]) * jnp.exp(-rl[i] * bdepth)
                ends[MODES + k : MODES + k + 1, lanes] = jnp.sum(full, axis=0, keepdims=True)
        return carry

    lax.fori_loop(0, PADC // 128, tile, 0)
    endb[...] = ends[...].astype(BF16)


def make_level(span):
    def level(index, own, r1, r2, r3, rates, total, totalb, prefix):
        me = index[0]
        rate = rates[...] * float(span)
        before = jnp.zeros((MODES, PADC), F32)
        after = before
        whole_f = before
        whole_b = before
        for d, ref in enumerate((own, r1, r2, r3)):
            m = lax.rem(me + (4 - d), 4)
            f = ref[0:MODES, :].astype(F32)
            b = ref[MODES : 2 * MODES, :].astype(F32)
            whole_f = whole_f + f * jnp.exp(-rate * (3 - m).astype(F32))
            whole_b = whole_b + b * jnp.exp(-rate * m.astype(F32))
            if d > 0:
                gf = me - 1 - m
                gb = m - me - 1
                wf = jnp.exp(-rate * jnp.maximum(gf, 0).astype(F32))
                wb = jnp.exp(-rate * jnp.maximum(gb, 0).astype(F32))
                before = before + jnp.where(gf >= 0, 1.0, 0.0) * (wf * f)
                after = after + jnp.where(gb >= 0, 1.0, 0.0) * (wb * b)
        prefix[0:MODES, :] = before
        prefix[MODES : 2 * MODES, :] = after
        total[0:MODES, :] = whole_f
        total[MODES : 2 * MODES, :] = whole_b
        totalb[0:MODES, :] = whole_f.astype(BF16)
        totalb[MODES : 2 * MODES, :] = whole_b.astype(BF16)

    return level


def finish(
    zi, yi, zq, zk, zv, mq, mk, mv, es, py, pz, px, taps, rates, reff, cots,
    outt, dz, dzb, sumb, sums, inc, ut, dt, longs, dps, dms, dzt,
):
    own = dz.shape[1]
    rate = rates[...]
    for back in range(2):
        part = pl.ds(back * MODES, MODES)
        near, mid = yi[0], zi[0]
        if back:
            near, mid = 3 - near, 3 - mid
        far = pz[part, :] + jnp.exp(-rate * (4 * own * mid).astype(F32)) * px[part, :]
        inc[part, :] = py[part, :] + jnp.exp(-rate * (own * near).astype(F32)) * far
    sub = lax.broadcasted_iota(jnp.int32, (8, 128), 0)
    ut[...] = rounded(mk[...] * mv[...])
    dt[...] = rounded(cots[...] * mq[...])
    decay = jnp.exp(-rate)
    gain = reff[...]
    for half in range(2):
        ks = range(half * 8, half * 8 + 8)
        al = [jnp.broadcast_to(decay[k : k + 1, :], (8, 128)) for k in ks]
        gl = [jnp.broadcast_to(gain[k : k + 1, :], (8, 128)) for k in ks]
        rl = [jnp.broadcast_to(rate[k : k + 1, :], (8, 128)) for k in ks]
        fwd = []
        bwd = []
        for i, k in enumerate(ks):
            jump = [jnp.exp(-float(SEG * m) * rl[i]) for m in (1, 2, 4)]
            x = jnp.where(sub == 0, inc[k : k + 1, :], pltpu.roll(es[0, k], 1, 0))
            for m, d in zip((1, 2, 4), jump):
                x = x + jnp.where(sub >= m, pltpu.roll(x, m, 0) * d, 0.0)
            fwd.append(x)
            x = jnp.where(
                sub == 7, inc[MODES + k : MODES + k + 1, :], pltpu.roll(es[1, k], 7, 0)
            )
            for m, d in zip((1, 2, 4), jump):
                x = x + jnp.where(sub < 8 - m, pltpu.roll(x, 8 - m, 0) * d, 0.0)
            bwd.append(x)
        gr = [jnp.zeros((8, 128), F32)] * 8
        st = fwd
        for t in range(SEG):
            uv = ut[pl.ds(t, 8, stride=SEG), :]
            dv = dt[pl.ds(t, 8, stride=SEG), :]
            if t >= 9:
                dv = jnp.where(sub < 7, dv, 0.0)
            st = [a * s + uv for a, s in zip(al, st)]
            gr = [q + dv * s for q, s in zip(gr, st)]
            total = sum(g * s for g, s in zip(gl, st))
            if half:
                total = total + longs[pl.ds(t, 8, stride=SEG), :]
            longs[pl.ds(t, 8, stride=SEG), :] = total
        for i, k in enumerate(ks):
            sums[24 + k : 25 + k, :] = jnp.sum(gr[i], axis=0, keepdims=True)
        st = bwd
        for t in range(SEG - 1, -1, -1):
            dv = dt[pl.ds(t, 8, stride=SEG), :]
            st = [a * s + dv for a, s in zip(al, st)]
            total = sum(g * s for g, s in zip(gl, st))
            if half:
                total = total + dps[pl.ds(t, 8, stride=SEG), :]
            dps[pl.ds(t, 8, stride=SEG), :] = total
    long_out = rounded(longs[...])
    dprod = rounded(dps[...])
    outt[...] = (mq[0:own, :] * long_out[0:own]).T.astype(BF16)
    dms[0] = rounded(cots[...] * long_out)
    dms[1] = rounded(dprod * mv[...])
    dms[2] = rounded(dprod * mk[...])
    ct = pl.program_id(0)
    for g, zg in enumerate((zq, zk, zv)):
        mine = dms[g, 0:own, :]
        total = taps[g, 0:1, :] * mine
        sums[8 * g : 8 * g + 1, :] = jnp.sum(mine * zg[pl.ds(HALO, own), :], axis=0, keepdims=True)
        for j in range(1, 7):
            total = total + taps[g, j : j + 1, :] * dms[g, pl.ds(j, own), :]
            sums[8 * g + j : 8 * g + j + 1, :] = jnp.sum(
                mine * zg[pl.ds(HALO - j, own), :], axis=0, keepdims=True
            )
        sums[8 * g + 7 : 8 * g + 8, :] = jnp.zeros((1, 128), F32)
        dz[g] = total.astype(BF16)
        dzt[g, pl.ds(pl.multiple_of(ct * 128, 128), 128), :] = total.T

    sumb[...] = sums[...].astype(BF16)

    @pl.when(ct == pl.num_programs(0) - 1)
    def _():
        piece = dzb.shape[1] // 2
        width = 16 * piece // 3
        for b in range(8):
            both = []
            for h in range(2):
                off = h * 8 * piece + (b % 2) * 4 * piece + (b // 2) * piece
                g, low = off // width, off % width
                size = min(piece, width - low)
                both.append(dzt[g, low : low + size, :])
                if size < piece:
                    both.append(dzt[g + 1, 0 : piece - size, :])
            dzb[b] = jnp.concatenate(both, axis=0).astype(BF16)


def token_grads(dz, wt, out, acc):
    g = pl.program_id(0)
    part = jnp.dot(dz[0, :, 0 : wt.shape[0]], wt[...], preferred_element_type=F32)

    @pl.when(g == 0)
    def _():
        acc[...] = part

    @pl.when(g > 0)
    def _():
        acc[...] += part

    @pl.when(g == pl.num_programs(0) - 1)
    def _():
        out[...] = acc[...].astype(BF16)


def weight_term(xi, yi, ci, arrived, *refs):
    tokens, terms = refs[:8], refs[8:]
    me = yi[0]
    core = ci[0]
    chunk = terms[0].shape[1]
    slots = (me, lax.bitwise_xor(me, 1), 3 - me, lax.bitwise_xor(3 - me, 1))
    pairs = []
    for half, c in ((0, core), (1, 1 - core)):
        for p in (0, 2):
            left = [arrived[slots[p + i] * 2 + c] for i in range(2)]
            pairs.append((jnp.concatenate(left, axis=1), tokens[4 * half + p : 4 * half + p + 2]))
    for d, term in enumerate(terms):
        total = None
        cols = pl.ds(pl.multiple_of(lax.rem(xi[0] + d, 4) * chunk, 128), chunk)
        for left, (one, two) in pairs:
            right = jnp.concatenate([one[:, cols], two[:, cols]], axis=0)
            part = jnp.dot(left, right, preferred_element_type=F32)
            total = part if total is None else total + part
        term[...] = total.astype(BF16)


def split_rows(g0, g1, g2, g3, blocks, turn):
    chans = g0.shape[0]
    fblk = blocks.shape[1]
    piece = blocks.shape[2]
    turn[0:chans, :] = added((g0, g1, g2, g3))
    turn[chans:, :] = jnp.zeros((turn.shape[0] - chans, turn.shape[1]), F32)
    flipped = turn[...].T
    for q in range(16):
        for h in range(2):
            part = flipped[q * fblk : (q + 1) * fblk, h * piece : (h + 1) * piece]
            blocks[2 * q + h] = part.astype(BF16)


def added(refs):
    total = refs[0][...].astype(F32)
    for ref in refs[1:]:
        total = total + ref[...].astype(F32)
    return total


def add_parts(*refs):
    refs[-1][...] = added(refs[:-1]).astype(BF16)


def make_close_sums(scale):
    def close_sums(xi, zi, yi, amp, *refs):
        *parts, grad_taps, grad_res, held = refs
        total = added(parts) * scale
        width = grad_taps.shape[1] // 3
        for g in range(3):
            grad_taps[:, g * width : (g + 1) * width] = total[8 * g : 8 * g + 7, 0:width]
        count = grad_res.shape[0]
        index = (xi[0] * 4 + zi[0]) * 4 + yi[0]
        moved = pltpu.roll(total[24:40, :], lax.rem(PADC - index * count, PADC), 1)
        held[...] = jnp.zeros(held.shape, F32)
        held[0:MODES, :] = moved[:, 0:128]
        grad_res[...] = held[...].T[0:count, 0:MODES] * amp[...]

    return close_sums


def make_close(scale):
    def close_weight(last, out):
        fblk, piece = last.shape[1:]
        for y in range(4):
            total = jnp.zeros((fblk, piece), F32)
            for z in range(4):
                for h in range(2):
                    total = total + last[(z * 4 + y) * 2 + h].astype(F32)
            out[:, y * piece : (y + 1) * piece] = (total * scale).astype(BF16)

    return close_weight


def ring(a, ax, d):
    return lax.ppermute(a, ax, [(i, (i + d) % 4) for i in range(4)])


def params(mb):
    return pltpu.CompilerParams(vmem_limit_bytes=int(mb * 1024 * 1024))


def local(tokens, w_in, conv_taps, residues, rates, cotangent):
    feats = tokens[0]
    cot = cotangent[0]
    own, width = cot.shape
    depth = feats.shape[1]
    chans = 3 * width
    count = 64
    piece = chans // 16
    fblk = depth // count
    ctx = ("x", "zl", "y")
    scale = 1.0 / math.sqrt(4 * count * own)
    smem = pl.BlockSpec(memory_space=pltpu.SMEM)
    vm = pl.BlockSpec(memory_space=pltpu.VMEM)
    free = pl.BlockSpec()
    names = ("x", "zl", "y", "core")
    feats, cot, rates, *where = lax.optimization_barrier(
        (feats, cot, rates, *[lax.axis_index(n) for n in names])
    )
    xi, zi, yi, ci = [w.reshape(1) for w in where]
    anywhere = pl.BlockSpec(memory_space=pl.ANY)
    head, tail, block, taps, amp_mine, cown = pl.pallas_call(
        prepare,
        in_specs=[anywhere] * 5,
        out_specs=[vm] * 6,
        out_shape=[
            jax.ShapeDtypeStruct((HALO, depth + PADC), BF16),
            jax.ShapeDtypeStruct((HALO, depth), BF16),
            jax.ShapeDtypeStruct((2 * MODES, width // count), F32),
            jax.ShapeDtypeStruct((3, 8, PADC), F32),
            jax.ShapeDtypeStruct(rates.shape, F32),
            jax.ShapeDtypeStruct((own, PADC), F32),
        ],
        scratch_shapes=[
            pltpu.VMEM((128, 128), F32),
            pltpu.VMEM((PADC, own), F32),
            pltpu.VMEM((width, own), BF16),
            pltpu.VMEM(rates.shape, F32),
            pltpu.VMEM(rates.shape, F32),
            pltpu.VMEM(conv_taps.shape, F32),
            pltpu.SemaphoreType.DMA((6,)),
        ],
        compiler_params=params(54),
        name="prepare",
    )(feats, cot.T, rates, residues, conv_taps)
    tprev = lax.ppermute(tail, ctx, [(i, i + 1) for i in range(count - 1)])
    nexts = lax.ppermute(head, ctx, [(i, i - 1) for i in range(1, count)])
    ext_rows = own + 2 * HALO
    steps = depth // KBLK // 2

    def project(part, *before):
        many = 3 if part else 1
        shape = (ext_rows, PADC) if part else (ext_rows, chans)
        return pl.pallas_call(
            make_project(part),
            in_specs=[vm] * (2 + part) + [anywhere] * 2,
            out_specs=[vm] * many,
            out_shape=[jax.ShapeDtypeStruct(shape, F32)] * many,
            scratch_shapes=[
                pltpu.VMEM((own, steps * KBLK), BF16),
                pltpu.VMEM((steps, chans, KBLK), BF16),
                pltpu.SemaphoreType.DMA,
                pltpu.SemaphoreType.DMA((steps,)),
                *[pltpu.VMEM((ext_rows, chans), F32)] * part,
            ],
            compiler_params=params((52, 51)[part]),
            cost_estimate=pl.CostEstimate(flops=800000000, bytes_accessed=6000000, transcendentals=0),
            name="project",
        )(tprev, nexts, *before, feats, w_in.T)

    def mixed(*zs):
        return pl.pallas_call(
            mix_taps,
            in_specs=[vm] * 4,
            out_specs=[vm] * 3,
            out_shape=[jax.ShapeDtypeStruct((EXT, PADC), F32)] * 3,
            compiler_params=params(8),
            cost_estimate=pl.CostEstimate(flops=800000000, bytes_accessed=6000000, transcendentals=0),
            name="mix_taps",
        )(taps, *zs)

    held, each = block, width // count
    work = []
    for g, (me, ax) in enumerate(((yi, "y"), (zi, "zl"), (xi, "x"))):
        blocks = [held] + [ring(held, ax, d) for d in (1, 2, 3)]
        work = project(0) if g == 0 else project(1, *work) if g == 1 else mixed(*work)
        *blocks, last_work = lax.optimization_barrier((*blocks, work[-1]))
        work = [*work[:-1], last_work]
        if g == 1:
            zq, zk, zv = work
        if g == 2:
            break
        each = 4 * each
        held = pl.pallas_call(
            join_params,
            in_specs=[smem] + [vm] * 4,
            out_specs=vm,
            out_shape=jax.ShapeDtypeStruct((2 * MODES, each), F32),
            scratch_shapes=[pltpu.VMEM((2 * MODES, 256), F32)],
            compiler_params=params(4),
            name="join_params",
        )(me, *blocks)
    mq, mk, mv = work
    cots, rate, gain, es, ends, endb = pl.pallas_call(
        end_states,
        in_specs=[smem] + [vm] * 9,
        out_specs=[vm] * 6,
        out_shape=[
            jax.ShapeDtypeStruct((EXT, PADC), F32),
            jax.ShapeDtypeStruct((MODES, PADC), F32),
            jax.ShapeDtypeStruct((MODES, PADC), F32),
            jax.ShapeDtypeStruct((2, MODES, 8, PADC), F32),
            jax.ShapeDtypeStruct((2 * MODES, PADC), F32),
            jax.ShapeDtypeStruct((2 * MODES, PADC), BF16),
        ],
        scratch_shapes=[
            pltpu.VMEM((EXT, 128), F32),
            pltpu.VMEM((EXT, 128), F32),
            pltpu.VMEM((2 * MODES, PADC), F32),
        ],
        compiler_params=params(16),
        cost_estimate=pl.CostEstimate(flops=20000000, bytes_accessed=3000000, transcendentals=0),
        name="end_states",
    )(xi, *blocks, mq, mk, mv, cown, nexts)

    prefixes = []
    total, sent = ends, endb
    for me, ax, span in ((yi, "y", own), (zi, "zl", 4 * own), (xi, "x", 16 * own)):
        near = [ring(sent, ax, d) for d in (1, 2, 3)]
        total, sent, prefix = pl.pallas_call(
            make_level(span),
            in_specs=[smem] + [vm] * 5,
            out_specs=[vm] * 3,
            out_shape=[
                jax.ShapeDtypeStruct((2 * MODES, PADC), F32),
                jax.ShapeDtypeStruct((2 * MODES, PADC), BF16),
                jax.ShapeDtypeStruct((2 * MODES, PADC), F32),
            ],
            compiler_params=params(8),
            name="level",
        )(me, total, *near, rate)
        prefixes.append(prefix)
        if ax == "zl":
            mine, _ = lax.optimization_barrier((feats, sent))
            pair = lax.ppermute(mine, "y", [(i, i ^ 1) for i in range(4)])
            opposite = lax.ppermute(mine, "y", [(i, 3 - i) for i in range(4)])
    pair, opposite, prefixes[2] = lax.optimization_barrier((pair, opposite, prefixes[2]))
    far = lax.ppermute(pair, "y", [(i, 3 - i) for i in range(4)])

    def swapped(a):
        return lax.ppermute(a, "core", [(0, 1), (1, 0)])

    def tiles(shape):
        lead = len(shape) - 1
        return pl.BlockSpec(shape, lambda k: (0,) * lead + (k,))

    outt, dz, dzb, sums = pl.pallas_call(
        finish,
        grid=(PADC // 128,),
        in_specs=[
            smem,
            smem,
            *[tiles((ext_rows, 128))] * 3,
            *[tiles((EXT, 128))] * 3,
            tiles((2, MODES, 8, 128)),
            tiles((2 * MODES, 128)),
            tiles((2 * MODES, 128)),
            tiles((2 * MODES, 128)),
            tiles((3, 8, 128)),
            tiles((MODES, 128)),
            tiles((MODES, 128)),
            tiles((EXT, 128)),
        ],
        out_specs=[
            pl.BlockSpec((128, own), lambda k: (k, 0)),
            tiles((3, own, 128)),
            pl.BlockSpec((8, 2 * piece, own), lambda k: (0, 0, 0)),
            tiles((40, 128)),
        ],
        out_shape=[
            jax.ShapeDtypeStruct((width, own), BF16),
            jax.ShapeDtypeStruct((3, own, PADC), BF16),
            jax.ShapeDtypeStruct((8, 2 * piece, own), BF16),
            jax.ShapeDtypeStruct((40, PADC), BF16),
        ],
        scratch_shapes=[
            pltpu.VMEM((40, 128), F32),
            pltpu.VMEM((2 * MODES, 128), F32),
            pltpu.VMEM((EXT, 128), F32),
            pltpu.VMEM((EXT, 128), F32),
            pltpu.VMEM((EXT, 128), F32),
            pltpu.VMEM((EXT, 128), F32),
            pltpu.VMEM((3, EXT, 128), F32),
            pltpu.VMEM((3, PADC, own), F32),
        ],
        compiler_params=params(50),
        cost_estimate=pl.CostEstimate(flops=200000000, bytes_accessed=10000000, transcendentals=0),
        name="finish",
    )(zi, yi, zq, zk, zv, mq, mk, mv, es, *prefixes, taps, rate, gain, cots)
    output = outt.T
    blocks_of = [mine, pair, opposite, far]
    mine, pair, opposite, _ = lax.optimization_barrier((mine, pair, opposite, sums))
    blocks_of = [mine, pair, opposite, far]
    theirs = [swapped(a) for a in blocks_of]

    def spread(a, ax):
        return [a] + [ring(a, ax, d) for d in (1, 2, 3)]

    def swap(a, ax):
        return [a, lax.ppermute(a, ax, [(0, 1), (1, 0)])]

    def summed(parts):
        return pl.pallas_call(
            add_parts,
            in_specs=[free] * len(parts),
            out_specs=free,
            out_shape=jax.ShapeDtypeStruct((40, PADC), BF16),
            compiler_params=params(4),
            name="add_parts",
        )(*parts)

    arrived = lax.all_to_all(dzb, ("y", "core"), split_axis=0, concat_axis=0, tiled=True)
    sums = summed(swap(sums, "core"))
    *theirs, sums = lax.optimization_barrier((*theirs, sums))
    parts = spread(sums, "zl")
    grad_feats = pl.pallas_call(
        token_grads,
        grid=(3,),
        in_specs=[
            pl.BlockSpec((1, own, PADC), lambda g: (g, 0, 0)),
            pl.BlockSpec((width, depth), lambda g: (g, 0)),
        ],
        out_specs=pl.BlockSpec((own, depth), lambda g: (0, 0)),
        out_shape=jax.ShapeDtypeStruct((own, depth), BF16),
        scratch_shapes=[pltpu.VMEM((own, depth), F32)],
        compiler_params=params(57),
        cost_estimate=pl.CostEstimate(flops=1200000000, bytes_accessed=11000000, transcendentals=0),
        name="token_grads",
    )(dz, w_in.T)
    *parts, grad_feats = lax.optimization_barrier((*parts, grad_feats))
    sums = summed(parts)
    arrived, sums = lax.optimization_barrier((arrived, sums))
    terms = pl.pallas_call(
        weight_term,
        in_specs=[smem] * 3 + [vm] + [free] * 8,
        out_specs=[vm] * 4,
        out_shape=[jax.ShapeDtypeStruct((2 * piece, depth // 4), BF16)] * 4,
        compiler_params=params(24),
        cost_estimate=pl.CostEstimate(flops=1200000000, bytes_accessed=6000000, transcendentals=0),
        name="weight_term",
    )(xi, yi, ci, arrived, *blocks_of, *theirs)
    got = [terms[0]] + [ring(terms[d], "x", d) for d in (1, 2, 3)]
    sums, _ = lax.optimization_barrier((sums, terms[0]))
    sums = summed(swap(summed(spread(sums, "y")), "zh"))
    *got, sums = lax.optimization_barrier((*got, sums))
    blocks = pl.pallas_call(
        split_rows,
        in_specs=[vm] * 4,
        out_specs=vm,
        out_shape=jax.ShapeDtypeStruct((32, fblk, piece), BF16),
        scratch_shapes=[pltpu.VMEM((384, depth // 4), F32)],
        compiler_params=params(12),
        name="split_rows",
    )(*got)
    last = lax.all_to_all(blocks, ("zl", "y", "zh"), 0, 0, tiled=True)
    sums, _ = lax.optimization_barrier((sums, blocks))
    parts = spread(sums, "x")
    grad_taps, grad_residues = pl.pallas_call(
        make_close_sums(scale),
        in_specs=[smem] * 3 + [free] * 5,
        out_specs=[vm] * 2,
        out_shape=[
            jax.ShapeDtypeStruct((7, chans), F32),
            jax.ShapeDtypeStruct(rates.shape, F32),
        ],
        scratch_shapes=[pltpu.VMEM((128, 128), F32)],
        compiler_params=params(4),
        name="close_sums",
    )(xi, zi, yi, amp_mine, *parts)
    grad_weight = pl.pallas_call(
        make_close(scale),
        in_specs=[vm],
        out_specs=vm,
        out_shape=jax.ShapeDtypeStruct((fblk, 4 * piece), BF16),
        compiler_params=params(4),
        name="close_weight",
    )(last)
    return (output[None], grad_feats[None], grad_weight, grad_taps, grad_residues)


def solution(mesh):
    fine = Mesh(mesh.devices.reshape(4, 4, 4, 2, 2), ("x", "zl", "y", "zh", "core"))
    ctx = ("x", "zl", "y")
    dp = ("zh", "core")
    in_specs = (P(dp, ctx, None), P(), P(), P(ctx, None), P(ctx, None), P(dp, ctx, None))
    out_specs = (P(dp, ctx, None), P(dp, ctx, None), P(ctx, dp), P(), P(ctx, None))
    return jax.shard_map(local, mesh=fine, in_specs=in_specs, out_specs=out_specs, check_vma=False)
```

profile of v0, /device:TPU:32, one launch (start us, length us, event | category | flops | bytes accessed | tf_op | source)
XLA Modules:
  0.0 156.4 jit_solution(6462720272881812471)
XLA Ops:
  0.7 2.2 %prepare.1 = (bf16[16,2560]{1,0:T(8,128)(2,1)}, bf16[16,1536]{1,0:T(8,128)(2,1)}, f32[32,15]{1,0:T(8,128)}, f32[3,8,1024]{2,1,0:T(8,128)}, f32[15,16]{1,0:T(8,128)}, /*index=5*/f32[128,1024]{1,0:T(8,128)}) custom-call(bf16[128,1536]{1,0:T(8,128)(2,1)} %bitcast.12, bf16[960,128]{1,0:T(8,128)(2,1)} %bitcast.23, f32[15,16]{1,0:T(8,128)} %rates, ...), custom_call_target="tpu_custom_call" | custom-call | tf_op jit(solution)/shard_map/prepare/pallas_call | solution.py:440
  2.9 4.5 %collective-permute-start.1 = (bf16[16,2560]{1,0:T(8,128)(2,1)}, bf16[16,2560]{1,0:T(8,128)(2,1)S(1)}, u32[]{:S(2)}, u32[]{:S(2)}) collective-permute-start(bf16[16,2560]{1,0:T(8,128)(2,1)} %get-tuple-element.94), channel_id=1, source_target_pairs={{4,0},{8,4},{12,8},{16,12},{20,16},{24,20},{28,24},{32,28},{36,32}... | collective-permute-start | bytes 245768 | tf_op jit(solution)/shard_map/ppermute | solution.py:465
  7.4 1.9 %collective-permute-start = (bf16[16,1536]{1,0:T(8,128)(2,1)}, bf16[16,1536]{1,0:T(8,128)(2,1)S(1)}, u32[]{:S(2)}, u32[]{:S(2)}) collective-permute-start(bf16[16,1536]{1,0:T(8,128)(2,1)} %get-tuple-element.93), channel_id=1, source_target_pairs={{0,4},{4,8},{8,12},{12,16},{16,20},{20,24},{24,28},{28,32},{32,36}... | collective-permute-start | bytes 147464 | tf_op jit(solution)/shard_map/ppermute | solution.py:464
  9.3 4.7 %collective-permute-start.4 = (f32[32,15]{1,0:T(8,128)}, f32[32,15]{1,0:T(8,128)S(1)}, u32[]{:S(2)}, u32[]{:S(2)}) collective-permute-start(f32[32,15]{1,0:T(8,128)} %get-tuple-element.99.r0), channel_id=1, source_target_pairs={{0,12},{4,0},{8,4},{12,8},{1,13},{5,1},{9,5},{13,9},{2,14},{6,2},{... | collective-permute-start | bytes 5768 | tf_op jit(solution)/shard_map/ppermute | solution.py:413
  16.7 4.7 %project.2.refs_2_ = f32[160,2880]{1,0:T(8,128)} custom-call(bf16[16,1536]{1,0:T(8,128)(2,1)S(1)} %collective-permute-done.refs_0_, bf16[16,2560]{1,0:T(8,128)(2,1)S(1)} %collective-permute-done.1.refs_1_.nexts, bf16[128,1536]{1,0:T(8,128)(2,1)S(1)} %bitcast.13, bf16[2880,1536]{1,0:T(8,128)(2,1)} %bitcast.19), custom_call_target="tpu_custom_call" | custom-call | flops 800000000 | bytes 6000000 | tf_op jit(solution)/shard_map/project/pallas_call | solution.py:472
  21.6 5.3 %collective-permute-start.6 = (f32[32,60]{1,0:T(8,128)S(1)}, f32[32,60]{1,0:T(8,128)S(1)}, u32[]{:S(2)}, u32[]{:S(2)}) collective-permute-start(f32[32,60]{1,0:T(8,128)S(1)} %join_params.2.r0), channel_id=1, source_target_pairs={{0,32},{16,48},{32,0},{48,16},{1,33},{17,49},{33,1},{49,17},{2,34}... | collective-permute-start | bytes 23048 | tf_op jit(solution)/shard_map/ppermute | solution.py:413
  26.9 2.8 %collective-permute-start.5 = (f32[32,60]{1,0:T(8,128)S(1)}, f32[32,60]{1,0:T(8,128)S(1)}, u32[]{:S(2)}, u32[]{:S(2)}) collective-permute-start(f32[32,60]{1,0:T(8,128)S(1)} %join_params.2.r0), channel_id=1, source_target_pairs={{0,16},{16,32},{32,48},{48,0},{1,17},{17,33},{33,49},{49,1},{2,18}... | collective-permute-start | bytes 23048 | tf_op jit(solution)/shard_map/ppermute | solution.py:413
  29.8 4.9 %project.3 = (f32[160,1024]{1,0:T(8,128)S(1)}, f32[160,1024]{1,0:T(8,128)S(1)}, f32[160,1024]{1,0:T(8,128)S(1)}) custom-call(bf16[16,1536]{1,0:T(8,128)(2,1)S(1)} %collective-permute-done.refs_0_, bf16[16,2560]{1,0:T(8,128)(2,1)S(1)} %collective-permute-done.1.refs_1_.nexts, f32[160,2880]{1,0:T(8,128)} %project.2.refs_2_, bf16[128,1536]{1,0:T(8,128)(2,1)S(1)} %bitcast.14, ...), custom_call_target="tpu_custom_call" | custom-call | flops 800000000 | bytes 6000000 | tf_op jit(solution)/shard_map/project/pallas_call | solution.py:472
  34.8 3.9 %collective-permute-start.10 = (f32[32,240]{1,0:T(8,128)S(1)}, f32[32,240]{1,0:T(8,128)S(1)}, u32[]{:S(2)}, u32[]{:S(2)}) collective-permute-start(f32[32,240]{1,0:T(8,128)S(1)} %join_params.3.r0), channel_id=1, source_target_pairs={{0,192},{64,0},{128,64},{192,128},{1,193},{65,1},{129,65},{193,129... | collective-permute-start | bytes 92168 | tf_op jit(solution)/shard_map/ppermute | solution.py:413
  40.1 1.4 mix_taps.1
  41.6 2.6 %collective-permute-done.9.r2 = f32[32,240]{1,0:T(8,128)S(1)} collective-permute-done((f32[32,240]{1,0:T(8,128)S(1)}, f32[32,240]{1,0:T(8,128)S(1)}, u32[]{:S(2)}, u32[]{:S(2)}) %collective-permute-start.9) | collective-permute-done | bytes 30752 | tf_op jit(solution)/shard_map/ppermute | solution.py:413
  44.5 2.2 %end_states.1 = (f32[136,1024]{1,0:T(8,128)S(1)}, f32[16,1024]{1,0:T(8,128)S(1)}, f32[16,1024]{1,0:T(8,128)S(1)}, f32[2,16,8,1024]{3,2,1,0:T(8,128)S(1)}, f32[32...) custom-call(s32[1]{0:T(128)} %bitcast.6.me.index.xi, f32[32,240]{1,0:T(8,128)S(1)} %join_params.3.r0, ...), custom_call_target="tpu_custom_call" | custom-call | flops 20000000 | bytes 3000000 | tf_op jit(solution)/shard_map/end_states/pallas_call | solution.py:522
  46.7 1.5 collective-permute-start.13
  48.2 2.3 %collective-permute-start.12 = (bf16[32,1024]{1,0:T(8,128)(2,1)S(1)}, bf16[32,1024]{1,0:T(8,128)(2,1)S(1)}, u32[]{:S(2)}, u32[]{:S(2)}) collective-permute-start(bf16[32,1024]{1,0:T(8,128)(2,1)S(1)} %get-tuple-element.122), channel_id=1, source_target_pairs={{0,8},{4,12},{8,0},{12,4},{1,9},{5,13},{9,1},{13,5},{2,10},{6,14},... | collective-permute-start | bytes 196616 | tf_op jit(solution)/shard_map/ppermute | solution.py:413
  51.0 2.9 %collective-permute-done.12.r2 = bf16[32,1024]{1,0:T(8,128)(2,1)S(1)} collective-permute-done((bf16[32,1024]{1,0:T(8,128)(2,1)S(1)}, bf16[32,1024]{1,0:T(8,128)(2,1)S(1)}, u32[]{:S(2)}, u32[]{:S(2)}) %collective-permute-start.12) | collective-permute-done | bytes 65568 | tf_op jit(solution)/shard_map/ppermute | solution.py:413
  53.9 2.0 %collective-permute-done.11.r1 = bf16[32,1024]{1,0:T(8,128)(2,1)S(1)} collective-permute-done((bf16[32,1024]{1,0:T(8,128)(2,1)S(1)}, bf16[32,1024]{1,0:T(8,128)(2,1)S(1)}, u32[]{:S(2)}, u32[]{:S(2)}) %collective-permute-start.11) | collective-permute-done | bytes 65568 | tf_op jit(solution)/shard_map/ppermute | solution.py:413
  56.3 1.5 collective-permute-start.15
  57.7 2.4 %collective-permute-start.14 = (bf16[32,1024]{1,0:T(8,128)(2,1)S(1)}, bf16[32,1024]{1,0:T(8,128)(2,1)S(1)}, u32[]{:S(2)}, u32[]{:S(2)}) collective-permute-start(bf16[32,1024]{1,0:T(8,128)(2,1)S(1)} %get-tuple-element.126), channel_id=1, source_target_pairs={{0,16},{16,32},{32,48},{48,0},{1,17},{17,33},{33,49},{49,1},{2,18}... | collective-permute-start | bytes 196616 | tf_op jit(solution)/shard_map/ppermute | solution.py:413
  61.5 1.2 collective-permute-done.14.r1
  62.9 1.1 collective-permute-start.18
  64.5 1.1 collective-permute-start.20
  65.6 1.4 collective-permute-start.19
  67.0 1.2 collective-permute-done.21.r3
  68.2 2.1 %collective-permute-done.20.r2 = bf16[32,1024]{1,0:T(8,128)(2,1)S(1)} collective-permute-done((bf16[32,1024]{1,0:T(8,128)(2,1)S(1)}, bf16[32,1024]{1,0:T(8,128)(2,1)S(1)}, u32[]{:S(2)}, u32[]{:S(2)}) %collective-permute-start.20) | collective-permute-done | bytes 65568 | tf_op jit(solution)/shard_map/ppermute | solution.py:413
  71.9 4.2 %collective-permute-done.18.refs_2_ = bf16[128,1536]{1,0:T(8,128)(2,1)S(1)} collective-permute-done((bf16[128,1536]{1,0:T(8,128)(2,1)S(1)}, bf16[128,1536]{1,0:T(8,128)(2,1)S(1)}, u32[]{:S(2)}, u32[]{:S(2)}) %collective-permute-start.18) | collective-permute-done | bytes 393248 | tf_op jit(solution)/shard_map/ppermute | solution.py:564
  76.3 9.6 %finish.1 = (bf16[960,128]{1,0:T(8,128)(2,1)}, bf16[3,128,1024]{2,1,0:T(8,128)(2,1)}, bf16[8,360,128]{2,1,0:T(8,128)(2,1)}, bf16[40,1024]{1,0:T(8,128)(2,1)S(1)}) custom-call(s32[1]{0:T(128)} %bitcast.2.me.index.zi, s32[1]{0:T(128)} %bitcast.3.me.index.yi, f32[160,1024]{1,0:T(8,128)S(1)} %get-tuple-element.97.zq, f32[160,1024]{1,0:T(8,128)} %copy-done.3, ...), custom_call_target="tpu_custom_call" | custom-call | flops 200000000 | bytes 10000000 | tf_op jit(solution)/shard_map/finish/pallas_call | solution.py:575
  85.9 4.3 %all-to-all-start = ((bf16[8,360,128]{2,1,0:T(8,128)(2,1)}), bf16[8,360,128]{2,1,0:T(8,128)(2,1)S(1)}, u32[]{:S(2)}, u32[]{:S(2)}) async-start(bf16[8,360,128]{2,1,0:T(8,128)(2,1)} %get-tuple-element.146), calls=%async_computation | async-start | bytes 1474560 | tf_op jit(solution)/shard_map/all_to_all | solution.py:640
  91.8 2.1 %collective-permute-done.27.refs_1_ = bf16[40,1024]{1,0:T(8,128)(2,1)S(1)} collective-permute-done((bf16[40,1024]{1,0:T(8,128)(2,1)S(1)}, bf16[40,1024]{1,0:T(8,128)(2,1)S(1)}, u32[]{:S(2)}, u32[]{:S(2)}) %collective-permute-start.27) | collective-permute-done | bytes 81952 | tf_op jit(solution)/shard_map/ppermute | solution.py:628
  94.7 2.6 %collective-permute-start.30 = (bf16[40,1024]{1,0:T(8,128)(2,1)S(1)}, bf16[40,1024]{1,0:T(8,128)(2,1)S(1)}, u32[]{:S(2)}, u32[]{:S(2)}) collective-permute-start(bf16[40,1024]{1,0:T(8,128)(2,1)S(1)} %add_parts.4.refs_0_), channel_id=1, source_target_pairs={{0,48},{16,0},{32,16},{48,32},{1,49},{17,1},{33,17},{49,33},{2,50}... | collective-permute-start | bytes 245768 | tf_op jit(solution)/shard_map/ppermute | solution.py:413
  97.6 1.7 %collective-permute-start.28 = (bf16[40,1024]{1,0:T(8,128)(2,1)S(1)}, bf16[40,1024]{1,0:T(8,128)(2,1)S(1)}, u32[]{:S(2)}, u32[]{:S(2)}) collective-permute-start(bf16[40,1024]{1,0:T(8,128)(2,1)S(1)} %add_parts.4.refs_0_), channel_id=1, source_target_pairs={{0,16},{16,32},{32,48},{48,0},{1,17},{17,33},{33,49},{49,1},{2,18}... | collective-permute-start | bytes 245768 | tf_op jit(solution)/shard_map/ppermute | solution.py:413
  99.3 6.0 %token_grads.1 = bf16[128,1536]{1,0:T(8,128)(2,1)} custom-call(bf16[3,128,1024]{2,1,0:T(8,128)(2,1)} %get-tuple-element.143.dz, bf16[2880,1536]{1,0:T(8,128)(2,1)} %bitcast.21), custom_call_target="tpu_custom_call" | custom-call | flops 1200000000 | bytes 11000000 | tf_op jit(solution)/shard_map/token_grads/pallas_call | solution.py:644
  107.4 1.7 %weight_term.1 = (bf16[360,384]{1,0:T(8,128)(2,1)S(1)}, bf16[360,384]{1,0:T(8,128)(2,1)S(1)}, bf16[360,384]{1,0:T(8,128)(2,1)S(1)}, bf16[360,384]{1,0:T(8,128)(2,1)S(1)}) custom-call(s32[1]{0:T(128)} %bitcast.6.me.index.xi, s32[1]{0:T(128)} %bitcast.3.me.index.yi, s32[1]{0:T(128)} %bitcast.10.ci, bf16[8,360,128]{2,1,0:T(8,128)(2,1)S(1)} %all-to-all-done.arrived, ...), custom_call_target="tpu_custom_call" | custom-call | flops 1200000000 | bytes 6000000 | tf_op jit(solution)/shard_map/weight_term/pallas_call | solution.py:661
  109.2 1.8 %collective-permute-start.32 = (bf16[360,384]{1,0:T(8,128)(2,1)S(1)}, bf16[360,384]{1,0:T(8,128)(2,1)S(1)}, u32[]{:S(2)}, u32[]{:S(2)}) collective-permute-start(bf16[360,384]{1,0:T(8,128)(2,1)S(1)} %get-tuple-element.158), channel_id=1, source_target_pairs={{0,128},{64,192},{128,0},{192,64},{1,129},{65,193},{129,1},{193,65... | collective-permute-start | bytes 829448 | tf_op jit(solution)/shard_map/ppermute | solution.py:413
  111.0 1.6 %collective-permute-start.33 = (bf16[360,384]{1,0:T(8,128)(2,1)S(1)}, bf16[360,384]{1,0:T(8,128)(2,1)S(1)}, u32[]{:S(2)}, u32[]{:S(2)}) collective-permute-start(bf16[360,384]{1,0:T(8,128)(2,1)S(1)} %get-tuple-element.159), channel_id=1, source_target_pairs={{0,192},{64,0},{128,64},{192,128},{1,193},{65,1},{129,65},{193,129... | collective-permute-start | bytes 829448 | tf_op jit(solution)/shard_map/ppermute | solution.py:413
  112.6 3.1 %collective-permute-start.36 = (bf16[40,1024]{1,0:T(8,128)(2,1)S(1)}, bf16[40,1024]{1,0:T(8,128)(2,1)S(1)}, u32[]{:S(2)}, u32[]{:S(2)}) collective-permute-start(bf16[40,1024]{1,0:T(8,128)(2,1)S(1)} %add_parts.5.refs_0_), channel_id=1, source_target_pairs={{0,12},{4,0},{8,4},{12,8},{1,13},{5,1},{9,5},{13,9},{2,14},{6,2},{... | collective-permute-start | bytes 245768 | tf_op jit(solution)/shard_map/ppermute | solution.py:413
  116.5 1.3 collective-permute-done.36.refs_3_
  117.8 1.4 collective-permute-start.34
  119.2 3.0 %collective-permute-done.35.refs_2_ = bf16[40,1024]{1,0:T(8,128)(2,1)S(1)} collective-permute-done((bf16[40,1024]{1,0:T(8,128)(2,1)S(1)}, bf16[40,1024]{1,0:T(8,128)(2,1)S(1)}, u32[]{:S(2)}, u32[]{:S(2)}) %collective-permute-start.35) | collective-permute-done | bytes 81952 | tf_op jit(solution)/shard_map/ppermute | solution.py:413
  122.2 1.7 %collective-permute-done.34.refs_1_ = bf16[40,1024]{1,0:T(8,128)(2,1)S(1)} collective-permute-done((bf16[40,1024]{1,0:T(8,128)(2,1)S(1)}, bf16[40,1024]{1,0:T(8,128)(2,1)S(1)}, u32[]{:S(2)}, u32[]{:S(2)}) %collective-permute-start.34) | collective-permute-done | bytes 81952 | tf_op jit(solution)/shard_map/ppermute | solution.py:413
  123.9 4.6 %collective-permute-start.37 = (bf16[40,1024]{1,0:T(8,128)(2,1)S(1)}, bf16[40,1024]{1,0:T(8,128)(2,1)S(1)}, u32[]{:S(2)}, u32[]{:S(2)}) collective-permute-start(bf16[40,1024]{1,0:T(8,128)(2,1)S(1)} %add_parts.6.refs_0_), channel_id=1, source_target_pairs={{0,2},{2,0},{1,3},{3,1},{4,6},{6,4},{5,7},{7,5},{8,10},{10,8},{9,1... | collective-permute-start | bytes 245768 | tf_op jit(solution)/shard_map/ppermute | solution.py:628
  128.5 3.9 %collective-permute-done.37.refs_1_ = bf16[40,1024]{1,0:T(8,128)(2,1)S(1)} collective-permute-done((bf16[40,1024]{1,0:T(8,128)(2,1)S(1)}, bf16[40,1024]{1,0:T(8,128)(2,1)S(1)}, u32[]{:S(2)}, u32[]{:S(2)}) %collective-permute-start.37) | collective-permute-done | bytes 81952 | tf_op jit(solution)/shard_map/ppermute | solution.py:628
  132.5 1.1 split_rows.1
  133.5 9.6 %all-to-all-start.1 = ((bf16[32,24,180]{2,1,0:T(8,128)(2,1)}), bf16[32,24,180]{2,1,0:T(8,128)(2,1)S(1)}, u32[]{:S(2)}, u32[]{:S(2)}) async-start(bf16[32,24,180]{2,1,0:T(8,128)(2,1)} %split_rows.1), calls=%async_computation.1 | async-start | bytes 786432 | tf_op jit(solution)/shard_map/all_to_all | solution.py:683
  143.7 2.1 %collective-permute-start.39 = (bf16[40,1024]{1,0:T(8,128)(2,1)S(1)}, bf16[40,1024]{1,0:T(8,128)(2,1)S(1)}, u32[]{:S(2)}, u32[]{:S(2)}) collective-permute-start(bf16[40,1024]{1,0:T(8,128)(2,1)S(1)} %add_parts.7.refs_0_), channel_id=1, source_target_pairs={{0,128},{64,192},{128,0},{192,64},{1,129},{65,193},{129,1},{193,65... | collective-permute-start | bytes 245768 | tf_op jit(solution)/shard_map/ppermute | solution.py:413
  145.8 1.3 collective-permute-start.38
  147.6 2.0 %collective-permute-done.39.refs_2_ = bf16[40,1024]{1,0:T(8,128)(2,1)S(1)} collective-permute-done((bf16[40,1024]{1,0:T(8,128)(2,1)S(1)}, bf16[40,1024]{1,0:T(8,128)(2,1)S(1)}, u32[]{:S(2)}, u32[]{:S(2)}) %collective-permute-start.39) | collective-permute-done | bytes 81952 | tf_op jit(solution)/shard_map/ppermute | solution.py:413
  149.7 1.8 %collective-permute-done.38.refs_1_ = bf16[40,1024]{1,0:T(8,128)(2,1)S(1)} collective-permute-done((bf16[40,1024]{1,0:T(8,128)(2,1)S(1)}, bf16[40,1024]{1,0:T(8,128)(2,1)S(1)}, u32[]{:S(2)}, u32[]{:S(2)}) %collective-permute-start.38) | collective-permute-done | bytes 81952 | tf_op jit(solution)/shard_map/ppermute | solution.py:413
  152.2 3.5 %all-to-all-done.1.last = bf16[32,24,180]{2,1,0:T(8,128)(2,1)S(1)} async-done(((bf16[32,24,180]{2,1,0:T(8,128)(2,1)}), bf16[32,24,180]{2,1,0:T(8,128)(2,1)S(1)}, u32[]{:S(2)}, u32[]{:S(2)}) %all-to-all-start.1) | async-done | bytes 276512 | tf_op jit(solution)/shard_map/all_to_all | solution.py:683
  (84 shorter events, 17.9 us)
Async XLA Ops:
  0.6 29.1 %copy-start.1 = (bf16[1,128,1536]{2,1,0:T(8,128)(2,1)S(1)}, bf16[1,128,1536]{2,1,0:T(8,128)(2,1)}, u32[]{:S(2)}) copy-start(bf16[1,128,1536]{2,1,0:T(8,128)(2,1)} %param.6) | copy-start | bytes 1179652
  2.9 12.8 %collective-permute-start.1 = (bf16[16,2560]{1,0:T(8,128)(2,1)}, bf16[16,2560]{1,0:T(8,128)(2,1)S(1)}, u32[]{:S(2)}, u32[]{:S(2)}) collective-permute-start(bf16[16,2560]{1,0:T(8,128)(2,1)} %get-tuple-element.94), channel_id=1, source_target_pairs={{4,0},{8,4},{12,8},{16,12},{20,16},{24,20},{28,24},{32,28},{36,32}... | collective-permute-start | bytes 245768 | tf_op jit(solution)/shard_map/ppermute | solution.py:465
  7.4 8.3 %collective-permute-start = (bf16[16,1536]{1,0:T(8,128)(2,1)}, bf16[16,1536]{1,0:T(8,128)(2,1)S(1)}, u32[]{:S(2)}, u32[]{:S(2)}) collective-permute-start(bf16[16,1536]{1,0:T(8,128)(2,1)} %get-tuple-element.93), channel_id=1, source_target_pairs={{0,4},{4,8},{8,12},{12,16},{16,20},{20,24},{24,28},{28,32},{32,36}... | collective-permute-start | bytes 147464 | tf_op jit(solution)/shard_map/ppermute | solution.py:464
  9.3 12.1 %collective-permute-start.4 = (f32[32,15]{1,0:T(8,128)}, f32[32,15]{1,0:T(8,128)S(1)}, u32[]{:S(2)}, u32[]{:S(2)}) collective-permute-start(f32[32,15]{1,0:T(8,128)} %get-tuple-element.99.r0), channel_id=1, source_target_pairs={{0,12},{4,0},{8,4},{12,8},{1,13},{5,1},{9,5},{13,9},{2,14},{6,2},{... | collective-permute-start | bytes 5768 | tf_op jit(solution)/shard_map/ppermute | solution.py:413
  13.9 7.5 %collective-permute-start.3 = (f32[32,15]{1,0:T(8,128)}, f32[32,15]{1,0:T(8,128)S(1)}, u32[]{:S(2)}, u32[]{:S(2)}) collective-permute-start(f32[32,15]{1,0:T(8,128)} %get-tuple-element.99.r0), channel_id=1, source_target_pairs={{0,8},{4,12},{8,0},{12,4},{1,9},{5,13},{9,1},{13,5},{2,10},{6,14},... | collective-permute-start | bytes 5768 | tf_op jit(solution)/shard_map/ppermute | solution.py:413
  13.9 7.5 %collective-permute-start.2 = (f32[32,15]{1,0:T(8,128)}, f32[32,15]{1,0:T(8,128)S(1)}, u32[]{:S(2)}, u32[]{:S(2)}) collective-permute-start(f32[32,15]{1,0:T(8,128)} %get-tuple-element.99.r0), channel_id=1, source_target_pairs={{0,4},{4,8},{8,12},{12,0},{1,5},{5,9},{9,13},{13,1},{2,6},{6,10},{... | collective-permute-start | bytes 5768 | tf_op jit(solution)/shard_map/ppermute | solution.py:413
  21.5 13.2 %collective-permute-start.7 = (f32[32,60]{1,0:T(8,128)S(1)}, f32[32,60]{1,0:T(8,128)S(1)}, u32[]{:S(2)}, u32[]{:S(2)}) collective-permute-start(f32[32,60]{1,0:T(8,128)S(1)} %join_params.2.r0), channel_id=1, source_target_pairs={{0,48},{16,0},{32,16},{48,32},{1,49},{17,1},{33,17},{49,33},{2,50}... | collective-permute-start | bytes 23048 | tf_op jit(solution)/shard_map/ppermute | solution.py:413
  21.6 13.1 %collective-permute-start.6 = (f32[32,60]{1,0:T(8,128)S(1)}, f32[32,60]{1,0:T(8,128)S(1)}, u32[]{:S(2)}, u32[]{:S(2)}) collective-permute-start(f32[32,60]{1,0:T(8,128)S(1)} %join_params.2.r0), channel_id=1, source_target_pairs={{0,32},{16,48},{32,0},{48,16},{1,33},{17,49},{33,1},{49,17},{2,34}... | collective-permute-start | bytes 23048 | tf_op jit(solution)/shard_map/ppermute | solution.py:413
  26.9 7.8 %collective-permute-start.5 = (f32[32,60]{1,0:T(8,128)S(1)}, f32[32,60]{1,0:T(8,128)S(1)}, u32[]{:S(2)}, u32[]{:S(2)}) collective-permute-start(f32[32,60]{1,0:T(8,128)S(1)} %join_params.2.r0), channel_id=1, source_target_pairs={{0,16},{16,32},{32,48},{48,0},{1,17},{17,33},{33,49},{49,1},{2,18}... | collective-permute-start | bytes 23048 | tf_op jit(solution)/shard_map/ppermute | solution.py:413
  34.7 41.6 %copy-start.3 = (f32[160,1024]{1,0:T(8,128)}, f32[160,1024]{1,0:T(8,128)S(1)}, u32[]{:S(2)}) copy-start(f32[160,1024]{1,0:T(8,128)S(1)} %get-tuple-element.98.zk) | copy-start | bytes 1966084
  34.7 41.6 %copy-start.4 = (f32[160,1024]{1,0:T(8,128)}, f32[160,1024]{1,0:T(8,128)S(1)}, u32[]{:S(2)}) copy-start(f32[160,1024]{1,0:T(8,128)S(1)} %get-tuple-element.104.zv) | copy-start | bytes 1966084
  34.8 6.7 %collective-permute-start.10 = (f32[32,240]{1,0:T(8,128)S(1)}, f32[32,240]{1,0:T(8,128)S(1)}, u32[]{:S(2)}, u32[]{:S(2)}) collective-permute-start(f32[32,240]{1,0:T(8,128)S(1)} %join_params.3.r0), channel_id=1, source_target_pairs={{0,192},{64,0},{128,64},{192,128},{1,193},{65,1},{129,65},{193,129... | collective-permute-start | bytes 92168 | tf_op jit(solution)/shard_map/ppermute | solution.py:413
  38.7 5.4 %collective-permute-start.9 = (f32[32,240]{1,0:T(8,128)S(1)}, f32[32,240]{1,0:T(8,128)S(1)}, u32[]{:S(2)}, u32[]{:S(2)}) collective-permute-start(f32[32,240]{1,0:T(8,128)S(1)} %join_params.3.r0), channel_id=1, source_target_pairs={{0,128},{64,192},{128,0},{192,64},{1,129},{65,193},{129,1},{193,65... | collective-permute-start | bytes 92168 | tf_op jit(solution)/shard_map/ppermute | solution.py:413
  39.2 5.3 %collective-permute-start.8 = (f32[32,240]{1,0:T(8,128)S(1)}, f32[32,240]{1,0:T(8,128)S(1)}, u32[]{:S(2)}, u32[]{:S(2)}) collective-permute-start(f32[32,240]{1,0:T(8,128)S(1)} %join_params.3.r0), channel_id=1, source_target_pairs={{0,64},{64,128},{128,192},{192,0},{1,65},{65,129},{129,193},{193,1... | collective-permute-start | bytes 92168 | tf_op jit(solution)/shard_map/ppermute | solution.py:413
  46.7 29.4 %copy-start.2 = (f32[2,16,8,1024]{3,2,1,0:T(8,128)}, f32[2,16,8,1024]{3,2,1,0:T(8,128)S(1)}, u32[]{:S(2)}) copy-start(f32[2,16,8,1024]{3,2,1,0:T(8,128)S(1)} %get-tuple-element.120.es) | copy-start | bytes 3145732
  46.7 4.3 %collective-permute-start.13 = (bf16[32,1024]{1,0:T(8,128)(2,1)S(1)}, bf16[32,1024]{1,0:T(8,128)(2,1)S(1)}, u32[]{:S(2)}, u32[]{:S(2)}) collective-permute-start(bf16[32,1024]{1,0:T(8,128)(2,1)S(1)} %get-tuple-element.122), channel_id=1, source_target_pairs={{0,12},{4,0},{8,4},{12,8},{1,13},{5,1},{9,5},{13,9},{2,14},{6,2},{... | collective-permute-start | bytes 196616 | tf_op jit(solution)/shard_map/ppermute | solution.py:413
  48.2 5.8 %collective-permute-start.12 = (bf16[32,1024]{1,0:T(8,128)(2,1)S(1)}, bf16[32,1024]{1,0:T(8,128)(2,1)S(1)}, u32[]{:S(2)}, u32[]{:S(2)}) collective-permute-start(bf16[32,1024]{1,0:T(8,128)(2,1)S(1)} %get-tuple-element.122), channel_id=1, source_target_pairs={{0,8},{4,12},{8,0},{12,4},{1,9},{5,13},{9,1},{13,5},{2,10},{6,14},... | collective-permute-start | bytes 196616 | tf_op jit(solution)/shard_map/ppermute | solution.py:413
  50.5 5.5 %collective-permute-start.11 = (bf16[32,1024]{1,0:T(8,128)(2,1)S(1)}, bf16[32,1024]{1,0:T(8,128)(2,1)S(1)}, u32[]{:S(2)}, u32[]{:S(2)}) collective-permute-start(bf16[32,1024]{1,0:T(8,128)(2,1)S(1)} %get-tuple-element.122), channel_id=1, source_target_pairs={{0,4},{4,8},{8,12},{12,0},{1,5},{5,9},{9,13},{13,1},{2,6},{6,10},{... | collective-permute-start | bytes 196616 | tf_op jit(solution)/shard_map/ppermute | solution.py:413
  56.2 4.3 %collective-permute-start.16 = (bf16[32,1024]{1,0:T(8,128)(2,1)S(1)}, bf16[32,1024]{1,0:T(8,128)(2,1)S(1)}, u32[]{:S(2)}, u32[]{:S(2)}) collective-permute-start(bf16[32,1024]{1,0:T(8,128)(2,1)S(1)} %get-tuple-element.126), channel_id=1, source_target_pairs={{0,48},{16,0},{32,16},{48,32},{1,49},{17,1},{33,17},{49,33},{2,50}... | collective-permute-start | bytes 196616 | tf_op jit(solution)/shard_map/ppermute | solution.py:413
  56.3 5.3 %collective-permute-start.15 = (bf16[32,1024]{1,0:T(8,128)(2,1)S(1)}, bf16[32,1024]{1,0:T(8,128)(2,1)S(1)}, u32[]{:S(2)}, u32[]{:S(2)}) collective-permute-start(bf16[32,1024]{1,0:T(8,128)(2,1)S(1)} %get-tuple-element.126), channel_id=1, source_target_pairs={{0,32},{16,48},{32,0},{48,16},{1,33},{17,49},{33,1},{49,17},{2,34}... | collective-permute-start | bytes 196616 | tf_op jit(solution)/shard_map/ppermute | solution.py:413
  57.7 5.0 %collective-permute-start.14 = (bf16[32,1024]{1,0:T(8,128)(2,1)S(1)}, bf16[32,1024]{1,0:T(8,128)(2,1)S(1)}, u32[]{:S(2)}, u32[]{:S(2)}) collective-permute-start(bf16[32,1024]{1,0:T(8,128)(2,1)S(1)} %get-tuple-element.126), channel_id=1, source_target_pairs={{0,16},{16,32},{32,48},{48,0},{1,17},{17,33},{33,49},{49,1},{2,18}... | collective-permute-start | bytes 196616 | tf_op jit(solution)/shard_map/ppermute | solution.py:413
  62.9 13.2 %collective-permute-start.18 = (bf16[128,1536]{1,0:T(8,128)(2,1)S(1)}, bf16[128,1536]{1,0:T(8,128)(2,1)S(1)}, u32[]{:S(2)}, u32[]{:S(2)}) collective-permute-start(bf16[128,1536]{1,0:T(8,128)(2,1)S(1)} %bitcast.15), channel_id=1, source_target_pairs={{0,12},{4,8},{8,4},{12,0},{1,13},{5,9},{9,5},{13,1},{2,14},{6,10},... | collective-permute-start | bytes 1179656 | tf_op jit(solution)/shard_map/ppermute | solution.py:564
  63.9 12.1 %collective-permute-start.17 = (bf16[128,1536]{1,0:T(8,128)(2,1)S(1)}, bf16[128,1536]{1,0:T(8,128)(2,1)S(1)}, u32[]{:S(2)}, u32[]{:S(2)}) collective-permute-start(bf16[128,1536]{1,0:T(8,128)(2,1)S(1)} %bitcast.16), channel_id=1, source_target_pairs={{0,4},{4,0},{8,12},{12,8},{1,5},{5,1},{9,13},{13,9},{2,6},{6,2},{1... | collective-permute-start | bytes 1179656 | tf_op jit(solution)/shard_map/ppermute | solution.py:563
  63.9 4.3 %collective-permute-start.21 = (bf16[32,1024]{1,0:T(8,128)(2,1)S(1)}, bf16[32,1024]{1,0:T(8,128)(2,1)S(1)}, u32[]{:S(2)}, u32[]{:S(2)}) collective-permute-start(bf16[32,1024]{1,0:T(8,128)(2,1)S(1)} %get-tuple-element.128), channel_id=1, source_target_pairs={{0,192},{64,0},{128,64},{192,128},{1,193},{65,1},{129,65},{193,129... | collective-permute-start | bytes 196616 | tf_op jit(solution)/shard_map/ppermute | solution.py:413
  64.5 5.8 %collective-permute-start.20 = (bf16[32,1024]{1,0:T(8,128)(2,1)S(1)}, bf16[32,1024]{1,0:T(8,128)(2,1)S(1)}, u32[]{:S(2)}, u32[]{:S(2)}) collective-permute-start(bf16[32,1024]{1,0:T(8,128)(2,1)S(1)} %get-tuple-element.128), channel_id=1, source_target_pairs={{0,128},{64,192},{128,0},{192,64},{1,129},{65,193},{129,1},{193,65... | collective-permute-start | bytes 196616 | tf_op jit(solution)/shard_map/ppermute | solution.py:413
  65.6 5.5 %collective-permute-start.19 = (bf16[32,1024]{1,0:T(8,128)(2,1)S(1)}, bf16[32,1024]{1,0:T(8,128)(2,1)S(1)}, u32[]{:S(2)}, u32[]{:S(2)}) collective-permute-start(bf16[32,1024]{1,0:T(8,128)(2,1)S(1)} %get-tuple-element.128), channel_id=1, source_target_pairs={{0,64},{64,128},{128,192},{192,0},{1,65},{65,129},{129,193},{193,1... | collective-permute-start | bytes 196616 | tf_op jit(solution)/shard_map/ppermute | solution.py:413
  76.1 15.2 %collective-permute-start.25 = (bf16[128,1536]{1,0:T(8,128)(2,1)S(1)}, bf16[128,1536]{1,0:T(8,128)(2,1)S(1)}, u32[]{:S(2)}, u32[]{:S(2)}) collective-permute-start(bf16[128,1536]{1,0:T(8,128)(2,1)S(1)} %collective-permute-done.17.refs_1_), channel_id=1, source_target_pairs={{0,12},{4,8},{8,4},{12,0},{1,13},{5,9},{9,5},{13,1},{2,14},{6,10},... | collective-permute-start | bytes 1179656 | tf_op jit(solution)/shard_map/ppermute | solution.py:566
  85.9 19.4 %all-to-all-start = ((bf16[8,360,128]{2,1,0:T(8,128)(2,1)}), bf16[8,360,128]{2,1,0:T(8,128)(2,1)S(1)}, u32[]{:S(2)}, u32[]{:S(2)}) async-start(bf16[8,360,128]{2,1,0:T(8,128)(2,1)} %get-tuple-element.146), calls=%async_computation | async-start | bytes 1474560 | tf_op jit(solution)/shard_map/all_to_all | solution.py:640
  90.3 3.7 %collective-permute-start.22 = (bf16[128,1536]{1,0:T(8,128)(2,1)S(1)}, bf16[128,1536]{1,0:T(8,128)(2,1)S(1)}, u32[]{:S(2)}, u32[]{:S(2)}) collective-permute-start(bf16[128,1536]{1,0:T(8,128)(2,1)S(1)} %bitcast.17), channel_id=1, source_target_pairs={{0,1},{1,0},{2,3},{3,2},{4,5},{5,4},{6,7},{7,6},{8,9},{9,8},{10,11... | collective-permute-start | bytes 1179656 | tf_op jit(solution)/shard_map/ppermute | solution.py:569
  90.8 3.2 %collective-permute-start.23 = (bf16[128,1536]{1,0:T(8,128)(2,1)S(1)}, bf16[128,1536]{1,0:T(8,128)(2,1)S(1)}, u32[]{:S(2)}, u32[]{:S(2)}) collective-permute-start(bf16[128,1536]{1,0:T(8,128)(2,1)S(1)} %collective-permute-done.17.refs_1_), channel_id=1, source_target_pairs={{0,1},{1,0},{2,3},{3,2},{4,5},{5,4},{6,7},{7,6},{8,9},{9,8},{10,11... | collective-permute-start | bytes 1179656 | tf_op jit(solution)/shard_map/ppermute | solution.py:569
  90.8 3.2 %collective-permute-start.24 = (bf16[128,1536]{1,0:T(8,128)(2,1)S(1)}, bf16[128,1536]{1,0:T(8,128)(2,1)S(1)}, u32[]{:S(2)}, u32[]{:S(2)}) collective-permute-start(bf16[128,1536]{1,0:T(8,128)(2,1)S(1)} %collective-permute-done.18.refs_2_), channel_id=1, source_target_pairs={{0,1},{1,0},{2,3},{3,2},{4,5},{5,4},{6,7},{7,6},{8,9},{9,8},{10,11... | collective-permute-start | bytes 1179656 | tf_op jit(solution)/shard_map/ppermute | solution.py:569
  91.3 3.5 %collective-permute-start.26 = (bf16[128,1536]{1,0:T(8,128)(2,1)S(1)}, bf16[128,1536]{1,0:T(8,128)(2,1)S(1)}, u32[]{:S(2)}, u32[]{:S(2)}) collective-permute-start(bf16[128,1536]{1,0:T(8,128)(2,1)S(1)} %collective-permute-done.25.refs_3_), channel_id=1, source_target_pairs={{0,1},{1,0},{2,3},{3,2},{4,5},{5,4},{6,7},{7,6},{8,9},{9,8},{10,11... | collective-permute-start | bytes 1179656 | tf_op jit(solution)/shard_map/ppermute | solution.py:569
  91.3 2.6 %collective-permute-start.27 = (bf16[40,1024]{1,0:T(8,128)(2,1)S(1)}, bf16[40,1024]{1,0:T(8,128)(2,1)S(1)}, u32[]{:S(2)}, u32[]{:S(2)}) collective-permute-start(bf16[40,1024]{1,0:T(8,128)(2,1)S(1)} %get-tuple-element.138.refs_0_), channel_id=1, source_target_pairs={{0,1},{1,0},{2,3},{3,2},{4,5},{5,4},{6,7},{7,6},{8,9},{9,8},{10,11... | collective-permute-start | bytes 245768 | tf_op jit(solution)/shard_map/ppermute | solution.py:628
  94.7 10.6 %collective-permute-start.30 = (bf16[40,1024]{1,0:T(8,128)(2,1)S(1)}, bf16[40,1024]{1,0:T(8,128)(2,1)S(1)}, u32[]{:S(2)}, u32[]{:S(2)}) collective-permute-start(bf16[40,1024]{1,0:T(8,128)(2,1)S(1)} %add_parts.4.refs_0_), channel_id=1, source_target_pairs={{0,48},{16,0},{32,16},{48,32},{1,49},{17,1},{33,17},{49,33},{2,50}... | collective-permute-start | bytes 245768 | tf_op jit(solution)/shard_map/ppermute | solution.py:413
  97.3 8.0 %collective-permute-start.29 = (bf16[40,1024]{1,0:T(8,128)(2,1)S(1)}, bf16[40,1024]{1,0:T(8,128)(2,1)S(1)}, u32[]{:S(2)}, u32[]{:S(2)}) collective-permute-start(bf16[40,1024]{1,0:T(8,128)(2,1)S(1)} %add_parts.4.refs_0_), channel_id=1, source_target_pairs={{0,32},{16,48},{32,0},{48,16},{1,33},{17,49},{33,1},{49,17},{2,34}... | collective-permute-start | bytes 245768 | tf_op jit(solution)/shard_map/ppermute | solution.py:413
  97.6 7.7 %collective-permute-start.28 = (bf16[40,1024]{1,0:T(8,128)(2,1)S(1)}, bf16[40,1024]{1,0:T(8,128)(2,1)S(1)}, u32[]{:S(2)}, u32[]{:S(2)}) collective-permute-start(bf16[40,1024]{1,0:T(8,128)(2,1)S(1)} %add_parts.4.refs_0_), channel_id=1, source_target_pairs={{0,16},{16,32},{32,48},{48,0},{1,17},{17,33},{33,49},{49,1},{2,18}... | collective-permute-start | bytes 245768 | tf_op jit(solution)/shard_map/ppermute | solution.py:413
  99.3 52.2 %copy-start.8 = (f32[15,16]{1,0:T(8,128)S(1)}, f32[15,16]{1,0:T(8,128)}, u32[]{:S(2)}) copy-start(f32[15,16]{1,0:T(8,128)} %get-tuple-element.166.amp) | copy-start | bytes 2884
  109.1 23.3 %collective-permute-start.31 = (bf16[360,384]{1,0:T(8,128)(2,1)S(1)}, bf16[360,384]{1,0:T(8,128)(2,1)S(1)}, u32[]{:S(2)}, u32[]{:S(2)}) collective-permute-start(bf16[360,384]{1,0:T(8,128)(2,1)S(1)} %get-tuple-element.157), channel_id=1, source_target_pairs={{0,64},{64,128},{128,192},{192,0},{1,65},{65,129},{129,193},{193,1... | collective-permute-start | bytes 829448 | tf_op jit(solution)/shard_map/ppermute | solution.py:413
  109.2 23.2 %collective-permute-start.32 = (bf16[360,384]{1,0:T(8,128)(2,1)S(1)}, bf16[360,384]{1,0:T(8,128)(2,1)S(1)}, u32[]{:S(2)}, u32[]{:S(2)}) collective-permute-start(bf16[360,384]{1,0:T(8,128)(2,1)S(1)} %get-tuple-element.158), channel_id=1, source_target_pairs={{0,128},{64,192},{128,0},{192,64},{1,129},{65,193},{129,1},{193,65... | collective-permute-start | bytes 829448 | tf_op jit(solution)/shard_map/ppermute | solution.py:413
  111.0 21.5 %collective-permute-start.33 = (bf16[360,384]{1,0:T(8,128)(2,1)S(1)}, bf16[360,384]{1,0:T(8,128)(2,1)S(1)}, u32[]{:S(2)}, u32[]{:S(2)}) collective-permute-start(bf16[360,384]{1,0:T(8,128)(2,1)S(1)} %get-tuple-element.159), channel_id=1, source_target_pairs={{0,192},{64,0},{128,64},{192,128},{1,193},{65,1},{129,65},{193,129... | collective-permute-start | bytes 829448 | tf_op jit(solution)/shard_map/ppermute | solution.py:413
  112.6 5.2 %collective-permute-start.36 = (bf16[40,1024]{1,0:T(8,128)(2,1)S(1)}, bf16[40,1024]{1,0:T(8,128)(2,1)S(1)}, u32[]{:S(2)}, u32[]{:S(2)}) collective-permute-start(bf16[40,1024]{1,0:T(8,128)(2,1)S(1)} %add_parts.5.refs_0_), channel_id=1, source_target_pairs={{0,12},{4,0},{8,4},{12,8},{1,13},{5,1},{9,5},{13,9},{2,14},{6,2},{... | collective-permute-start | bytes 245768 | tf_op jit(solution)/shard_map/ppermute | solution.py:413
  115.7 6.5 %collective-permute-start.35 = (bf16[40,1024]{1,0:T(8,128)(2,1)S(1)}, bf16[40,1024]{1,0:T(8,128)(2,1)S(1)}, u32[]{:S(2)}, u32[]{:S(2)}) collective-permute-start(bf16[40,1024]{1,0:T(8,128)(2,1)S(1)} %add_parts.5.refs_0_), channel_id=1, source_target_pairs={{0,8},{4,12},{8,0},{12,4},{1,9},{5,13},{9,1},{13,5},{2,10},{6,14},... | collective-permute-start | bytes 245768 | tf_op jit(solution)/shard_map/ppermute | solution.py:413
  117.8 6.1 %collective-permute-start.34 = (bf16[40,1024]{1,0:T(8,128)(2,1)S(1)}, bf16[40,1024]{1,0:T(8,128)(2,1)S(1)}, u32[]{:S(2)}, u32[]{:S(2)}) collective-permute-start(bf16[40,1024]{1,0:T(8,128)(2,1)S(1)} %add_parts.5.refs_0_), channel_id=1, source_target_pairs={{0,4},{4,8},{8,12},{12,0},{1,5},{5,9},{9,13},{13,1},{2,6},{6,10},{... | collective-permute-start | bytes 245768 | tf_op jit(solution)/shard_map/ppermute | solution.py:413
  123.9 8.5 %collective-permute-start.37 = (bf16[40,1024]{1,0:T(8,128)(2,1)S(1)}, bf16[40,1024]{1,0:T(8,128)(2,1)S(1)}, u32[]{:S(2)}, u32[]{:S(2)}) collective-permute-start(bf16[40,1024]{1,0:T(8,128)(2,1)S(1)} %add_parts.6.refs_0_), channel_id=1, source_target_pairs={{0,2},{2,0},{1,3},{3,1},{4,6},{6,4},{5,7},{7,5},{8,10},{10,8},{9,1... | collective-permute-start | bytes 245768 | tf_op jit(solution)/shard_map/ppermute | solution.py:628
  133.5 22.2 %all-to-all-start.1 = ((bf16[32,24,180]{2,1,0:T(8,128)(2,1)}), bf16[32,24,180]{2,1,0:T(8,128)(2,1)S(1)}, u32[]{:S(2)}, u32[]{:S(2)}) async-start(bf16[32,24,180]{2,1,0:T(8,128)(2,1)} %split_rows.1), calls=%async_computation.1 | async-start | bytes 786432 | tf_op jit(solution)/shard_map/all_to_all | solution.py:683
  143.1 4.5 %collective-permute-start.40 = (bf16[40,1024]{1,0:T(8,128)(2,1)S(1)}, bf16[40,1024]{1,0:T(8,128)(2,1)S(1)}, u32[]{:S(2)}, u32[]{:S(2)}) collective-permute-start(bf16[40,1024]{1,0:T(8,128)(2,1)S(1)} %add_parts.7.refs_0_), channel_id=1, source_target_pairs={{0,192},{64,0},{128,64},{192,128},{1,193},{65,1},{129,65},{193,129... | collective-permute-start | bytes 245768 | tf_op jit(solution)/shard_map/ppermute | solution.py:413
  143.7 5.9 %collective-permute-start.39 = (bf16[40,1024]{1,0:T(8,128)(2,1)S(1)}, bf16[40,1024]{1,0:T(8,128)(2,1)S(1)}, u32[]{:S(2)}, u32[]{:S(2)}) collective-permute-start(bf16[40,1024]{1,0:T(8,128)(2,1)S(1)} %add_parts.7.refs_0_), channel_id=1, source_target_pairs={{0,128},{64,192},{128,0},{192,64},{1,129},{65,193},{129,1},{193,65... | collective-permute-start | bytes 245768 | tf_op jit(solution)/shard_map/ppermute | solution.py:413
  145.8 5.7 %collective-permute-start.38 = (bf16[40,1024]{1,0:T(8,128)(2,1)S(1)}, bf16[40,1024]{1,0:T(8,128)(2,1)S(1)}, u32[]{:S(2)}, u32[]{:S(2)}) collective-permute-start(bf16[40,1024]{1,0:T(8,128)(2,1)S(1)} %add_parts.7.refs_0_), channel_id=1, source_target_pairs={{0,64},{64,128},{128,192},{192,0},{1,65},{65,129},{129,193},{193,1... | collective-permute-start | bytes 245768 | tf_op jit(solution)/shard_map/ppermute | solution.py:413
  (8 other events, 65.6 us)
where the time goes:
time: 157 us; the launch traced here: 156 us
  starting transfers between devices  74.8 us (48%)
  waiting for transfers between devices  39.9 us (25%)
  Pallas kernels  36.9 us (24%)
  local copies, waits for them, and re-layouts  3.77 us (2%)
    ppermute x30, starting transfers between devices, ring(): return lax.ppermute(a, ax, [(i, (i + d) % 4) for i in range(4)])  47.2 us
    ppermute x30, waiting for transfers between devices, ring(): return lax.ppermute(a, ax, [(i, (i + d) % 4) for i in range(4)])  25.4 us
    pallas_call x1, Pallas kernels, local(): pl.pallas_call(finish, grid=(PADC // 128,), in_specs=[smem, smem, *[tiles...  9.63 us
    pallas_call x2, Pallas kernels, project(): pl.pallas_call(make_project(part), in_specs=[vm] * (2 + part) + [anywhere...  9.62 us
    all_to_all x1, starting transfers between devices, local(): last = lax.all_to_all(blocks, ('zl', 'y', 'zh'), 0, 0, tiled=True)  9.58 us
    ppermute x2, waiting for transfers between devices, swap(): return [a, lax.ppermute(a, ax, [(0, 1), (1, 0)])]  6.03 us
    pallas_call x1, Pallas kernels, local(): pl.pallas_call(token_grads, grid=(3,), in_specs=[pl.BlockSpec((1, own, PA...  6.01 us
    ppermute x2, starting transfers between devices, swap(): return [a, lax.ppermute(a, ax, [(0, 1), (1, 0)])]  5.08 us
  transfers between devices with their start and end apart: 43, of which 22 were waited for; matrix products, arithmetic and copies ran while one was open for 0% of the time, Pallas kernels for 18%

commit v1 on v0

--- a/solution.py
+++ b/solution.py
@@ -461,8 +461,6 @@
         compiler_params=params(54),
         name="prepare",
     )(feats, cot.T, rates, residues, conv_taps)
-    tprev = lax.ppermute(tail, ctx, [(i, i + 1) for i in range(count - 1)])
-    nexts = lax.ppermute(head, ctx, [(i, i - 1) for i in range(1, count)])
     ext_rows = own + 2 * HALO
     steps = depth // KBLK // 2
 
@@ -500,12 +498,15 @@
     held, each = block, width // count
     work = []
     for g, (me, ax) in enumerate(((yi, "y"), (zi, "zl"), (xi, "x"))):
+        if g == 1:
+            head, tail, held = lax.optimization_barrier((head, tail, held))
+            tprev = lax.ppermute(tail, ctx, [(i, i + 1) for i in range(count - 1)])
+            nexts = lax.ppermute(head, ctx, [(i, i - 1) for i in range(1, count)])
         blocks = [held] + [ring(held, ax, d) for d in (1, 2, 3)]
-        work = project(0) if g == 0 else project(1, *work) if g == 1 else mixed(*work)
-        *blocks, last_work = lax.optimization_barrier((*blocks, work[-1]))
-        work = [*work[:-1], last_work]
-        if g == 1:
-            zq, zk, zv = work
+        if g > 0:
+            work = project(g - 1, *work)
+            *blocks, last_work = lax.optimization_barrier((*blocks, work[-1]))
+            work = [*work[:-1], last_work]
         if g == 2:
             break
         each = 4 * each
@@ -518,7 +519,8 @@
             compiler_params=params(4),
             name="join_params",
         )(me, *blocks)
-    mq, mk, mv = work
+    zq, zk, zv = work
+    mq, mk, mv = mixed(*work)
     cots, rate, gain, es, ends, endb = pl.pallas_call(
         end_states,
         in_specs=[smem] + [vm] * 9,

time: 157 us -> 158 us (level)
  starting transfers between devices: 74.8 us -> 76.5 us
    ppermute x1, waiting for transfers between devices: 4.2 us -> 0.01 us  [local(): opposite = lax.ppermute(mine, 'y', [(i, 3 - i) for i in range(4)])]
    ppermute x30, waiting for transfers between devices: 25.4 us -> 29 us  [ring(): return lax.ppermute(a, ax, [(i, (i + d) % 4) for i in range(4)])]
    ppermute x30, starting transfers between devices: 47.2 us -> 48.8 us  [ring(): return lax.ppermute(a, ax, [(i, (i + d) % 4) for i in range(4)])]
  transfers between devices with their start and end apart: 43 -> 43, of which waited for: 22 -> 21; matrix products, arithmetic and copies ran while one was open for 0% -> 0% of each run, Pallas kernels for 18% -> 17%
where the time goes in v1:
time: 158 us
  starting transfers between devices  76.5 us (48%)
  waiting for transfers between devices  38.8 us (25%)
  Pallas kernels  37 us (23%)
  local copies, waits for them, and re-layouts  4.48 us (3%)
    ppermute x30, starting transfers between devices, ring(): return lax.ppermute(a, ax, [(i, (i + d) % 4) for i in range(4)])  48.8 us
    ppermute x30, waiting for transfers between devices, ring(): return lax.ppermute(a, ax, [(i, (i + d) % 4) for i in range(4)])  29 us
    pallas_call x1, Pallas kernels, local(): pl.pallas_call(finish, grid=(PADC // 128,), in_specs=[smem, smem, *[tiles...  9.63 us
    pallas_call x2, Pallas kernels, project(): pl.pallas_call(make_project(part), in_specs=[vm] * (2 + part) + [anywhere...  9.62 us
    all_to_all x1, starting transfers between devices, local(): last = lax.all_to_all(blocks, ('zl', 'y', 'zh'), 0, 0, tiled=True)  8.57 us
    ppermute x2, waiting for transfers between devices, swap(): return [a, lax.ppermute(a, ax, [(0, 1), (1, 0)])]  6.64 us
    pallas_call x1, Pallas kernels, local(): pl.pallas_call(token_grads, grid=(3,), in_specs=[pl.BlockSpec((1, own, PA...  6.02 us
    ppermute x2, starting transfers between devices, swap(): return [a, lax.ppermute(a, ax, [(0, 1), (1, 0)])]  5.06 us
  transfers between devices with their start and end apart: 43, of which 21 were waited for; matrix products, arithmetic and copies ran while one was open for 0% of the time, Pallas kernels for 17%

profile of v1, /device:TPU:32, one launch (start us, length us, event | category | flops | bytes accessed | tf_op | source)
XLA Modules:
  0.0 157.7 jit_solution(290800972981727797)
XLA Ops:
  0.7 2.2 %prepare.1 = (bf16[16,2560]{1,0:T(8,128)(2,1)}, bf16[16,1536]{1,0:T(8,128)(2,1)}, f32[32,15]{1,0:T(8,128)}, f32[3,8,1024]{2,1,0:T(8,128)}, f32[15,16]{1,0:T(8,128)}, /*index=5*/f32[128,1024]{1,0:T(8,128)}) custom-call(bf16[128,1536]{1,0:T(8,128)(2,1)} %bitcast.12, bf16[960,128]{1,0:T(8,128)(2,1)} %bitcast.23, f32[15,16]{1,0:T(8,128)} %rates, ...), custom_call_target="tpu_custom_call" | custom-call | tf_op jit(solution)/shard_map/prepare/pallas_call | solution.py:440
  2.9 3.1 %collective-permute-start.2 = (f32[32,15]{1,0:T(8,128)}, f32[32,15]{1,0:T(8,128)S(1)}, u32[]{:S(2)}, u32[]{:S(2)}) collective-permute-start(f32[32,15]{1,0:T(8,128)} %get-tuple-element.93.r0), channel_id=1, source_target_pairs={{0,12},{4,0},{8,4},{12,8},{1,13},{5,1},{9,5},{13,9},{2,14},{6,2},{... | collective-permute-start | bytes 5768 | tf_op jit(solution)/shard_map/ppermute | solution.py:413
  7.6 3.8 %collective-permute-done.1.r2 = f32[32,15]{1,0:T(8,128)S(1)} collective-permute-done((f32[32,15]{1,0:T(8,128)}, f32[32,15]{1,0:T(8,128)S(1)}, u32[]{:S(2)}, u32[]{:S(2)}) %collective-permute-start.1) | collective-permute-done | bytes 1952 | tf_op jit(solution)/shard_map/ppermute | solution.py:413
  12.6 3.0 %collective-permute-start.4 = (bf16[16,2560]{1,0:T(8,128)(2,1)}, bf16[16,2560]{1,0:T(8,128)(2,1)S(1)}, u32[]{:S(2)}, u32[]{:S(2)}) collective-permute-start(bf16[16,2560]{1,0:T(8,128)(2,1)} %get-tuple-element.95), channel_id=1, source_target_pairs={{4,0},{8,4},{12,8},{16,12},{20,16},{24,20},{28,24},{32,28},{36,32}... | collective-permute-start | bytes 245768 | tf_op jit(solution)/shard_map/ppermute | solution.py:504
  15.6 2.8 %collective-permute-start.3 = (bf16[16,1536]{1,0:T(8,128)(2,1)}, bf16[16,1536]{1,0:T(8,128)(2,1)S(1)}, u32[]{:S(2)}, u32[]{:S(2)}) collective-permute-start(bf16[16,1536]{1,0:T(8,128)(2,1)} %get-tuple-element.94), channel_id=1, source_target_pairs={{0,4},{4,8},{8,12},{12,16},{16,20},{20,24},{24,28},{28,32},{32,36}... | collective-permute-start | bytes 147464 | tf_op jit(solution)/shard_map/ppermute | solution.py:503
  18.6 3.3 %collective-permute-start.6 = (f32[32,60]{1,0:T(8,128)S(1)}, f32[32,60]{1,0:T(8,128)S(1)}, u32[]{:S(2)}, u32[]{:S(2)}) collective-permute-start(f32[32,60]{1,0:T(8,128)S(1)} %join_params.2.r0), channel_id=1, source_target_pairs={{0,32},{16,48},{32,0},{48,16},{1,33},{17,49},{33,1},{49,17},{2,34}... | collective-permute-start | bytes 23048 | tf_op jit(solution)/shard_map/ppermute | solution.py:413
  21.9 2.8 %collective-permute-start.5 = (f32[32,60]{1,0:T(8,128)S(1)}, f32[32,60]{1,0:T(8,128)S(1)}, u32[]{:S(2)}, u32[]{:S(2)}) collective-permute-start(f32[32,60]{1,0:T(8,128)S(1)} %join_params.2.r0), channel_id=1, source_target_pairs={{0,16},{16,32},{32,48},{48,0},{1,17},{17,33},{33,49},{49,1},{2,18}... | collective-permute-start | bytes 23048 | tf_op jit(solution)/shard_map/ppermute | solution.py:413
  25.7 4.7 %project.2.refs_2_ = f32[160,2880]{1,0:T(8,128)} custom-call(bf16[16,1536]{1,0:T(8,128)(2,1)S(1)} %collective-permute-done.3.refs_0_, bf16[16,2560]{1,0:T(8,128)(2,1)S(1)} %collective-permute-done.4.refs_1_.nexts, bf16[128,1536]{1,0:T(8,128)(2,1)S(1)} %bitcast.13, bf16[2880,1536]{1,0:T(8,128)(2,1)} %bitcast.19), custom_call_target="tpu_custom_call" | custom-call | flops 800000000 | bytes 6000000 | tf_op jit(solution)/shard_map/project/pallas_call | solution.py:470
  30.6 2.8 %collective-permute-start.10 = (f32[32,240]{1,0:T(8,128)S(1)}, f32[32,240]{1,0:T(8,128)S(1)}, u32[]{:S(2)}, u32[]{:S(2)}) collective-permute-start(f32[32,240]{1,0:T(8,128)S(1)} %join_params.3.r0), channel_id=1, source_target_pairs={{0,192},{64,0},{128,64},{192,128},{1,193},{65,1},{129,65},{193,129... | collective-permute-start | bytes 92168 | tf_op jit(solution)/shard_map/ppermute | solution.py:413
  35.1 4.9 %project.3 = (f32[160,1024]{1,0:T(8,128)S(1)}, f32[160,1024]{1,0:T(8,128)S(1)}, f32[160,1024]{1,0:T(8,128)S(1)}) custom-call(bf16[16,1536]{1,0:T(8,128)(2,1)S(1)} %collective-permute-done.3.refs_0_, bf16[16,2560]{1,0:T(8,128)(2,1)S(1)} %collective-permute-done.4.refs_1_.nexts, f32[160,2880]{1,0:T(8,128)} %project.2.refs_2_, bf16[128,1536]{1,0:T(8,128)(2,1)S(1)} %bitcast.14, ...), custom_call_target="tpu_custom_call" | custom-call | flops 800000000 | bytes 6000000 | tf_op jit(solution)/shard_map/project/pallas_call | solution.py:470
  40.1 1.4 mix_taps.1
  41.6 2.2 %end_states.1 = (f32[136,1024]{1,0:T(8,128)S(1)}, f32[16,1024]{1,0:T(8,128)S(1)}, f32[16,1024]{1,0:T(8,128)S(1)}, f32[2,16,8,1024]{3,2,1,0:T(8,128)S(1)}, f32[32...) custom-call(s32[1]{0:T(128)} %bitcast.6.me.index.xi, f32[32,240]{1,0:T(8,128)S(1)} %join_params.3.r0, ...), custom_call_target="tpu_custom_call" | custom-call | flops 20000000 | bytes 3000000 | tf_op jit(solution)/shard_map/end_states/pallas_call | solution.py:524
  43.8 5.3 %collective-permute-start.13 = (bf16[32,1024]{1,0:T(8,128)(2,1)S(1)}, bf16[32,1024]{1,0:T(8,128)(2,1)S(1)}, u32[]{:S(2)}, u32[]{:S(2)}) collective-permute-start(bf16[32,1024]{1,0:T(8,128)(2,1)S(1)} %get-tuple-element.118), channel_id=1, source_target_pairs={{0,12},{4,0},{8,4},{12,8},{1,13},{5,1},{9,5},{13,9},{2,14},{6,2},{... | collective-permute-start | bytes 196616 | tf_op jit(solution)/shard_map/ppermute | solution.py:413
  50.0 1.6 collective-permute-done.13.r3
  51.6 3.4 %collective-permute-done.12.r2 = bf16[32,1024]{1,0:T(8,128)(2,1)S(1)} collective-permute-done((bf16[32,1024]{1,0:T(8,128)(2,1)S(1)}, bf16[32,1024]{1,0:T(8,128)(2,1)S(1)}, u32[]{:S(2)}, u32[]{:S(2)}) %collective-permute-start.12) | collective-permute-done | bytes 65568 | tf_op jit(solution)/shard_map/ppermute | solution.py:413
  57.0 2.4 %collective-permute-start.14 = (bf16[32,1024]{1,0:T(8,128)(2,1)S(1)}, bf16[32,1024]{1,0:T(8,128)(2,1)S(1)}, u32[]{:S(2)}, u32[]{:S(2)}) collective-permute-start(bf16[32,1024]{1,0:T(8,128)(2,1)S(1)} %get-tuple-element.122), channel_id=1, source_target_pairs={{0,16},{16,32},{32,48},{48,0},{1,17},{17,33},{33,49},{49,1},{2,18}... | collective-permute-start | bytes 196616 | tf_op jit(solution)/shard_map/ppermute | solution.py:413
  59.8 1.8 %collective-permute-done.15.r2 = bf16[32,1024]{1,0:T(8,128)(2,1)S(1)} collective-permute-done((bf16[32,1024]{1,0:T(8,128)(2,1)S(1)}, bf16[32,1024]{1,0:T(8,128)(2,1)S(1)}, u32[]{:S(2)}, u32[]{:S(2)}) %collective-permute-start.15) | collective-permute-done | bytes 65568 | tf_op jit(solution)/shard_map/ppermute | solution.py:413
  62.2 1.7 %collective-permute-start.18 = (bf16[128,1536]{1,0:T(8,128)(2,1)S(1)}, bf16[128,1536]{1,0:T(8,128)(2,1)S(1)}, u32[]{:S(2)}, u32[]{:S(2)}) collective-permute-start(bf16[128,1536]{1,0:T(8,128)(2,1)S(1)} %bitcast.15), channel_id=1, source_target_pairs={{0,12},{4,8},{8,4},{12,0},{1,13},{5,9},{9,5},{13,1},{2,14},{6,10},... | collective-permute-start | bytes 1179656 | tf_op jit(solution)/shard_map/ppermute | solution.py:566
  63.9 2.4 %collective-permute-start.21 = (bf16[32,1024]{1,0:T(8,128)(2,1)S(1)}, bf16[32,1024]{1,0:T(8,128)(2,1)S(1)}, u32[]{:S(2)}, u32[]{:S(2)}) collective-permute-start(bf16[32,1024]{1,0:T(8,128)(2,1)S(1)} %get-tuple-element.124), channel_id=1, source_target_pairs={{0,192},{64,0},{128,64},{192,128},{1,193},{65,1},{129,65},{193,129... | collective-permute-start | bytes 196616 | tf_op jit(solution)/shard_map/ppermute | solution.py:413
  66.3 1.8 %collective-permute-start.20 = (bf16[32,1024]{1,0:T(8,128)(2,1)S(1)}, bf16[32,1024]{1,0:T(8,128)(2,1)S(1)}, u32[]{:S(2)}, u32[]{:S(2)}) collective-permute-start(bf16[32,1024]{1,0:T(8,128)(2,1)S(1)} %get-tuple-element.124), channel_id=1, source_target_pairs={{0,128},{64,192},{128,0},{192,64},{1,129},{65,193},{129,1},{193,65... | collective-permute-start | bytes 196616 | tf_op jit(solution)/shard_map/ppermute | solution.py:413
  68.3 3.8 %collective-permute-done.20.r2 = bf16[32,1024]{1,0:T(8,128)(2,1)S(1)} collective-permute-done((bf16[32,1024]{1,0:T(8,128)(2,1)S(1)}, bf16[32,1024]{1,0:T(8,128)(2,1)S(1)}, u32[]{:S(2)}, u32[]{:S(2)}) %collective-permute-start.20) | collective-permute-done | bytes 65568 | tf_op jit(solution)/shard_map/ppermute | solution.py:413
  72.0 1.5 collective-permute-done.19.r1
  74.3 1.6 collective-permute-start.25
  75.9 9.6 %finish.1 = (bf16[960,128]{1,0:T(8,128)(2,1)}, bf16[3,128,1024]{2,1,0:T(8,128)(2,1)}, bf16[8,360,128]{2,1,0:T(8,128)(2,1)}, bf16[40,1024]{1,0:T(8,128)(2,1)S(1)}) custom-call(s32[1]{0:T(128)} %bitcast.2.me.index.zi, s32[1]{0:T(128)} %bitcast.3.me.index.yi, f32[160,1024]{1,0:T(8,128)S(1)} %get-tuple-element.98.zq, f32[160,1024]{1,0:T(8,128)} %copy-done.3, ...), custom_call_target="tpu_custom_call" | custom-call | flops 200000000 | bytes 10000000 | tf_op jit(solution)/shard_map/finish/pallas_call | solution.py:577
  85.5 3.9 %all-to-all-start = ((bf16[8,360,128]{2,1,0:T(8,128)(2,1)}), bf16[8,360,128]{2,1,0:T(8,128)(2,1)S(1)}, u32[]{:S(2)}, u32[]{:S(2)}) async-start(bf16[8,360,128]{2,1,0:T(8,128)(2,1)} %get-tuple-element.142), calls=%async_computation | async-start | bytes 1474560 | tf_op jit(solution)/shard_map/all_to_all | solution.py:642
  91.0 2.1 %collective-permute-done.27.refs_1_ = bf16[40,1024]{1,0:T(8,128)(2,1)S(1)} collective-permute-done((bf16[40,1024]{1,0:T(8,128)(2,1)S(1)}, bf16[40,1024]{1,0:T(8,128)(2,1)S(1)}, u32[]{:S(2)}, u32[]{:S(2)}) %collective-permute-start.27) | collective-permute-done | bytes 81952 | tf_op jit(solution)/shard_map/ppermute | solution.py:630
  93.9 2.2 %collective-permute-start.30 = (bf16[40,1024]{1,0:T(8,128)(2,1)S(1)}, bf16[40,1024]{1,0:T(8,128)(2,1)S(1)}, u32[]{:S(2)}, u32[]{:S(2)}) collective-permute-start(bf16[40,1024]{1,0:T(8,128)(2,1)S(1)} %add_parts.4.refs_0_), channel_id=1, source_target_pairs={{0,48},{16,0},{32,16},{48,32},{1,49},{17,1},{33,17},{49,33},{2,50}... | collective-permute-start | bytes 245768 | tf_op jit(solution)/shard_map/ppermute | solution.py:413
  96.1 2.8 %collective-permute-start.28 = (bf16[40,1024]{1,0:T(8,128)(2,1)S(1)}, bf16[40,1024]{1,0:T(8,128)(2,1)S(1)}, u32[]{:S(2)}, u32[]{:S(2)}) collective-permute-start(bf16[40,1024]{1,0:T(8,128)(2,1)S(1)} %add_parts.4.refs_0_), channel_id=1, source_target_pairs={{0,16},{16,32},{32,48},{48,0},{1,17},{17,33},{33,49},{49,1},{2,18}... | collective-permute-start | bytes 245768 | tf_op jit(solution)/shard_map/ppermute | solution.py:413
  98.9 6.0 %token_grads.1 = bf16[128,1536]{1,0:T(8,128)(2,1)} custom-call(bf16[3,128,1024]{2,1,0:T(8,128)(2,1)} %get-tuple-element.139.dz, bf16[2880,1536]{1,0:T(8,128)(2,1)} %bitcast.21), custom_call_target="tpu_custom_call" | custom-call | flops 1200000000 | bytes 11000000 | tf_op jit(solution)/shard_map/token_grads/pallas_call | solution.py:646
  107.0 1.7 %weight_term.1 = (bf16[360,384]{1,0:T(8,128)(2,1)S(1)}, bf16[360,384]{1,0:T(8,128)(2,1)S(1)}, bf16[360,384]{1,0:T(8,128)(2,1)S(1)}, bf16[360,384]{1,0:T(8,128)(2,1)S(1)}) custom-call(s32[1]{0:T(128)} %bitcast.6.me.index.xi, s32[1]{0:T(128)} %bitcast.3.me.index.yi, s32[1]{0:T(128)} %bitcast.10.ci, bf16[8,360,128]{2,1,0:T(8,128)(2,1)S(1)} %all-to-all-done.arrived, ...), custom_call_target="tpu_custom_call" | custom-call | flops 1200000000 | bytes 6000000 | tf_op jit(solution)/shard_map/weight_term/pallas_call | solution.py:663
  108.8 2.7 %collective-permute-start.31 = (bf16[360,384]{1,0:T(8,128)(2,1)S(1)}, bf16[360,384]{1,0:T(8,128)(2,1)S(1)}, u32[]{:S(2)}, u32[]{:S(2)}) collective-permute-start(bf16[360,384]{1,0:T(8,128)(2,1)S(1)} %get-tuple-element.153), channel_id=1, source_target_pairs={{0,64},{64,128},{128,192},{192,0},{1,65},{65,129},{129,193},{193,1... | collective-permute-start | bytes 829448 | tf_op jit(solution)/shard_map/ppermute | solution.py:413
  111.5 1.6 %collective-permute-start.32 = (bf16[360,384]{1,0:T(8,128)(2,1)S(1)}, bf16[360,384]{1,0:T(8,128)(2,1)S(1)}, u32[]{:S(2)}, u32[]{:S(2)}) collective-permute-start(bf16[360,384]{1,0:T(8,128)(2,1)S(1)} %get-tuple-element.154), channel_id=1, source_target_pairs={{0,128},{64,192},{128,0},{192,64},{1,129},{65,193},{129,1},{193,65... | collective-permute-start | bytes 829448 | tf_op jit(solution)/shard_map/ppermute | solution.py:413
  113.1 1.2 collective-permute-start.33
  114.2 3.1 %collective-permute-start.36 = (bf16[40,1024]{1,0:T(8,128)(2,1)S(1)}, bf16[40,1024]{1,0:T(8,128)(2,1)S(1)}, u32[]{:S(2)}, u32[]{:S(2)}) collective-permute-start(bf16[40,1024]{1,0:T(8,128)(2,1)S(1)} %add_parts.5.refs_0_), channel_id=1, source_target_pairs={{0,12},{4,0},{8,4},{12,8},{1,13},{5,1},{9,5},{13,9},{2,14},{6,2},{... | collective-permute-start | bytes 245768 | tf_op jit(solution)/shard_map/ppermute | solution.py:413
  118.2 1.3 collective-permute-done.36.refs_3_
  119.5 1.5 collective-permute-start.34
  121.0 2.7 %collective-permute-done.35.refs_2_ = bf16[40,1024]{1,0:T(8,128)(2,1)S(1)} collective-permute-done((bf16[40,1024]{1,0:T(8,128)(2,1)S(1)}, bf16[40,1024]{1,0:T(8,128)(2,1)S(1)}, u32[]{:S(2)}, u32[]{:S(2)}) %collective-permute-start.35) | collective-permute-done | bytes 81952 | tf_op jit(solution)/shard_map/ppermute | solution.py:413
  123.7 1.8 %collective-permute-done.34.refs_1_ = bf16[40,1024]{1,0:T(8,128)(2,1)S(1)} collective-permute-done((bf16[40,1024]{1,0:T(8,128)(2,1)S(1)}, bf16[40,1024]{1,0:T(8,128)(2,1)S(1)}, u32[]{:S(2)}, u32[]{:S(2)}) %collective-permute-start.34) | collective-permute-done | bytes 81952 | tf_op jit(solution)/shard_map/ppermute | solution.py:413
  125.6 4.6 %collective-permute-start.37 = (bf16[40,1024]{1,0:T(8,128)(2,1)S(1)}, bf16[40,1024]{1,0:T(8,128)(2,1)S(1)}, u32[]{:S(2)}, u32[]{:S(2)}) collective-permute-start(bf16[40,1024]{1,0:T(8,128)(2,1)S(1)} %add_parts.6.refs_0_), channel_id=1, source_target_pairs={{0,2},{2,0},{1,3},{3,1},{4,6},{6,4},{5,7},{7,5},{8,10},{10,8},{9,1... | collective-permute-start | bytes 245768 | tf_op jit(solution)/shard_map/ppermute | solution.py:630
  130.1 4.5 %collective-permute-done.37.refs_1_ = bf16[40,1024]{1,0:T(8,128)(2,1)S(1)} collective-permute-done((bf16[40,1024]{1,0:T(8,128)(2,1)S(1)}, bf16[40,1024]{1,0:T(8,128)(2,1)S(1)}, u32[]{:S(2)}, u32[]{:S(2)}) %collective-permute-start.37) | collective-permute-done | bytes 81952 | tf_op jit(solution)/shard_map/ppermute | solution.py:630
  134.7 1.1 split_rows.1
  135.8 8.6 %all-to-all-start.1 = ((bf16[32,24,180]{2,1,0:T(8,128)(2,1)}), bf16[32,24,180]{2,1,0:T(8,128)(2,1)S(1)}, u32[]{:S(2)}, u32[]{:S(2)}) async-start(bf16[32,24,180]{2,1,0:T(8,128)(2,1)} %split_rows.1), calls=%async_computation.1 | async-start | bytes 786432 | tf_op jit(solution)/shard_map/all_to_all | solution.py:685
  144.4 1.2 collective-permute-start.40
  145.6 1.8 %collective-permute-start.39 = (bf16[40,1024]{1,0:T(8,128)(2,1)S(1)}, bf16[40,1024]{1,0:T(8,128)(2,1)S(1)}, u32[]{:S(2)}, u32[]{:S(2)}) collective-permute-start(bf16[40,1024]{1,0:T(8,128)(2,1)S(1)} %add_parts.7.refs_0_), channel_id=1, source_target_pairs={{0,128},{64,192},{128,0},{192,64},{1,129},{65,193},{129,1},{193,65... | collective-permute-start | bytes 245768 | tf_op jit(solution)/shard_map/ppermute | solution.py:413
  147.4 1.5 collective-permute-done.40.refs_3_
  148.9 2.7 %collective-permute-done.39.refs_2_ = bf16[40,1024]{1,0:T(8,128)(2,1)S(1)} collective-permute-done((bf16[40,1024]{1,0:T(8,128)(2,1)S(1)}, bf16[40,1024]{1,0:T(8,128)(2,1)S(1)}, u32[]{:S(2)}, u32[]{:S(2)}) %collective-permute-start.39) | collective-permute-done | bytes 81952 | tf_op jit(solution)/shard_map/ppermute | solution.py:413
  151.5 1.5 collective-permute-done.38.refs_1_
  153.8 3.1 %all-to-all-done.1.last = bf16[32,24,180]{2,1,0:T(8,128)(2,1)S(1)} async-done(((bf16[32,24,180]{2,1,0:T(8,128)(2,1)}), bf16[32,24,180]{2,1,0:T(8,128)(2,1)S(1)}, u32[]{:S(2)}, u32[]{:S(2)}) %all-to-all-start.1) | async-done | bytes 276512 | tf_op jit(solution)/shard_map/all_to_all | solution.py:685
  (84 shorter events, 17.5 us)
Async XLA Ops:
  0.6 34.5 %copy-start.1 = (bf16[1,128,1536]{2,1,0:T(8,128)(2,1)S(1)}, bf16[1,128,1536]{2,1,0:T(8,128)(2,1)}, u32[]{:S(2)}) copy-start(bf16[1,128,1536]{2,1,0:T(8,128)(2,1)} %param.6) | copy-start | bytes 1179652
  2.9 4.7 %collective-permute-start.2 = (f32[32,15]{1,0:T(8,128)}, f32[32,15]{1,0:T(8,128)S(1)}, u32[]{:S(2)}, u32[]{:S(2)}) collective-permute-start(f32[32,15]{1,0:T(8,128)} %get-tuple-element.93.r0), channel_id=1, source_target_pairs={{0,12},{4,0},{8,4},{12,8},{1,13},{5,1},{9,5},{13,9},{2,14},{6,2},{... | collective-permute-start | bytes 5768 | tf_op jit(solution)/shard_map/ppermute | solution.py:413
  6.0 5.5 %collective-permute-start.1 = (f32[32,15]{1,0:T(8,128)}, f32[32,15]{1,0:T(8,128)S(1)}, u32[]{:S(2)}, u32[]{:S(2)}) collective-permute-start(f32[32,15]{1,0:T(8,128)} %get-tuple-element.93.r0), channel_id=1, source_target_pairs={{0,8},{4,12},{8,0},{12,4},{1,9},{5,13},{9,1},{13,5},{2,10},{6,14},... | collective-permute-start | bytes 5768 | tf_op jit(solution)/shard_map/ppermute | solution.py:413
  6.6 5.2 %collective-permute-start = (f32[32,15]{1,0:T(8,128)}, f32[32,15]{1,0:T(8,128)S(1)}, u32[]{:S(2)}, u32[]{:S(2)}) collective-permute-start(f32[32,15]{1,0:T(8,128)} %get-tuple-element.93.r0), channel_id=1, source_target_pairs={{0,4},{4,8},{8,12},{12,0},{1,5},{5,9},{9,13},{13,1},{2,6},{6,10},{... | collective-permute-start | bytes 5768 | tf_op jit(solution)/shard_map/ppermute | solution.py:413
  12.6 12.1 %collective-permute-start.4 = (bf16[16,2560]{1,0:T(8,128)(2,1)}, bf16[16,2560]{1,0:T(8,128)(2,1)S(1)}, u32[]{:S(2)}, u32[]{:S(2)}) collective-permute-start(bf16[16,2560]{1,0:T(8,128)(2,1)} %get-tuple-element.95), channel_id=1, source_target_pairs={{4,0},{8,4},{12,8},{16,12},{20,16},{24,20},{28,24},{32,28},{36,32}... | collective-permute-start | bytes 245768 | tf_op jit(solution)/shard_map/ppermute | solution.py:504
  15.6 9.1 %collective-permute-start.3 = (bf16[16,1536]{1,0:T(8,128)(2,1)}, bf16[16,1536]{1,0:T(8,128)(2,1)S(1)}, u32[]{:S(2)}, u32[]{:S(2)}) collective-permute-start(bf16[16,1536]{1,0:T(8,128)(2,1)} %get-tuple-element.94), channel_id=1, source_target_pairs={{0,4},{4,8},{8,12},{12,16},{16,20},{20,24},{24,28},{28,32},{32,36}... | collective-permute-start | bytes 147464 | tf_op jit(solution)/shard_map/ppermute | solution.py:503
  18.4 12.0 %collective-permute-start.7 = (f32[32,60]{1,0:T(8,128)S(1)}, f32[32,60]{1,0:T(8,128)S(1)}, u32[]{:S(2)}, u32[]{:S(2)}) collective-permute-start(f32[32,60]{1,0:T(8,128)S(1)} %join_params.2.r0), channel_id=1, source_target_pairs={{0,48},{16,0},{32,16},{48,32},{1,49},{17,1},{33,17},{49,33},{2,50}... | collective-permute-start | bytes 23048 | tf_op jit(solution)/shard_map/ppermute | solution.py:413
  18.6 11.8 %collective-permute-start.6 = (f32[32,60]{1,0:T(8,128)S(1)}, f32[32,60]{1,0:T(8,128)S(1)}, u32[]{:S(2)}, u32[]{:S(2)}) collective-permute-start(f32[32,60]{1,0:T(8,128)S(1)} %join_params.2.r0), channel_id=1, source_target_pairs={{0,32},{16,48},{32,0},{48,16},{1,33},{17,49},{33,1},{49,17},{2,34}... | collective-permute-start | bytes 23048 | tf_op jit(solution)/shard_map/ppermute | solution.py:413
  21.9 8.6 %collective-permute-start.5 = (f32[32,60]{1,0:T(8,128)S(1)}, f32[32,60]{1,0:T(8,128)S(1)}, u32[]{:S(2)}, u32[]{:S(2)}) collective-permute-start(f32[32,60]{1,0:T(8,128)S(1)} %join_params.2.r0), channel_id=1, source_target_pairs={{0,16},{16,32},{32,48},{48,0},{1,17},{17,33},{33,49},{49,1},{2,18}... | collective-permute-start | bytes 23048 | tf_op jit(solution)/shard_map/ppermute | solution.py:413
  30.6 9.5 %collective-permute-start.10 = (f32[32,240]{1,0:T(8,128)S(1)}, f32[32,240]{1,0:T(8,128)S(1)}, u32[]{:S(2)}, u32[]{:S(2)}) collective-permute-start(f32[32,240]{1,0:T(8,128)S(1)} %join_params.3.r0), channel_id=1, source_target_pairs={{0,192},{64,0},{128,64},{192,128},{1,193},{65,1},{129,65},{193,129... | collective-permute-start | bytes 92168 | tf_op jit(solution)/shard_map/ppermute | solution.py:413
  33.4 6.6 %collective-permute-start.9 = (f32[32,240]{1,0:T(8,128)S(1)}, f32[32,240]{1,0:T(8,128)S(1)}, u32[]{:S(2)}, u32[]{:S(2)}) collective-permute-start(f32[32,240]{1,0:T(8,128)S(1)} %join_params.3.r0), channel_id=1, source_target_pairs={{0,128},{64,192},{128,0},{192,64},{1,129},{65,193},{129,1},{193,65... | collective-permute-start | bytes 92168 | tf_op jit(solution)/shard_map/ppermute | solution.py:413
  34.2 5.9 %collective-permute-start.8 = (f32[32,240]{1,0:T(8,128)S(1)}, f32[32,240]{1,0:T(8,128)S(1)}, u32[]{:S(2)}, u32[]{:S(2)}) collective-permute-start(f32[32,240]{1,0:T(8,128)S(1)} %join_params.3.r0), channel_id=1, source_target_pairs={{0,64},{64,128},{128,192},{192,0},{1,65},{65,129},{129,193},{193,1... | collective-permute-start | bytes 92168 | tf_op jit(solution)/shard_map/ppermute | solution.py:413
  40.0 35.9 %copy-start.3 = (f32[160,1024]{1,0:T(8,128)}, f32[160,1024]{1,0:T(8,128)S(1)}, u32[]{:S(2)}) copy-start(f32[160,1024]{1,0:T(8,128)S(1)} %get-tuple-element.99.zk) | copy-start | bytes 1966084
  40.1 35.8 %copy-start.4 = (f32[160,1024]{1,0:T(8,128)}, f32[160,1024]{1,0:T(8,128)S(1)}, u32[]{:S(2)}) copy-start(f32[160,1024]{1,0:T(8,128)S(1)} %get-tuple-element.105.zv) | copy-start | bytes 1966084
  43.8 30.6 %copy-start.2 = (f32[2,16,8,1024]{3,2,1,0:T(8,128)}, f32[2,16,8,1024]{3,2,1,0:T(8,128)S(1)}, u32[]{:S(2)}) copy-start(f32[2,16,8,1024]{3,2,1,0:T(8,128)S(1)} %get-tuple-element.116.es) | copy-start | bytes 3145732
  43.8 7.8 %collective-permute-start.13 = (bf16[32,1024]{1,0:T(8,128)(2,1)S(1)}, bf16[32,1024]{1,0:T(8,128)(2,1)S(1)}, u32[]{:S(2)}, u32[]{:S(2)}) collective-permute-start(bf16[32,1024]{1,0:T(8,128)(2,1)S(1)} %get-tuple-element.118), channel_id=1, source_target_pairs={{0,12},{4,0},{8,4},{12,8},{1,13},{5,1},{9,5},{13,9},{2,14},{6,2},{... | collective-permute-start | bytes 196616 | tf_op jit(solution)/shard_map/ppermute | solution.py:413
  49.1 5.9 %collective-permute-start.12 = (bf16[32,1024]{1,0:T(8,128)(2,1)S(1)}, bf16[32,1024]{1,0:T(8,128)(2,1)S(1)}, u32[]{:S(2)}, u32[]{:S(2)}) collective-permute-start(bf16[32,1024]{1,0:T(8,128)(2,1)S(1)} %get-tuple-element.118), channel_id=1, source_target_pairs={{0,8},{4,12},{8,0},{12,4},{1,9},{5,13},{9,1},{13,5},{2,10},{6,14},... | collective-permute-start | bytes 196616 | tf_op jit(solution)/shard_map/ppermute | solution.py:413
  49.1 6.2 %collective-permute-start.11 = (bf16[32,1024]{1,0:T(8,128)(2,1)S(1)}, bf16[32,1024]{1,0:T(8,128)(2,1)S(1)}, u32[]{:S(2)}, u32[]{:S(2)}) collective-permute-start(bf16[32,1024]{1,0:T(8,128)(2,1)S(1)} %get-tuple-element.118), channel_id=1, source_target_pairs={{0,4},{4,8},{8,12},{12,0},{1,5},{5,9},{9,13},{13,1},{2,6},{6,10},{... | collective-permute-start | bytes 196616 | tf_op jit(solution)/shard_map/ppermute | solution.py:413
  55.5 4.3 %collective-permute-start.16 = (bf16[32,1024]{1,0:T(8,128)(2,1)S(1)}, bf16[32,1024]{1,0:T(8,128)(2,1)S(1)}, u32[]{:S(2)}, u32[]{:S(2)}) collective-permute-start(bf16[32,1024]{1,0:T(8,128)(2,1)S(1)} %get-tuple-element.122), channel_id=1, source_target_pairs={{0,48},{16,0},{32,16},{48,32},{1,49},{17,1},{33,17},{49,33},{2,50}... | collective-permute-start | bytes 196616 | tf_op jit(solution)/shard_map/ppermute | solution.py:413
  56.4 5.2 %collective-permute-start.15 = (bf16[32,1024]{1,0:T(8,128)(2,1)S(1)}, bf16[32,1024]{1,0:T(8,128)(2,1)S(1)}, u32[]{:S(2)}, u32[]{:S(2)}) collective-permute-start(bf16[32,1024]{1,0:T(8,128)(2,1)S(1)} %get-tuple-element.122), channel_id=1, source_target_pairs={{0,32},{16,48},{32,0},{48,16},{1,33},{17,49},{33,1},{49,17},{2,34}... | collective-permute-start | bytes 196616 | tf_op jit(solution)/shard_map/ppermute | solution.py:413
  57.0 5.0 %collective-permute-start.14 = (bf16[32,1024]{1,0:T(8,128)(2,1)S(1)}, bf16[32,1024]{1,0:T(8,128)(2,1)S(1)}, u32[]{:S(2)}, u32[]{:S(2)}) collective-permute-start(bf16[32,1024]{1,0:T(8,128)(2,1)S(1)} %get-tuple-element.122), channel_id=1, source_target_pairs={{0,16},{16,32},{32,48},{48,0},{1,17},{17,33},{33,49},{49,1},{2,18}... | collective-permute-start | bytes 196616 | tf_op jit(solution)/shard_map/ppermute | solution.py:413
  62.2 12.2 %collective-permute-start.18 = (bf16[128,1536]{1,0:T(8,128)(2,1)S(1)}, bf16[128,1536]{1,0:T(8,128)(2,1)S(1)}, u32[]{:S(2)}, u32[]{:S(2)}) collective-permute-start(bf16[128,1536]{1,0:T(8,128)(2,1)S(1)} %bitcast.15), channel_id=1, source_target_pairs={{0,12},{4,8},{8,4},{12,0},{1,13},{5,9},{9,5},{13,1},{2,14},{6,10},... | collective-permute-start | bytes 1179656 | tf_op jit(solution)/shard_map/ppermute | solution.py:566
  63.9 10.4 %collective-permute-start.17 = (bf16[128,1536]{1,0:T(8,128)(2,1)S(1)}, bf16[128,1536]{1,0:T(8,128)(2,1)S(1)}, u32[]{:S(2)}, u32[]{:S(2)}) collective-permute-start(bf16[128,1536]{1,0:T(8,128)(2,1)S(1)} %bitcast.16), channel_id=1, source_target_pairs={{0,4},{4,0},{8,12},{12,8},{1,5},{5,1},{9,13},{13,9},{2,6},{6,2},{1... | collective-permute-start | bytes 1179656 | tf_op jit(solution)/shard_map/ppermute | solution.py:565
  63.9 4.3 %collective-permute-start.21 = (bf16[32,1024]{1,0:T(8,128)(2,1)S(1)}, bf16[32,1024]{1,0:T(8,128)(2,1)S(1)}, u32[]{:S(2)}, u32[]{:S(2)}) collective-permute-start(bf16[32,1024]{1,0:T(8,128)(2,1)S(1)} %get-tuple-element.124), channel_id=1, source_target_pairs={{0,192},{64,0},{128,64},{192,128},{1,193},{65,1},{129,65},{193,129... | collective-permute-start | bytes 196616 | tf_op jit(solution)/shard_map/ppermute | solution.py:413
  66.3 5.8 %collective-permute-start.20 = (bf16[32,1024]{1,0:T(8,128)(2,1)S(1)}, bf16[32,1024]{1,0:T(8,128)(2,1)S(1)}, u32[]{:S(2)}, u32[]{:S(2)}) collective-permute-start(bf16[32,1024]{1,0:T(8,128)(2,1)S(1)} %get-tuple-element.124), channel_id=1, source_target_pairs={{0,128},{64,192},{128,0},{192,64},{1,129},{65,193},{129,1},{193,65... | collective-permute-start | bytes 196616 | tf_op jit(solution)/shard_map/ppermute | solution.py:413
  68.1 5.5 %collective-permute-start.19 = (bf16[32,1024]{1,0:T(8,128)(2,1)S(1)}, bf16[32,1024]{1,0:T(8,128)(2,1)S(1)}, u32[]{:S(2)}, u32[]{:S(2)}) collective-permute-start(bf16[32,1024]{1,0:T(8,128)(2,1)S(1)} %get-tuple-element.124), channel_id=1, source_target_pairs={{0,64},{64,128},{128,192},{192,0},{1,65},{65,129},{129,193},{193,1... | collective-permute-start | bytes 196616 | tf_op jit(solution)/shard_map/ppermute | solution.py:413
  74.3 16.1 %collective-permute-start.25 = (bf16[128,1536]{1,0:T(8,128)(2,1)S(1)}, bf16[128,1536]{1,0:T(8,128)(2,1)S(1)}, u32[]{:S(2)}, u32[]{:S(2)}) collective-permute-start(bf16[128,1536]{1,0:T(8,128)(2,1)S(1)} %collective-permute-done.17.refs_1_), channel_id=1, source_target_pairs={{0,12},{4,8},{8,4},{12,0},{1,13},{5,9},{9,5},{13,1},{2,14},{6,10},... | collective-permute-start | bytes 1179656 | tf_op jit(solution)/shard_map/ppermute | solution.py:568
  85.5 19.5 %all-to-all-start = ((bf16[8,360,128]{2,1,0:T(8,128)(2,1)}), bf16[8,360,128]{2,1,0:T(8,128)(2,1)S(1)}, u32[]{:S(2)}, u32[]{:S(2)}) async-start(bf16[8,360,128]{2,1,0:T(8,128)(2,1)} %get-tuple-element.142), calls=%async_computation | async-start | bytes 1474560 | tf_op jit(solution)/shard_map/all_to_all | solution.py:642
  89.4 3.7 %collective-permute-start.22 = (bf16[128,1536]{1,0:T(8,128)(2,1)S(1)}, bf16[128,1536]{1,0:T(8,128)(2,1)S(1)}, u32[]{:S(2)}, u32[]{:S(2)}) collective-permute-start(bf16[128,1536]{1,0:T(8,128)(2,1)S(1)} %bitcast.17), channel_id=1, source_target_pairs={{0,1},{1,0},{2,3},{3,2},{4,5},{5,4},{6,7},{7,6},{8,9},{9,8},{10,11... | collective-permute-start | bytes 1179656 | tf_op jit(solution)/shard_map/ppermute | solution.py:571
  90.0 3.2 %collective-permute-start.23 = (bf16[128,1536]{1,0:T(8,128)(2,1)S(1)}, bf16[128,1536]{1,0:T(8,128)(2,1)S(1)}, u32[]{:S(2)}, u32[]{:S(2)}) collective-permute-start(bf16[128,1536]{1,0:T(8,128)(2,1)S(1)} %collective-permute-done.17.refs_1_), channel_id=1, source_target_pairs={{0,1},{1,0},{2,3},{3,2},{4,5},{5,4},{6,7},{7,6},{8,9},{9,8},{10,11... | collective-permute-start | bytes 1179656 | tf_op jit(solution)/shard_map/ppermute | solution.py:571
  90.0 3.2 %collective-permute-start.24 = (bf16[128,1536]{1,0:T(8,128)(2,1)S(1)}, bf16[128,1536]{1,0:T(8,128)(2,1)S(1)}, u32[]{:S(2)}, u32[]{:S(2)}) collective-permute-start(bf16[128,1536]{1,0:T(8,128)(2,1)S(1)} %collective-permute-done.18.refs_2_), channel_id=1, source_target_pairs={{0,1},{1,0},{2,3},{3,2},{4,5},{5,4},{6,7},{7,6},{8,9},{9,8},{10,11... | collective-permute-start | bytes 1179656 | tf_op jit(solution)/shard_map/ppermute | solution.py:571
  90.5 3.5 %collective-permute-start.26 = (bf16[128,1536]{1,0:T(8,128)(2,1)S(1)}, bf16[128,1536]{1,0:T(8,128)(2,1)S(1)}, u32[]{:S(2)}, u32[]{:S(2)}) collective-permute-start(bf16[128,1536]{1,0:T(8,128)(2,1)S(1)} %collective-permute-done.25.refs_3_), channel_id=1, source_target_pairs={{0,1},{1,0},{2,3},{3,2},{4,5},{5,4},{6,7},{7,6},{8,9},{9,8},{10,11... | collective-permute-start | bytes 1179656 | tf_op jit(solution)/shard_map/ppermute | solution.py:571
  90.5 2.6 %collective-permute-start.27 = (bf16[40,1024]{1,0:T(8,128)(2,1)S(1)}, bf16[40,1024]{1,0:T(8,128)(2,1)S(1)}, u32[]{:S(2)}, u32[]{:S(2)}) collective-permute-start(bf16[40,1024]{1,0:T(8,128)(2,1)S(1)} %get-tuple-element.134.refs_0_), channel_id=1, source_target_pairs={{0,1},{1,0},{2,3},{3,2},{4,5},{5,4},{6,7},{7,6},{8,9},{9,8},{10,11... | collective-permute-start | bytes 245768 | tf_op jit(solution)/shard_map/ppermute | solution.py:630
  93.9 11.0 %collective-permute-start.30 = (bf16[40,1024]{1,0:T(8,128)(2,1)S(1)}, bf16[40,1024]{1,0:T(8,128)(2,1)S(1)}, u32[]{:S(2)}, u32[]{:S(2)}) collective-permute-start(bf16[40,1024]{1,0:T(8,128)(2,1)S(1)} %add_parts.4.refs_0_), channel_id=1, source_target_pairs={{0,48},{16,0},{32,16},{48,32},{1,49},{17,1},{33,17},{49,33},{2,50}... | collective-permute-start | bytes 245768 | tf_op jit(solution)/shard_map/ppermute | solution.py:413
  96.1 8.8 %collective-permute-start.29 = (bf16[40,1024]{1,0:T(8,128)(2,1)S(1)}, bf16[40,1024]{1,0:T(8,128)(2,1)S(1)}, u32[]{:S(2)}, u32[]{:S(2)}) collective-permute-start(bf16[40,1024]{1,0:T(8,128)(2,1)S(1)} %add_parts.4.refs_0_), channel_id=1, source_target_pairs={{0,32},{16,48},{32,0},{48,16},{1,33},{17,49},{33,1},{49,17},{2,34}... | collective-permute-start | bytes 245768 | tf_op jit(solution)/shard_map/ppermute | solution.py:413
  96.1 8.8 %collective-permute-start.28 = (bf16[40,1024]{1,0:T(8,128)(2,1)S(1)}, bf16[40,1024]{1,0:T(8,128)(2,1)S(1)}, u32[]{:S(2)}, u32[]{:S(2)}) collective-permute-start(bf16[40,1024]{1,0:T(8,128)(2,1)S(1)} %add_parts.4.refs_0_), channel_id=1, source_target_pairs={{0,16},{16,32},{32,48},{48,0},{1,17},{17,33},{33,49},{49,1},{2,18}... | collective-permute-start | bytes 245768 | tf_op jit(solution)/shard_map/ppermute | solution.py:413
  98.9 54.2 %copy-start.8 = (f32[15,16]{1,0:T(8,128)S(1)}, f32[15,16]{1,0:T(8,128)}, u32[]{:S(2)}) copy-start(f32[15,16]{1,0:T(8,128)} %get-tuple-element.162.amp) | copy-start | bytes 2884
  108.8 25.9 %collective-permute-start.31 = (bf16[360,384]{1,0:T(8,128)(2,1)S(1)}, bf16[360,384]{1,0:T(8,128)(2,1)S(1)}, u32[]{:S(2)}, u32[]{:S(2)}) collective-permute-start(bf16[360,384]{1,0:T(8,128)(2,1)S(1)} %get-tuple-element.153), channel_id=1, source_target_pairs={{0,64},{64,128},{128,192},{192,0},{1,65},{65,129},{129,193},{193,1... | collective-permute-start | bytes 829448 | tf_op jit(solution)/shard_map/ppermute | solution.py:413
  111.5 23.2 %collective-permute-start.32 = (bf16[360,384]{1,0:T(8,128)(2,1)S(1)}, bf16[360,384]{1,0:T(8,128)(2,1)S(1)}, u32[]{:S(2)}, u32[]{:S(2)}) collective-permute-start(bf16[360,384]{1,0:T(8,128)(2,1)S(1)} %get-tuple-element.154), channel_id=1, source_target_pairs={{0,128},{64,192},{128,0},{192,64},{1,129},{65,193},{129,1},{193,65... | collective-permute-start | bytes 829448 | tf_op jit(solution)/shard_map/ppermute | solution.py:413
  113.1 21.6 %collective-permute-start.33 = (bf16[360,384]{1,0:T(8,128)(2,1)S(1)}, bf16[360,384]{1,0:T(8,128)(2,1)S(1)}, u32[]{:S(2)}, u32[]{:S(2)}) collective-permute-start(bf16[360,384]{1,0:T(8,128)(2,1)S(1)} %get-tuple-element.155), channel_id=1, source_target_pairs={{0,192},{64,0},{128,64},{192,128},{1,193},{65,1},{129,65},{193,129... | collective-permute-start | bytes 829448 | tf_op jit(solution)/shard_map/ppermute | solution.py:413
  114.2 5.2 %collective-permute-start.36 = (bf16[40,1024]{1,0:T(8,128)(2,1)S(1)}, bf16[40,1024]{1,0:T(8,128)(2,1)S(1)}, u32[]{:S(2)}, u32[]{:S(2)}) collective-permute-start(bf16[40,1024]{1,0:T(8,128)(2,1)S(1)} %add_parts.5.refs_0_), channel_id=1, source_target_pairs={{0,12},{4,0},{8,4},{12,8},{1,13},{5,1},{9,5},{13,9},{2,14},{6,2},{... | collective-permute-start | bytes 245768 | tf_op jit(solution)/shard_map/ppermute | solution.py:413
  117.4 6.4 %collective-permute-start.35 = (bf16[40,1024]{1,0:T(8,128)(2,1)S(1)}, bf16[40,1024]{1,0:T(8,128)(2,1)S(1)}, u32[]{:S(2)}, u32[]{:S(2)}) collective-permute-start(bf16[40,1024]{1,0:T(8,128)(2,1)S(1)} %add_parts.5.refs_0_), channel_id=1, source_target_pairs={{0,8},{4,12},{8,0},{12,4},{1,9},{5,13},{9,1},{13,5},{2,10},{6,14},... | collective-permute-start | bytes 245768 | tf_op jit(solution)/shard_map/ppermute | solution.py:413
  119.5 6.1 %collective-permute-start.34 = (bf16[40,1024]{1,0:T(8,128)(2,1)S(1)}, bf16[40,1024]{1,0:T(8,128)(2,1)S(1)}, u32[]{:S(2)}, u32[]{:S(2)}) collective-permute-start(bf16[40,1024]{1,0:T(8,128)(2,1)S(1)} %add_parts.5.refs_0_), channel_id=1, source_target_pairs={{0,4},{4,8},{8,12},{12,0},{1,5},{5,9},{9,13},{13,1},{2,6},{6,10},{... | collective-permute-start | bytes 245768 | tf_op jit(solution)/shard_map/ppermute | solution.py:413
  125.6 9.1 %collective-permute-start.37 = (bf16[40,1024]{1,0:T(8,128)(2,1)S(1)}, bf16[40,1024]{1,0:T(8,128)(2,1)S(1)}, u32[]{:S(2)}, u32[]{:S(2)}) collective-permute-start(bf16[40,1024]{1,0:T(8,128)(2,1)S(1)} %add_parts.6.refs_0_), channel_id=1, source_target_pairs={{0,2},{2,0},{1,3},{3,1},{4,6},{6,4},{5,7},{7,5},{8,10},{10,8},{9,1... | collective-permute-start | bytes 245768 | tf_op jit(solution)/shard_map/ppermute | solution.py:630
  135.8 21.2 %all-to-all-start.1 = ((bf16[32,24,180]{2,1,0:T(8,128)(2,1)}), bf16[32,24,180]{2,1,0:T(8,128)(2,1)S(1)}, u32[]{:S(2)}, u32[]{:S(2)}) async-start(bf16[32,24,180]{2,1,0:T(8,128)(2,1)} %split_rows.1), calls=%async_computation.1 | async-start | bytes 786432 | tf_op jit(solution)/shard_map/all_to_all | solution.py:685
  144.4 4.5 %collective-permute-start.40 = (bf16[40,1024]{1,0:T(8,128)(2,1)S(1)}, bf16[40,1024]{1,0:T(8,128)(2,1)S(1)}, u32[]{:S(2)}, u32[]{:S(2)}) collective-permute-start(bf16[40,1024]{1,0:T(8,128)(2,1)S(1)} %add_parts.7.refs_0_), channel_id=1, source_target_pairs={{0,192},{64,0},{128,64},{192,128},{1,193},{65,1},{129,65},{193,129... | collective-permute-start | bytes 245768 | tf_op jit(solution)/shard_map/ppermute | solution.py:413
  145.6 5.9 %collective-permute-start.39 = (bf16[40,1024]{1,0:T(8,128)(2,1)S(1)}, bf16[40,1024]{1,0:T(8,128)(2,1)S(1)}, u32[]{:S(2)}, u32[]{:S(2)}) collective-permute-start(bf16[40,1024]{1,0:T(8,128)(2,1)S(1)} %add_parts.7.refs_0_), channel_id=1, source_target_pairs={{0,128},{64,192},{128,0},{192,64},{1,129},{65,193},{129,1},{193,65... | collective-permute-start | bytes 245768 | tf_op jit(solution)/shard_map/ppermute | solution.py:413
  147.4 5.7 %collective-permute-start.38 = (bf16[40,1024]{1,0:T(8,128)(2,1)S(1)}, bf16[40,1024]{1,0:T(8,128)(2,1)S(1)}, u32[]{:S(2)}, u32[]{:S(2)}) collective-permute-start(bf16[40,1024]{1,0:T(8,128)(2,1)S(1)} %add_parts.7.refs_0_), channel_id=1, source_target_pairs={{0,64},{64,128},{128,192},{192,0},{1,65},{65,129},{129,193},{193,1... | collective-permute-start | bytes 245768 | tf_op jit(solution)/shard_map/ppermute | solution.py:413
  (8 other events, 41.0 us)

commit v2 on v0

--- a/solution.py
+++ b/solution.py
@@ -149,12 +149,12 @@
 
     def tile(ct, carry):
         lanes = pl.ds(pl.multiple_of(ct * 128, 128), 128)
-        ut[...] = rounded(mk[:, lanes] * mv[:, lanes])
+        ut[0:EXT, :] = rounded(mk[:, lanes] * mv[:, lanes])
         lane = pl.multiple_of(nexts.shape[1] - PADC + ct * 128, 128)
         after = nexts[:, pl.ds(lane, 128)].astype(F32)
         cot = jnp.concatenate([cown[:, lanes], after[0 : EXT - 128]], axis=0)
         cots[:, lanes] = cot
-        dt[...] = rounded(cot * mq[:, lanes])
+        dt[0:EXT, :] = rounded(cot * mq[:, lanes])
         rate = rates[:, lanes]
         decay = jnp.exp(-rate)
         for half in range(2):
@@ -233,8 +233,8 @@
         far = pz[part, :] + jnp.exp(-rate * (4 * own * mid).astype(F32)) * px[part, :]
         inc[part, :] = py[part, :] + jnp.exp(-rate * (own * near).astype(F32)) * far
     sub = lax.broadcasted_iota(jnp.int32, (8, 128), 0)
-    ut[...] = rounded(mk[...] * mv[...])
-    dt[...] = rounded(cots[...] * mq[...])
+    ut[0:EXT, :] = rounded(mk[...] * mv[...])
+    dt[0:EXT, :] = rounded(cots[...] * mq[...])
     decay = jnp.exp(-rate)
     gain = reff[...]
     for half in range(2):
@@ -279,8 +279,8 @@
             if half:
                 total = total + dps[pl.ds(t, 8, stride=SEG), :]
             dps[pl.ds(t, 8, stride=SEG), :] = total
-    long_out = rounded(longs[...])
-    dprod = rounded(dps[...])
+    long_out = rounded(longs[0:EXT, :])
+    dprod = rounded(dps[0:EXT, :])
     outt[...] = (mq[0:own, :] * long_out[0:own]).T.astype(BF16)
     dms[0] = rounded(cots[...] * long_out)
     dms[1] = rounded(dprod * mv[...])
@@ -532,8 +532,8 @@
             jax.ShapeDtypeStruct((2 * MODES, PADC), BF16),
         ],
         scratch_shapes=[
-            pltpu.VMEM((EXT, 128), F32),
-            pltpu.VMEM((EXT, 128), F32),
+            pltpu.VMEM((EXT + 24, 128), F32),
+            pltpu.VMEM((EXT + 24, 128), F32),
             pltpu.VMEM((2 * MODES, PADC), F32),
         ],
         compiler_params=params(16),
@@ -604,10 +604,10 @@
         scratch_shapes=[
             pltpu.VMEM((40, 128), F32),
             pltpu.VMEM((2 * MODES, 128), F32),
-            pltpu.VMEM((EXT, 128), F32),
-            pltpu.VMEM((EXT, 128), F32),
-            pltpu.VMEM((EXT, 128), F32),
-            pltpu.VMEM((EXT, 128), F32),
+            pltpu.VMEM((EXT + 24, 128), F32),
+            pltpu.VMEM((EXT + 24, 128), F32),
+            pltpu.VMEM((EXT + 24, 128), F32),
+            pltpu.VMEM((EXT + 24, 128), F32),
             pltpu.VMEM((3, EXT, 128), F32),
             pltpu.VMEM((3, PADC, own), F32),
         ],

time: 157 us -> 157 us (level)
  no operation moved by 1% of the time
where the time goes in v2:
time: 157 us; the launch traced here: 156 us
  starting transfers between devices  74.9 us (48%)
  waiting for transfers between devices  39.9 us (25%)
  Pallas kernels  36.9 us (24%)
  local copies, waits for them, and re-layouts  3.77 us (2%)
    ppermute x30, starting transfers between devices, ring(): return lax.ppermute(a, ax, [(i, (i + d) % 4) for i in range(4)])  47.2 us
    ppermute x30, waiting for transfers between devices, ring(): return lax.ppermute(a, ax, [(i, (i + d) % 4) for i in range(4)])  25.4 us
    pallas_call x1, Pallas kernels, local(): pl.pallas_call(finish, grid=(PADC // 128,), in_specs=[smem, smem, *[tiles...  9.63 us
    pallas_call x2, Pallas kernels, project(): pl.pallas_call(make_project(part), in_specs=[vm] * (2 + part) + [anywhere...  9.62 us
    all_to_all x1, starting transfers between devices, local(): last = lax.all_to_all(blocks, ('zl', 'y', 'zh'), 0, 0, tiled=True)  9.58 us
    ppermute x2, waiting for transfers between devices, swap(): return [a, lax.ppermute(a, ax, [(0, 1), (1, 0)])]  6.02 us
    pallas_call x1, Pallas kernels, local(): pl.pallas_call(token_grads, grid=(3,), in_specs=[pl.BlockSpec((1, own, PA...  6.01 us
    ppermute x2, starting transfers between devices, swap(): return [a, lax.ppermute(a, ax, [(0, 1), (1, 0)])]  5.08 us
  transfers between devices with their start and end apart: 43, of which 22 were waited for; matrix products, arithmetic and copies ran while one was open for 0% of the time, Pallas kernels for 18%

profile of v2, /device:TPU:32, one launch (start us, length us, event | category | flops | bytes accessed | tf_op | source)
XLA Modules:
  0.0 156.4 jit_solution(7561374958525684248)
XLA Ops:
  0.7 2.2 %prepare.1 = (bf16[16,2560]{1,0:T(8,128)(2,1)}, bf16[16,1536]{1,0:T(8,128)(2,1)}, f32[32,15]{1,0:T(8,128)}, f32[3,8,1024]{2,1,0:T(8,128)}, f32[15,16]{1,0:T(8,128)}, /*index=5*/f32[128,1024]{1,0:T(8,128)}) custom-call(bf16[128,1536]{1,0:T(8,128)(2,1)} %bitcast.12, bf16[960,128]{1,0:T(8,128)(2,1)} %bitcast.23, f32[15,16]{1,0:T(8,128)} %rates, ...), custom_call_target="tpu_custom_call" | custom-call | tf_op jit(solution)/shard_map/prepare/pallas_call | solution.py:440
  2.9 4.5 %collective-permute-start.1 = (bf16[16,2560]{1,0:T(8,128)(2,1)}, bf16[16,2560]{1,0:T(8,128)(2,1)S(1)}, u32[]{:S(2)}, u32[]{:S(2)}) collective-permute-start(bf16[16,2560]{1,0:T(8,128)(2,1)} %get-tuple-element.94), channel_id=1, source_target_pairs={{4,0},{8,4},{12,8},{16,12},{20,16},{24,20},{28,24},{32,28},{36,32}... | collective-permute-start | bytes 245768 | tf_op jit(solution)/shard_map/ppermute | solution.py:465
  7.4 1.9 %collective-permute-start = (bf16[16,1536]{1,0:T(8,128)(2,1)}, bf16[16,1536]{1,0:T(8,128)(2,1)S(1)}, u32[]{:S(2)}, u32[]{:S(2)}) collective-permute-start(bf16[16,1536]{1,0:T(8,128)(2,1)} %get-tuple-element.93), channel_id=1, source_target_pairs={{0,4},{4,8},{8,12},{12,16},{16,20},{20,24},{24,28},{28,32},{32,36}... | collective-permute-start | bytes 147464 | tf_op jit(solution)/shard_map/ppermute | solution.py:464
  9.3 4.7 %collective-permute-start.4 = (f32[32,15]{1,0:T(8,128)}, f32[32,15]{1,0:T(8,128)S(1)}, u32[]{:S(2)}, u32[]{:S(2)}) collective-permute-start(f32[32,15]{1,0:T(8,128)} %get-tuple-element.99.r0), channel_id=1, source_target_pairs={{0,12},{4,0},{8,4},{12,8},{1,13},{5,1},{9,5},{13,9},{2,14},{6,2},{... | collective-permute-start | bytes 5768 | tf_op jit(solution)/shard_map/ppermute | solution.py:413
  16.7 4.7 %project.2.refs_2_ = f32[160,2880]{1,0:T(8,128)} custom-call(bf16[16,1536]{1,0:T(8,128)(2,1)S(1)} %collective-permute-done.refs_0_, bf16[16,2560]{1,0:T(8,128)(2,1)S(1)} %collective-permute-done.1.refs_1_.nexts, bf16[128,1536]{1,0:T(8,128)(2,1)S(1)} %bitcast.13, bf16[2880,1536]{1,0:T(8,128)(2,1)} %bitcast.19), custom_call_target="tpu_custom_call" | custom-call | flops 800000000 | bytes 6000000 | tf_op jit(solution)/shard_map/project/pallas_call | solution.py:472
  21.6 5.3 %collective-permute-start.6 = (f32[32,60]{1,0:T(8,128)S(1)}, f32[32,60]{1,0:T(8,128)S(1)}, u32[]{:S(2)}, u32[]{:S(2)}) collective-permute-start(f32[32,60]{1,0:T(8,128)S(1)} %join_params.2.r0), channel_id=1, source_target_pairs={{0,32},{16,48},{32,0},{48,16},{1,33},{17,49},{33,1},{49,17},{2,34}... | collective-permute-start | bytes 23048 | tf_op jit(solution)/shard_map/ppermute | solution.py:413
  26.9 2.8 %collective-permute-start.5 = (f32[32,60]{1,0:T(8,128)S(1)}, f32[32,60]{1,0:T(8,128)S(1)}, u32[]{:S(2)}, u32[]{:S(2)}) collective-permute-start(f32[32,60]{1,0:T(8,128)S(1)} %join_params.2.r0), channel_id=1, source_target_pairs={{0,16},{16,32},{32,48},{48,0},{1,17},{17,33},{33,49},{49,1},{2,18}... | collective-permute-start | bytes 23048 | tf_op jit(solution)/shard_map/ppermute | solution.py:413
  29.8 4.9 %project.3 = (f32[160,1024]{1,0:T(8,128)S(1)}, f32[160,1024]{1,0:T(8,128)S(1)}, f32[160,1024]{1,0:T(8,128)S(1)}) custom-call(bf16[16,1536]{1,0:T(8,128)(2,1)S(1)} %collective-permute-done.refs_0_, bf16[16,2560]{1,0:T(8,128)(2,1)S(1)} %collective-permute-done.1.refs_1_.nexts, f32[160,2880]{1,0:T(8,128)} %project.2.refs_2_, bf16[128,1536]{1,0:T(8,128)(2,1)S(1)} %bitcast.14, ...), custom_call_target="tpu_custom_call" | custom-call | flops 800000000 | bytes 6000000 | tf_op jit(solution)/shard_map/project/pallas_call | solution.py:472
  34.8 3.9 %collective-permute-start.10 = (f32[32,240]{1,0:T(8,128)S(1)}, f32[32,240]{1,0:T(8,128)S(1)}, u32[]{:S(2)}, u32[]{:S(2)}) collective-permute-start(f32[32,240]{1,0:T(8,128)S(1)} %join_params.3.r0), channel_id=1, source_target_pairs={{0,192},{64,0},{128,64},{192,128},{1,193},{65,1},{129,65},{193,129... | collective-permute-start | bytes 92168 | tf_op jit(solution)/shard_map/ppermute | solution.py:413
  40.1 1.4 mix_taps.1
  41.6 2.6 %collective-permute-done.9.r2 = f32[32,240]{1,0:T(8,128)S(1)} collective-permute-done((f32[32,240]{1,0:T(8,128)S(1)}, f32[32,240]{1,0:T(8,128)S(1)}, u32[]{:S(2)}, u32[]{:S(2)}) %collective-permute-start.9) | collective-permute-done | bytes 30752 | tf_op jit(solution)/shard_map/ppermute | solution.py:413
  44.5 2.2 %end_states.1 = (f32[136,1024]{1,0:T(8,128)S(1)}, f32[16,1024]{1,0:T(8,128)S(1)}, f32[16,1024]{1,0:T(8,128)S(1)}, f32[2,16,8,1024]{3,2,1,0:T(8,128)S(1)}, f32[32...) custom-call(s32[1]{0:T(128)} %bitcast.6.me.index.xi, f32[32,240]{1,0:T(8,128)S(1)} %join_params.3.r0, ...), custom_call_target="tpu_custom_call" | custom-call | flops 20000000 | bytes 3000000 | tf_op jit(solution)/shard_map/end_states/pallas_call | solution.py:522
  46.7 1.5 collective-permute-start.13
  48.2 2.3 %collective-permute-start.12 = (bf16[32,1024]{1,0:T(8,128)(2,1)S(1)}, bf16[32,1024]{1,0:T(8,128)(2,1)S(1)}, u32[]{:S(2)}, u32[]{:S(2)}) collective-permute-start(bf16[32,1024]{1,0:T(8,128)(2,1)S(1)} %get-tuple-element.122), channel_id=1, source_target_pairs={{0,8},{4,12},{8,0},{12,4},{1,9},{5,13},{9,1},{13,5},{2,10},{6,14},... | collective-permute-start | bytes 196616 | tf_op jit(solution)/shard_map/ppermute | solution.py:413
  51.0 2.9 %collective-permute-done.12.r2 = bf16[32,1024]{1,0:T(8,128)(2,1)S(1)} collective-permute-done((bf16[32,1024]{1,0:T(8,128)(2,1)S(1)}, bf16[32,1024]{1,0:T(8,128)(2,1)S(1)}, u32[]{:S(2)}, u32[]{:S(2)}) %collective-permute-start.12) | collective-permute-done | bytes 65568 | tf_op jit(solution)/shard_map/ppermute | solution.py:413
  53.9 2.0 %collective-permute-done.11.r1 = bf16[32,1024]{1,0:T(8,128)(2,1)S(1)} collective-permute-done((bf16[32,1024]{1,0:T(8,128)(2,1)S(1)}, bf16[32,1024]{1,0:T(8,128)(2,1)S(1)}, u32[]{:S(2)}, u32[]{:S(2)}) %collective-permute-start.11) | collective-permute-done | bytes 65568 | tf_op jit(solution)/shard_map/ppermute | solution.py:413
  56.3 1.5 collective-permute-start.15
  57.7 2.4 %collective-permute-start.14 = (bf16[32,1024]{1,0:T(8,128)(2,1)S(1)}, bf16[32,1024]{1,0:T(8,128)(2,1)S(1)}, u32[]{:S(2)}, u32[]{:S(2)}) collective-permute-start(bf16[32,1024]{1,0:T(8,128)(2,1)S(1)} %get-tuple-element.126), channel_id=1, source_target_pairs={{0,16},{16,32},{32,48},{48,0},{1,17},{17,33},{33,49},{49,1},{2,18}... | collective-permute-start | bytes 196616 | tf_op jit(solution)/shard_map/ppermute | solution.py:413
  61.5 1.2 collective-permute-done.14.r1
  62.9 1.1 collective-permute-start.18
  64.5 1.1 collective-permute-start.20
  65.6 1.4 collective-permute-start.19
  67.0 1.2 collective-permute-done.21.r3
  68.2 2.1 %collective-permute-done.20.r2 = bf16[32,1024]{1,0:T(8,128)(2,1)S(1)} collective-permute-done((bf16[32,1024]{1,0:T(8,128)(2,1)S(1)}, bf16[32,1024]{1,0:T(8,128)(2,1)S(1)}, u32[]{:S(2)}, u32[]{:S(2)}) %collective-permute-start.20) | collective-permute-done | bytes 65568 | tf_op jit(solution)/shard_map/ppermute | solution.py:413
  71.9 4.2 %collective-permute-done.18.refs_2_ = bf16[128,1536]{1,0:T(8,128)(2,1)S(1)} collective-permute-done((bf16[128,1536]{1,0:T(8,128)(2,1)S(1)}, bf16[128,1536]{1,0:T(8,128)(2,1)S(1)}, u32[]{:S(2)}, u32[]{:S(2)}) %collective-permute-start.18) | collective-permute-done | bytes 393248 | tf_op jit(solution)/shard_map/ppermute | solution.py:564
  76.3 9.6 %finish.1 = (bf16[960,128]{1,0:T(8,128)(2,1)}, bf16[3,128,1024]{2,1,0:T(8,128)(2,1)}, bf16[8,360,128]{2,1,0:T(8,128)(2,1)}, bf16[40,1024]{1,0:T(8,128)(2,1)S(1)}) custom-call(s32[1]{0:T(128)} %bitcast.2.me.index.zi, s32[1]{0:T(128)} %bitcast.3.me.index.yi, f32[160,1024]{1,0:T(8,128)S(1)} %get-tuple-element.97.zq, f32[160,1024]{1,0:T(8,128)} %copy-done.3, ...), custom_call_target="tpu_custom_call" | custom-call | flops 200000000 | bytes 10000000 | tf_op jit(solution)/shard_map/finish/pallas_call | solution.py:575
  85.9 4.3 %all-to-all-start = ((bf16[8,360,128]{2,1,0:T(8,128)(2,1)}), bf16[8,360,128]{2,1,0:T(8,128)(2,1)S(1)}, u32[]{:S(2)}, u32[]{:S(2)}) async-start(bf16[8,360,128]{2,1,0:T(8,128)(2,1)} %get-tuple-element.146), calls=%async_computation | async-start | bytes 1474560 | tf_op jit(solution)/shard_map/all_to_all | solution.py:640
  91.8 2.1 %collective-permute-done.27.refs_1_ = bf16[40,1024]{1,0:T(8,128)(2,1)S(1)} collective-permute-done((bf16[40,1024]{1,0:T(8,128)(2,1)S(1)}, bf16[40,1024]{1,0:T(8,128)(2,1)S(1)}, u32[]{:S(2)}, u32[]{:S(2)}) %collective-permute-start.27) | collective-permute-done | bytes 81952 | tf_op jit(solution)/shard_map/ppermute | solution.py:628
  94.7 2.6 %collective-permute-start.30 = (bf16[40,1024]{1,0:T(8,128)(2,1)S(1)}, bf16[40,1024]{1,0:T(8,128)(2,1)S(1)}, u32[]{:S(2)}, u32[]{:S(2)}) collective-permute-start(bf16[40,1024]{1,0:T(8,128)(2,1)S(1)} %add_parts.4.refs_0_), channel_id=1, source_target_pairs={{0,48},{16,0},{32,16},{48,32},{1,49},{17,1},{33,17},{49,33},{2,50}... | collective-permute-start | bytes 245768 | tf_op jit(solution)/shard_map/ppermute | solution.py:413
  97.6 1.7 %collective-permute-start.28 = (bf16[40,1024]{1,0:T(8,128)(2,1)S(1)}, bf16[40,1024]{1,0:T(8,128)(2,1)S(1)}, u32[]{:S(2)}, u32[]{:S(2)}) collective-permute-start(bf16[40,1024]{1,0:T(8,128)(2,1)S(1)} %add_parts.4.refs_0_), channel_id=1, source_target_pairs={{0,16},{16,32},{32,48},{48,0},{1,17},{17,33},{33,49},{49,1},{2,18}... | collective-permute-start | bytes 245768 | tf_op jit(solution)/shard_map/ppermute | solution.py:413
  99.3 6.0 %token_grads.1 = bf16[128,1536]{1,0:T(8,128)(2,1)} custom-call(bf16[3,128,1024]{2,1,0:T(8,128)(2,1)} %get-tuple-element.143.dz, bf16[2880,1536]{1,0:T(8,128)(2,1)} %bitcast.21), custom_call_target="tpu_custom_call" | custom-call | flops 1200000000 | bytes 11000000 | tf_op jit(solution)/shard_map/token_grads/pallas_call | solution.py:644
  107.4 1.7 %weight_term.1 = (bf16[360,384]{1,0:T(8,128)(2,1)S(1)}, bf16[360,384]{1,0:T(8,128)(2,1)S(1)}, bf16[360,384]{1,0:T(8,128)(2,1)S(1)}, bf16[360,384]{1,0:T(8,128)(2,1)S(1)}) custom-call(s32[1]{0:T(128)} %bitcast.6.me.index.xi, s32[1]{0:T(128)} %bitcast.3.me.index.yi, s32[1]{0:T(128)} %bitcast.10.ci, bf16[8,360,128]{2,1,0:T(8,128)(2,1)S(1)} %all-to-all-done.arrived, ...), custom_call_target="tpu_custom_call" | custom-call | flops 1200000000 | bytes 6000000 | tf_op jit(solution)/shard_map/weight_term/pallas_call | solution.py:661
  109.2 1.8 %collective-permute-start.32 = (bf16[360,384]{1,0:T(8,128)(2,1)S(1)}, bf16[360,384]{1,0:T(8,128)(2,1)S(1)}, u32[]{:S(2)}, u32[]{:S(2)}) collective-permute-start(bf16[360,384]{1,0:T(8,128)(2,1)S(1)} %get-tuple-element.158), channel_id=1, source_target_pairs={{0,128},{64,192},{128,0},{192,64},{1,129},{65,193},{129,1},{193,65... | collective-permute-start | bytes 829448 | tf_op jit(solution)/shard_map/ppermute | solution.py:413
  111.0 1.6 %collective-permute-start.33 = (bf16[360,384]{1,0:T(8,128)(2,1)S(1)}, bf16[360,384]{1,0:T(8,128)(2,1)S(1)}, u32[]{:S(2)}, u32[]{:S(2)}) collective-permute-start(bf16[360,384]{1,0:T(8,128)(2,1)S(1)} %get-tuple-element.159), channel_id=1, source_target_pairs={{0,192},{64,0},{128,64},{192,128},{1,193},{65,1},{129,65},{193,129... | collective-permute-start | bytes 829448 | tf_op jit(solution)/shard_map/ppermute | solution.py:413
  112.6 3.1 %collective-permute-start.36 = (bf16[40,1024]{1,0:T(8,128)(2,1)S(1)}, bf16[40,1024]{1,0:T(8,128)(2,1)S(1)}, u32[]{:S(2)}, u32[]{:S(2)}) collective-permute-start(bf16[40,1024]{1,0:T(8,128)(2,1)S(1)} %add_parts.5.refs_0_), channel_id=1, source_target_pairs={{0,12},{4,0},{8,4},{12,8},{1,13},{5,1},{9,5},{13,9},{2,14},{6,2},{... | collective-permute-start | bytes 245768 | tf_op jit(solution)/shard_map/ppermute | solution.py:413
  116.5 1.3 collective-permute-done.36.refs_3_
  117.8 1.4 collective-permute-start.34
  119.2 3.0 %collective-permute-done.35.refs_2_ = bf16[40,1024]{1,0:T(8,128)(2,1)S(1)} collective-permute-done((bf16[40,1024]{1,0:T(8,128)(2,1)S(1)}, bf16[40,1024]{1,0:T(8,128)(2,1)S(1)}, u32[]{:S(2)}, u32[]{:S(2)}) %collective-permute-start.35) | collective-permute-done | bytes 81952 | tf_op jit(solution)/shard_map/ppermute | solution.py:413
  122.2 1.7 %collective-permute-done.34.refs_1_ = bf16[40,1024]{1,0:T(8,128)(2,1)S(1)} collective-permute-done((bf16[40,1024]{1,0:T(8,128)(2,1)S(1)}, bf16[40,1024]{1,0:T(8,128)(2,1)S(1)}, u32[]{:S(2)}, u32[]{:S(2)}) %collective-permute-start.34) | collective-permute-done | bytes 81952 | tf_op jit(solution)/shard_map/ppermute | solution.py:413
  123.9 4.6 %collective-permute-start.37 = (bf16[40,1024]{1,0:T(8,128)(2,1)S(1)}, bf16[40,1024]{1,0:T(8,128)(2,1)S(1)}, u32[]{:S(2)}, u32[]{:S(2)}) collective-permute-start(bf16[40,1024]{1,0:T(8,128)(2,1)S(1)} %add_parts.6.refs_0_), channel_id=1, source_target_pairs={{0,2},{2,0},{1,3},{3,1},{4,6},{6,4},{5,7},{7,5},{8,10},{10,8},{9,1... | collective-permute-start | bytes 245768 | tf_op jit(solution)/shard_map/ppermute | solution.py:628
  128.5 3.9 %collective-permute-done.37.refs_1_ = bf16[40,1024]{1,0:T(8,128)(2,1)S(1)} collective-permute-done((bf16[40,1024]{1,0:T(8,128)(2,1)S(1)}, bf16[40,1024]{1,0:T(8,128)(2,1)S(1)}, u32[]{:S(2)}, u32[]{:S(2)}) %collective-permute-start.37) | collective-permute-done | bytes 81952 | tf_op jit(solution)/shard_map/ppermute | solution.py:628
  132.4 1.1 split_rows.1
  133.5 9.6 %all-to-all-start.1 = ((bf16[32,24,180]{2,1,0:T(8,128)(2,1)}), bf16[32,24,180]{2,1,0:T(8,128)(2,1)S(1)}, u32[]{:S(2)}, u32[]{:S(2)}) async-start(bf16[32,24,180]{2,1,0:T(8,128)(2,1)} %split_rows.1), calls=%async_computation.1 | async-start | bytes 786432 | tf_op jit(solution)/shard_map/all_to_all | solution.py:683
  143.7 2.1 %collective-permute-start.39 = (bf16[40,1024]{1,0:T(8,128)(2,1)S(1)}, bf16[40,1024]{1,0:T(8,128)(2,1)S(1)}, u32[]{:S(2)}, u32[]{:S(2)}) collective-permute-start(bf16[40,1024]{1,0:T(8,128)(2,1)S(1)} %add_parts.7.refs_0_), channel_id=1, source_target_pairs={{0,128},{64,192},{128,0},{192,64},{1,129},{65,193},{129,1},{193,65... | collective-permute-start | bytes 245768 | tf_op jit(solution)/shard_map/ppermute | solution.py:413
  145.8 1.3 collective-permute-start.38
  147.6 2.1 %collective-permute-done.39.refs_2_ = bf16[40,1024]{1,0:T(8,128)(2,1)S(1)} collective-permute-done((bf16[40,1024]{1,0:T(8,128)(2,1)S(1)}, bf16[40,1024]{1,0:T(8,128)(2,1)S(1)}, u32[]{:S(2)}, u32[]{:S(2)}) %collective-permute-start.39) | collective-permute-done | bytes 81952 | tf_op jit(solution)/shard_map/ppermute | solution.py:413
  149.7 1.8 %collective-permute-done.38.refs_1_ = bf16[40,1024]{1,0:T(8,128)(2,1)S(1)} collective-permute-done((bf16[40,1024]{1,0:T(8,128)(2,1)S(1)}, bf16[40,1024]{1,0:T(8,128)(2,1)S(1)}, u32[]{:S(2)}, u32[]{:S(2)}) %collective-permute-start.38) | collective-permute-done | bytes 81952 | tf_op jit(solution)/shard_map/ppermute | solution.py:413
  152.2 3.5 %all-to-all-done.1.last = bf16[32,24,180]{2,1,0:T(8,128)(2,1)S(1)} async-done(((bf16[32,24,180]{2,1,0:T(8,128)(2,1)}), bf16[32,24,180]{2,1,0:T(8,128)(2,1)S(1)}, u32[]{:S(2)}, u32[]{:S(2)}) %all-to-all-start.1) | async-done | bytes 276512 | tf_op jit(solution)/shard_map/all_to_all | solution.py:683
  (84 shorter events, 17.9 us)
Async XLA Ops:
  0.6 29.1 %copy-start.1 = (bf16[1,128,1536]{2,1,0:T(8,128)(2,1)S(1)}, bf16[1,128,1536]{2,1,0:T(8,128)(2,1)}, u32[]{:S(2)}) copy-start(bf16[1,128,1536]{2,1,0:T(8,128)(2,1)} %param.6) | copy-start | bytes 1179652
  2.9 12.8 %collective-permute-start.1 = (bf16[16,2560]{1,0:T(8,128)(2,1)}, bf16[16,2560]{1,0:T(8,128)(2,1)S(1)}, u32[]{:S(2)}, u32[]{:S(2)}) collective-permute-start(bf16[16,2560]{1,0:T(8,128)(2,1)} %get-tuple-element.94), channel_id=1, source_target_pairs={{4,0},{8,4},{12,8},{16,12},{20,16},{24,20},{28,24},{32,28},{36,32}... | collective-permute-start | bytes 245768 | tf_op jit(solution)/shard_map/ppermute | solution.py:465
  7.4 8.3 %collective-permute-start = (bf16[16,1536]{1,0:T(8,128)(2,1)}, bf16[16,1536]{1,0:T(8,128)(2,1)S(1)}, u32[]{:S(2)}, u32[]{:S(2)}) collective-permute-start(bf16[16,1536]{1,0:T(8,128)(2,1)} %get-tuple-element.93), channel_id=1, source_target_pairs={{0,4},{4,8},{8,12},{12,16},{16,20},{20,24},{24,28},{28,32},{32,36}... | collective-permute-start | bytes 147464 | tf_op jit(solution)/shard_map/ppermute | solution.py:464
  9.3 12.1 %collective-permute-start.4 = (f32[32,15]{1,0:T(8,128)}, f32[32,15]{1,0:T(8,128)S(1)}, u32[]{:S(2)}, u32[]{:S(2)}) collective-permute-start(f32[32,15]{1,0:T(8,128)} %get-tuple-element.99.r0), channel_id=1, source_target_pairs={{0,12},{4,0},{8,4},{12,8},{1,13},{5,1},{9,5},{13,9},{2,14},{6,2},{... | collective-permute-start | bytes 5768 | tf_op jit(solution)/shard_map/ppermute | solution.py:413
  13.9 7.5 %collective-permute-start.3 = (f32[32,15]{1,0:T(8,128)}, f32[32,15]{1,0:T(8,128)S(1)}, u32[]{:S(2)}, u32[]{:S(2)}) collective-permute-start(f32[32,15]{1,0:T(8,128)} %get-tuple-element.99.r0), channel_id=1, source_target_pairs={{0,8},{4,12},{8,0},{12,4},{1,9},{5,13},{9,1},{13,5},{2,10},{6,14},... | collective-permute-start | bytes 5768 | tf_op jit(solution)/shard_map/ppermute | solution.py:413
  13.9 7.5 %collective-permute-start.2 = (f32[32,15]{1,0:T(8,128)}, f32[32,15]{1,0:T(8,128)S(1)}, u32[]{:S(2)}, u32[]{:S(2)}) collective-permute-start(f32[32,15]{1,0:T(8,128)} %get-tuple-element.99.r0), channel_id=1, source_target_pairs={{0,4},{4,8},{8,12},{12,0},{1,5},{5,9},{9,13},{13,1},{2,6},{6,10},{... | collective-permute-start | bytes 5768 | tf_op jit(solution)/shard_map/ppermute | solution.py:413
  21.5 13.2 %collective-permute-start.7 = (f32[32,60]{1,0:T(8,128)S(1)}, f32[32,60]{1,0:T(8,128)S(1)}, u32[]{:S(2)}, u32[]{:S(2)}) collective-permute-start(f32[32,60]{1,0:T(8,128)S(1)} %join_params.2.r0), channel_id=1, source_target_pairs={{0,48},{16,0},{32,16},{48,32},{1,49},{17,1},{33,17},{49,33},{2,50}... | collective-permute-start | bytes 23048 | tf_op jit(solution)/shard_map/ppermute | solution.py:413
  21.6 13.1 %collective-permute-start.6 = (f32[32,60]{1,0:T(8,128)S(1)}, f32[32,60]{1,0:T(8,128)S(1)}, u32[]{:S(2)}, u32[]{:S(2)}) collective-permute-start(f32[32,60]{1,0:T(8,128)S(1)} %join_params.2.r0), channel_id=1, source_target_pairs={{0,32},{16,48},{32,0},{48,16},{1,33},{17,49},{33,1},{49,17},{2,34}... | collective-permute-start | bytes 23048 | tf_op jit(solution)/shard_map/ppermute | solution.py:413
  26.9 7.8 %collective-permute-start.5 = (f32[32,60]{1,0:T(8,128)S(1)}, f32[32,60]{1,0:T(8,128)S(1)}, u32[]{:S(2)}, u32[]{:S(2)}) collective-permute-start(f32[32,60]{1,0:T(8,128)S(1)} %join_params.2.r0), channel_id=1, source_target_pairs={{0,16},{16,32},{32,48},{48,0},{1,17},{17,33},{33,49},{49,1},{2,18}... | collective-permute-start | bytes 23048 | tf_op jit(solution)/shard_map/ppermute | solution.py:413
  34.7 41.6 %copy-start.3 = (f32[160,1024]{1,0:T(8,128)}, f32[160,1024]{1,0:T(8,128)S(1)}, u32[]{:S(2)}) copy-start(f32[160,1024]{1,0:T(8,128)S(1)} %get-tuple-element.98.zk) | copy-start | bytes 1966084
  34.7 41.6 %copy-start.4 = (f32[160,1024]{1,0:T(8,128)}, f32[160,1024]{1,0:T(8,128)S(1)}, u32[]{:S(2)}) copy-start(f32[160,1024]{1,0:T(8,128)S(1)} %get-tuple-element.104.zv) | copy-start | bytes 1966084
  34.8 6.7 %collective-permute-start.10 = (f32[32,240]{1,0:T(8,128)S(1)}, f32[32,240]{1,0:T(8,128)S(1)}, u32[]{:S(2)}, u32[]{:S(2)}) collective-permute-start(f32[32,240]{1,0:T(8,128)S(1)} %join_params.3.r0), channel_id=1, source_target_pairs={{0,192},{64,0},{128,64},{192,128},{1,193},{65,1},{129,65},{193,129... | collective-permute-start | bytes 92168 | tf_op jit(solution)/shard_map/ppermute | solution.py:413
  38.7 5.4 %collective-permute-start.9 = (f32[32,240]{1,0:T(8,128)S(1)}, f32[32,240]{1,0:T(8,128)S(1)}, u32[]{:S(2)}, u32[]{:S(2)}) collective-permute-start(f32[32,240]{1,0:T(8,128)S(1)} %join_params.3.r0), channel_id=1, source_target_pairs={{0,128},{64,192},{128,0},{192,64},{1,129},{65,193},{129,1},{193,65... | collective-permute-start | bytes 92168 | tf_op jit(solution)/shard_map/ppermute | solution.py:413
  39.2 5.3 %collective-permute-start.8 = (f32[32,240]{1,0:T(8,128)S(1)}, f32[32,240]{1,0:T(8,128)S(1)}, u32[]{:S(2)}, u32[]{:S(2)}) collective-permute-start(f32[32,240]{1,0:T(8,128)S(1)} %join_params.3.r0), channel_id=1, source_target_pairs={{0,64},{64,128},{128,192},{192,0},{1,65},{65,129},{129,193},{193,1... | collective-permute-start | bytes 92168 | tf_op jit(solution)/shard_map/ppermute | solution.py:413
  46.7 29.4 %copy-start.2 = (f32[2,16,8,1024]{3,2,1,0:T(8,128)}, f32[2,16,8,1024]{3,2,1,0:T(8,128)S(1)}, u32[]{:S(2)}) copy-start(f32[2,16,8,1024]{3,2,1,0:T(8,128)S(1)} %get-tuple-element.120.es) | copy-start | bytes 3145732
  46.7 4.3 %collective-permute-start.13 = (bf16[32,1024]{1,0:T(8,128)(2,1)S(1)}, bf16[32,1024]{1,0:T(8,128)(2,1)S(1)}, u32[]{:S(2)}, u32[]{:S(2)}) collective-permute-start(bf16[32,1024]{1,0:T(8,128)(2,1)S(1)} %get-tuple-element.122), channel_id=1, source_target_pairs={{0,12},{4,0},{8,4},{12,8},{1,13},{5,1},{9,5},{13,9},{2,14},{6,2},{... | collective-permute-start | bytes 196616 | tf_op jit(solution)/shard_map/ppermute | solution.py:413
  48.2 5.8 %collective-permute-start.12 = (bf16[32,1024]{1,0:T(8,128)(2,1)S(1)}, bf16[32,1024]{1,0:T(8,128)(2,1)S(1)}, u32[]{:S(2)}, u32[]{:S(2)}) collective-permute-start(bf16[32,1024]{1,0:T(8,128)(2,1)S(1)} %get-tuple-element.122), channel_id=1, source_target_pairs={{0,8},{4,12},{8,0},{12,4},{1,9},{5,13},{9,1},{13,5},{2,10},{6,14},... | collective-permute-start | bytes 196616 | tf_op jit(solution)/shard_map/ppermute | solution.py:413
  50.5 5.5 %collective-permute-start.11 = (bf16[32,1024]{1,0:T(8,128)(2,1)S(1)}, bf16[32,1024]{1,0:T(8,128)(2,1)S(1)}, u32[]{:S(2)}, u32[]{:S(2)}) collective-permute-start(bf16[32,1024]{1,0:T(8,128)(2,1)S(1)} %get-tuple-element.122), channel_id=1, source_target_pairs={{0,4},{4,8},{8,12},{12,0},{1,5},{5,9},{9,13},{13,1},{2,6},{6,10},{... | collective-permute-start | bytes 196616 | tf_op jit(solution)/shard_map/ppermute | solution.py:413
  56.2 4.3 %collective-permute-start.16 = (bf16[32,1024]{1,0:T(8,128)(2,1)S(1)}, bf16[32,1024]{1,0:T(8,128)(2,1)S(1)}, u32[]{:S(2)}, u32[]{:S(2)}) collective-permute-start(bf16[32,1024]{1,0:T(8,128)(2,1)S(1)} %get-tuple-element.126), channel_id=1, source_target_pairs={{0,48},{16,0},{32,16},{48,32},{1,49},{17,1},{33,17},{49,33},{2,50}... | collective-permute-start | bytes 196616 | tf_op jit(solution)/shard_map/ppermute | solution.py:413
  56.3 5.3 %collective-permute-start.15 = (bf16[32,1024]{1,0:T(8,128)(2,1)S(1)}, bf16[32,1024]{1,0:T(8,128)(2,1)S(1)}, u32[]{:S(2)}, u32[]{:S(2)}) collective-permute-start(bf16[32,1024]{1,0:T(8,128)(2,1)S(1)} %get-tuple-element.126), channel_id=1, source_target_pairs={{0,32},{16,48},{32,0},{48,16},{1,33},{17,49},{33,1},{49,17},{2,34}... | collective-permute-start | bytes 196616 | tf_op jit(solution)/shard_map/ppermute | solution.py:413
  57.7 5.0 %collective-permute-start.14 = (bf16[32,1024]{1,0:T(8,128)(2,1)S(1)}, bf16[32,1024]{1,0:T(8,128)(2,1)S(1)}, u32[]{:S(2)}, u32[]{:S(2)}) collective-permute-start(bf16[32,1024]{1,0:T(8,128)(2,1)S(1)} %get-tuple-element.126), channel_id=1, source_target_pairs={{0,16},{16,32},{32,48},{48,0},{1,17},{17,33},{33,49},{49,1},{2,18}... | collective-permute-start | bytes 196616 | tf_op jit(solution)/shard_map/ppermute | solution.py:413
  62.9 13.2 %collective-permute-start.18 = (bf16[128,1536]{1,0:T(8,128)(2,1)S(1)}, bf16[128,1536]{1,0:T(8,128)(2,1)S(1)}, u32[]{:S(2)}, u32[]{:S(2)}) collective-permute-start(bf16[128,1536]{1,0:T(8,128)(2,1)S(1)} %bitcast.15), channel_id=1, source_target_pairs={{0,12},{4,8},{8,4},{12,0},{1,13},{5,9},{9,5},{13,1},{2,14},{6,10},... | collective-permute-start | bytes 1179656 | tf_op jit(solution)/shard_map/ppermute | solution.py:564
  63.9 12.1 %collective-permute-start.17 = (bf16[128,1536]{1,0:T(8,128)(2,1)S(1)}, bf16[128,1536]{1,0:T(8,128)(2,1)S(1)}, u32[]{:S(2)}, u32[]{:S(2)}) collective-permute-start(bf16[128,1536]{1,0:T(8,128)(2,1)S(1)} %bitcast.16), channel_id=1, source_target_pairs={{0,4},{4,0},{8,12},{12,8},{1,5},{5,1},{9,13},{13,9},{2,6},{6,2},{1... | collective-permute-start | bytes 1179656 | tf_op jit(solution)/shard_map/ppermute | solution.py:563
  63.9 4.3 %collective-permute-start.21 = (bf16[32,1024]{1,0:T(8,128)(2,1)S(1)}, bf16[32,1024]{1,0:T(8,128)(2,1)S(1)}, u32[]{:S(2)}, u32[]{:S(2)}) collective-permute-start(bf16[32,1024]{1,0:T(8,128)(2,1)S(1)} %get-tuple-element.128), channel_id=1, source_target_pairs={{0,192},{64,0},{128,64},{192,128},{1,193},{65,1},{129,65},{193,129... | collective-permute-start | bytes 196616 | tf_op jit(solution)/shard_map/ppermute | solution.py:413
  64.5 5.8 %collective-permute-start.20 = (bf16[32,1024]{1,0:T(8,128)(2,1)S(1)}, bf16[32,1024]{1,0:T(8,128)(2,1)S(1)}, u32[]{:S(2)}, u32[]{:S(2)}) collective-permute-start(bf16[32,1024]{1,0:T(8,128)(2,1)S(1)} %get-tuple-element.128), channel_id=1, source_target_pairs={{0,128},{64,192},{128,0},{192,64},{1,129},{65,193},{129,1},{193,65... | collective-permute-start | bytes 196616 | tf_op jit(solution)/shard_map/ppermute | solution.py:413
  65.6 5.5 %collective-permute-start.19 = (bf16[32,1024]{1,0:T(8,128)(2,1)S(1)}, bf16[32,1024]{1,0:T(8,128)(2,1)S(1)}, u32[]{:S(2)}, u32[]{:S(2)}) collective-permute-start(bf16[32,1024]{1,0:T(8,128)(2,1)S(1)} %get-tuple-element.128), channel_id=1, source_target_pairs={{0,64},{64,128},{128,192},{192,0},{1,65},{65,129},{129,193},{193,1... | collective-permute-start | bytes 196616 | tf_op jit(solution)/shard_map/ppermute | solution.py:413
  76.1 15.2 %collective-permute-start.25 = (bf16[128,1536]{1,0:T(8,128)(2,1)S(1)}, bf16[128,1536]{1,0:T(8,128)(2,1)S(1)}, u32[]{:S(2)}, u32[]{:S(2)}) collective-permute-start(bf16[128,1536]{1,0:T(8,128)(2,1)S(1)} %collective-permute-done.17.refs_1_), channel_id=1, source_target_pairs={{0,12},{4,8},{8,4},{12,0},{1,13},{5,9},{9,5},{13,1},{2,14},{6,10},... | collective-permute-start | bytes 1179656 | tf_op jit(solution)/shard_map/ppermute | solution.py:566
  85.9 19.4 %all-to-all-start = ((bf16[8,360,128]{2,1,0:T(8,128)(2,1)}), bf16[8,360,128]{2,1,0:T(8,128)(2,1)S(1)}, u32[]{:S(2)}, u32[]{:S(2)}) async-start(bf16[8,360,128]{2,1,0:T(8,128)(2,1)} %get-tuple-element.146), calls=%async_computation | async-start | bytes 1474560 | tf_op jit(solution)/shard_map/all_to_all | solution.py:640
  90.3 3.7 %collective-permute-start.22 = (bf16[128,1536]{1,0:T(8,128)(2,1)S(1)}, bf16[128,1536]{1,0:T(8,128)(2,1)S(1)}, u32[]{:S(2)}, u32[]{:S(2)}) collective-permute-start(bf16[128,1536]{1,0:T(8,128)(2,1)S(1)} %bitcast.17), channel_id=1, source_target_pairs={{0,1},{1,0},{2,3},{3,2},{4,5},{5,4},{6,7},{7,6},{8,9},{9,8},{10,11... | collective-permute-start | bytes 1179656 | tf_op jit(solution)/shard_map/ppermute | solution.py:569
  90.8 3.2 %collective-permute-start.23 = (bf16[128,1536]{1,0:T(8,128)(2,1)S(1)}, bf16[128,1536]{1,0:T(8,128)(2,1)S(1)}, u32[]{:S(2)}, u32[]{:S(2)}) collective-permute-start(bf16[128,1536]{1,0:T(8,128)(2,1)S(1)} %collective-permute-done.17.refs_1_), channel_id=1, source_target_pairs={{0,1},{1,0},{2,3},{3,2},{4,5},{5,4},{6,7},{7,6},{8,9},{9,8},{10,11... | collective-permute-start | bytes 1179656 | tf_op jit(solution)/shard_map/ppermute | solution.py:569
  90.8 3.2 %collective-permute-start.24 = (bf16[128,1536]{1,0:T(8,128)(2,1)S(1)}, bf16[128,1536]{1,0:T(8,128)(2,1)S(1)}, u32[]{:S(2)}, u32[]{:S(2)}) collective-permute-start(bf16[128,1536]{1,0:T(8,128)(2,1)S(1)} %collective-permute-done.18.refs_2_), channel_id=1, source_target_pairs={{0,1},{1,0},{2,3},{3,2},{4,5},{5,4},{6,7},{7,6},{8,9},{9,8},{10,11... | collective-permute-start | bytes 1179656 | tf_op jit(solution)/shard_map/ppermute | solution.py:569
  91.3 3.5 %collective-permute-start.26 = (bf16[128,1536]{1,0:T(8,128)(2,1)S(1)}, bf16[128,1536]{1,0:T(8,128)(2,1)S(1)}, u32[]{:S(2)}, u32[]{:S(2)}) collective-permute-start(bf16[128,1536]{1,0:T(8,128)(2,1)S(1)} %collective-permute-done.25.refs_3_), channel_id=1, source_target_pairs={{0,1},{1,0},{2,3},{3,2},{4,5},{5,4},{6,7},{7,6},{8,9},{9,8},{10,11... | collective-permute-start | bytes 1179656 | tf_op jit(solution)/shard_map/ppermute | solution.py:569
  91.3 2.6 %collective-permute-start.27 = (bf16[40,1024]{1,0:T(8,128)(2,1)S(1)}, bf16[40,1024]{1,0:T(8,128)(2,1)S(1)}, u32[]{:S(2)}, u32[]{:S(2)}) collective-permute-start(bf16[40,1024]{1,0:T(8,128)(2,1)S(1)} %get-tuple-element.138.refs_0_), channel_id=1, source_target_pairs={{0,1},{1,0},{2,3},{3,2},{4,5},{5,4},{6,7},{7,6},{8,9},{9,8},{10,11... | collective-permute-start | bytes 245768 | tf_op jit(solution)/shard_map/ppermute | solution.py:628
  94.7 10.5 %collective-permute-start.30 = (bf16[40,1024]{1,0:T(8,128)(2,1)S(1)}, bf16[40,1024]{1,0:T(8,128)(2,1)S(1)}, u32[]{:S(2)}, u32[]{:S(2)}) collective-permute-start(bf16[40,1024]{1,0:T(8,128)(2,1)S(1)} %add_parts.4.refs_0_), channel_id=1, source_target_pairs={{0,48},{16,0},{32,16},{48,32},{1,49},{17,1},{33,17},{49,33},{2,50}... | collective-permute-start | bytes 245768 | tf_op jit(solution)/shard_map/ppermute | solution.py:413
  97.3 8.0 %collective-permute-start.29 = (bf16[40,1024]{1,0:T(8,128)(2,1)S(1)}, bf16[40,1024]{1,0:T(8,128)(2,1)S(1)}, u32[]{:S(2)}, u32[]{:S(2)}) collective-permute-start(bf16[40,1024]{1,0:T(8,128)(2,1)S(1)} %add_parts.4.refs_0_), channel_id=1, source_target_pairs={{0,32},{16,48},{32,0},{48,16},{1,33},{17,49},{33,1},{49,17},{2,34}... | collective-permute-start | bytes 245768 | tf_op jit(solution)/shard_map/ppermute | solution.py:413
  97.6 7.7 %collective-permute-start.28 = (bf16[40,1024]{1,0:T(8,128)(2,1)S(1)}, bf16[40,1024]{1,0:T(8,128)(2,1)S(1)}, u32[]{:S(2)}, u32[]{:S(2)}) collective-permute-start(bf16[40,1024]{1,0:T(8,128)(2,1)S(1)} %add_parts.4.refs_0_), channel_id=1, source_target_pairs={{0,16},{16,32},{32,48},{48,0},{1,17},{17,33},{33,49},{49,1},{2,18}... | collective-permute-start | bytes 245768 | tf_op jit(solution)/shard_map/ppermute | solution.py:413
  99.3 52.2 %copy-start.8 = (f32[15,16]{1,0:T(8,128)S(1)}, f32[15,16]{1,0:T(8,128)}, u32[]{:S(2)}) copy-start(f32[15,16]{1,0:T(8,128)} %get-tuple-element.166.amp) | copy-start | bytes 2884
  109.1 23.3 %collective-permute-start.31 = (bf16[360,384]{1,0:T(8,128)(2,1)S(1)}, bf16[360,384]{1,0:T(8,128)(2,1)S(1)}, u32[]{:S(2)}, u32[]{:S(2)}) collective-permute-start(bf16[360,384]{1,0:T(8,128)(2,1)S(1)} %get-tuple-element.157), channel_id=1, source_target_pairs={{0,64},{64,128},{128,192},{192,0},{1,65},{65,129},{129,193},{193,1... | collective-permute-start | bytes 829448 | tf_op jit(solution)/shard_map/ppermute | solution.py:413
  109.2 23.2 %collective-permute-start.32 = (bf16[360,384]{1,0:T(8,128)(2,1)S(1)}, bf16[360,384]{1,0:T(8,128)(2,1)S(1)}, u32[]{:S(2)}, u32[]{:S(2)}) collective-permute-start(bf16[360,384]{1,0:T(8,128)(2,1)S(1)} %get-tuple-element.158), channel_id=1, source_target_pairs={{0,128},{64,192},{128,0},{192,64},{1,129},{65,193},{129,1},{193,65... | collective-permute-start | bytes 829448 | tf_op jit(solution)/shard_map/ppermute | solution.py:413
  111.0 21.4 %collective-permute-start.33 = (bf16[360,384]{1,0:T(8,128)(2,1)S(1)}, bf16[360,384]{1,0:T(8,128)(2,1)S(1)}, u32[]{:S(2)}, u32[]{:S(2)}) collective-permute-start(bf16[360,384]{1,0:T(8,128)(2,1)S(1)} %get-tuple-element.159), channel_id=1, source_target_pairs={{0,192},{64,0},{128,64},{192,128},{1,193},{65,1},{129,65},{193,129... | collective-permute-start | bytes 829448 | tf_op jit(solution)/shard_map/ppermute | solution.py:413
  112.6 5.2 %collective-permute-start.36 = (bf16[40,1024]{1,0:T(8,128)(2,1)S(1)}, bf16[40,1024]{1,0:T(8,128)(2,1)S(1)}, u32[]{:S(2)}, u32[]{:S(2)}) collective-permute-start(bf16[40,1024]{1,0:T(8,128)(2,1)S(1)} %add_parts.5.refs_0_), channel_id=1, source_target_pairs={{0,12},{4,0},{8,4},{12,8},{1,13},{5,1},{9,5},{13,9},{2,14},{6,2},{... | collective-permute-start | bytes 245768 | tf_op jit(solution)/shard_map/ppermute | solution.py:413
  115.7 6.5 %collective-permute-start.35 = (bf16[40,1024]{1,0:T(8,128)(2,1)S(1)}, bf16[40,1024]{1,0:T(8,128)(2,1)S(1)}, u32[]{:S(2)}, u32[]{:S(2)}) collective-permute-start(bf16[40,1024]{1,0:T(8,128)(2,1)S(1)} %add_parts.5.refs_0_), channel_id=1, source_target_pairs={{0,8},{4,12},{8,0},{12,4},{1,9},{5,13},{9,1},{13,5},{2,10},{6,14},... | collective-permute-start | bytes 245768 | tf_op jit(solution)/shard_map/ppermute | solution.py:413
  117.8 6.1 %collective-permute-start.34 = (bf16[40,1024]{1,0:T(8,128)(2,1)S(1)}, bf16[40,1024]{1,0:T(8,128)(2,1)S(1)}, u32[]{:S(2)}, u32[]{:S(2)}) collective-permute-start(bf16[40,1024]{1,0:T(8,128)(2,1)S(1)} %add_parts.5.refs_0_), channel_id=1, source_target_pairs={{0,4},{4,8},{8,12},{12,0},{1,5},{5,9},{9,13},{13,1},{2,6},{6,10},{... | collective-permute-start | bytes 245768 | tf_op jit(solution)/shard_map/ppermute | solution.py:413
  123.9 8.5 %collective-permute-start.37 = (bf16[40,1024]{1,0:T(8,128)(2,1)S(1)}, bf16[40,1024]{1,0:T(8,128)(2,1)S(1)}, u32[]{:S(2)}, u32[]{:S(2)}) collective-permute-start(bf16[40,1024]{1,0:T(8,128)(2,1)S(1)} %add_parts.6.refs_0_), channel_id=1, source_target_pairs={{0,2},{2,0},{1,3},{3,1},{4,6},{6,4},{5,7},{7,5},{8,10},{10,8},{9,1... | collective-permute-start | bytes 245768 | tf_op jit(solution)/shard_map/ppermute | solution.py:628
  133.5 22.2 %all-to-all-start.1 = ((bf16[32,24,180]{2,1,0:T(8,128)(2,1)}), bf16[32,24,180]{2,1,0:T(8,128)(2,1)S(1)}, u32[]{:S(2)}, u32[]{:S(2)}) async-start(bf16[32,24,180]{2,1,0:T(8,128)(2,1)} %split_rows.1), calls=%async_computation.1 | async-start | bytes 786432 | tf_op jit(solution)/shard_map/all_to_all | solution.py:683
  143.1 4.5 %collective-permute-start.40 = (bf16[40,1024]{1,0:T(8,128)(2,1)S(1)}, bf16[40,1024]{1,0:T(8,128)(2,1)S(1)}, u32[]{:S(2)}, u32[]{:S(2)}) collective-permute-start(bf16[40,1024]{1,0:T(8,128)(2,1)S(1)} %add_parts.7.refs_0_), channel_id=1, source_target_pairs={{0,192},{64,0},{128,64},{192,128},{1,193},{65,1},{129,65},{193,129... | collective-permute-start | bytes 245768 | tf_op jit(solution)/shard_map/ppermute | solution.py:413
  143.7 5.9 %collective-permute-start.39 = (bf16[40,1024]{1,0:T(8,128)(2,1)S(1)}, bf16[40,1024]{1,0:T(8,128)(2,1)S(1)}, u32[]{:S(2)}, u32[]{:S(2)}) collective-permute-start(bf16[40,1024]{1,0:T(8,128)(2,1)S(1)} %add_parts.7.refs_0_), channel_id=1, source_target_pairs={{0,128},{64,192},{128,0},{192,64},{1,129},{65,193},{129,1},{193,65... | collective-permute-start | bytes 245768 | tf_op jit(solution)/shard_map/ppermute | solution.py:413
  145.8 5.7 %collective-permute-start.38 = (bf16[40,1024]{1,0:T(8,128)(2,1)S(1)}, bf16[40,1024]{1,0:T(8,128)(2,1)S(1)}, u32[]{:S(2)}, u32[]{:S(2)}) collective-permute-start(bf16[40,1024]{1,0:T(8,128)(2,1)S(1)} %add_parts.7.refs_0_), channel_id=1, source_target_pairs={{0,64},{64,128},{128,192},{192,0},{1,65},{65,129},{129,193},{193,1... | collective-permute-start | bytes 245768 | tf_op jit(solution)/shard_map/ppermute | solution.py:413
  (8 other events, 65.6 us)

commit v3 on v2

--- a/solution.py
+++ b/solution.py
@@ -669,8 +669,9 @@
     )(xi, yi, ci, arrived, *blocks_of, *theirs)
     got = [terms[0]] + [ring(terms[d], "x", d) for d in (1, 2, 3)]
     sums, _ = lax.optimization_barrier((sums, terms[0]))
-    sums = summed(swap(summed(spread(sums, "y")), "zh"))
+    sums = summed(spread(sums, "y"))
     *got, sums = lax.optimization_barrier((*got, sums))
+    parts = swap(sums, "zh")
     blocks = pl.pallas_call(
         split_rows,
         in_specs=[vm] * 4,
@@ -681,8 +682,8 @@
         name="split_rows",
     )(*got)
     last = lax.all_to_all(blocks, ("zl", "y", "zh"), 0, 0, tiled=True)
-    sums, _ = lax.optimization_barrier((sums, blocks))
-    parts = spread(sums, "x")
+    *parts, _ = lax.optimization_barrier((*parts, blocks))
+    parts = spread(summed(parts), "x")
     grad_taps, grad_residues = pl.pallas_call(
         make_close_sums(scale),
         in_specs=[smem] * 3 + [free] * 5,

time: 157 us -> 164 us (1.045)
  waiting for transfers between devices: 39.9 us -> 46.2 us
    ppermute x2, waiting for transfers between devices: 6.02 us -> 13.2 us  [swap(): return [a, lax.ppermute(a, ax, [(0, 1), (1, 0)])]]
    all_to_all x1, waiting for transfers between devices: 3.48 us -> 0.01 us  [local(): last = lax.all_to_all(blocks, ('zl', 'y', 'zh'), 0, 0, tiled=True)]
    ppermute x30, waiting for transfers between devices: 25.4 us -> 28 us  [ring(): return lax.ppermute(a, ax, [(i, (i + d) % 4) for i in range(4)])]
  transfers between devices with their start and end apart: 43 -> 43, of which waited for: 22 -> 23; matrix products, arithmetic and copies ran while one was open for 0% -> 0% of each run, Pallas kernels for 18% -> 17%
where the time goes in v3:
time: 164 us; the launch traced here: 163 us
  starting transfers between devices  75.4 us (46%)
  waiting for transfers between devices  46.2 us (28%)
  Pallas kernels  36.9 us (22%)
  local copies, waits for them, and re-layouts  3.77 us (2%)
    ppermute x30, starting transfers between devices, ring(): return lax.ppermute(a, ax, [(i, (i + d) % 4) for i in range(4)])  47.4 us
    ppermute x30, waiting for transfers between devices, ring(): return lax.ppermute(a, ax, [(i, (i + d) % 4) for i in range(4)])  28 us
    ppermute x2, waiting for transfers between devices, swap(): return [a, lax.ppermute(a, ax, [(0, 1), (1, 0)])]  13.2 us
    all_to_all x1, starting transfers between devices, local(): last = lax.all_to_all(blocks, ('zl', 'y', 'zh'), 0, 0, tiled=True)  10 us
    pallas_call x1, Pallas kernels, local(): pl.pallas_call(finish, grid=(PADC // 128,), in_specs=[smem, smem, *[tiles...  9.63 us
    pallas_call x2, Pallas kernels, project(): pl.pallas_call(make_project(part), in_specs=[vm] * (2 + part) + [anywhere...  9.62 us
    pallas_call x1, Pallas kernels, local(): pl.pallas_call(token_grads, grid=(3,), in_specs=[pl.BlockSpec((1, own, PA...  6.01 us
    ppermute x2, starting transfers between devices, swap(): return [a, lax.ppermute(a, ax, [(0, 1), (1, 0)])]  5.06 us
  transfers between devices with their start and end apart: 43, of which 23 were waited for; matrix products, arithmetic and copies ran while one was open for 0% of the time, Pallas kernels for 17%

profile of v3, /device:TPU:32, one launch (start us, length us, event | category | flops | bytes accessed | tf_op | source)
XLA Modules:
  0.0 163.3 jit_solution(12149079310595772238)
XLA Ops:
  0.7 2.2 %prepare.1 = (bf16[16,2560]{1,0:T(8,128)(2,1)}, bf16[16,1536]{1,0:T(8,128)(2,1)}, f32[32,15]{1,0:T(8,128)}, f32[3,8,1024]{2,1,0:T(8,128)}, f32[15,16]{1,0:T(8,128)}, /*index=5*/f32[128,1024]{1,0:T(8,128)}) custom-call(bf16[128,1536]{1,0:T(8,128)(2,1)} %bitcast.12, bf16[960,128]{1,0:T(8,128)(2,1)} %bitcast.23, f32[15,16]{1,0:T(8,128)} %rates, ...), custom_call_target="tpu_custom_call" | custom-call | tf_op jit(solution)/shard_map/prepare/pallas_call | solution.py:440
  2.9 4.5 %collective-permute-start.1 = (bf16[16,2560]{1,0:T(8,128)(2,1)}, bf16[16,2560]{1,0:T(8,128)(2,1)S(1)}, u32[]{:S(2)}, u32[]{:S(2)}) collective-permute-start(bf16[16,2560]{1,0:T(8,128)(2,1)} %get-tuple-element.95), channel_id=1, source_target_pairs={{4,0},{8,4},{12,8},{16,12},{20,16},{24,20},{28,24},{32,28},{36,32}... | collective-permute-start | bytes 245768 | tf_op jit(solution)/shard_map/ppermute | solution.py:465
  7.4 1.9 %collective-permute-start = (bf16[16,1536]{1,0:T(8,128)(2,1)}, bf16[16,1536]{1,0:T(8,128)(2,1)S(1)}, u32[]{:S(2)}, u32[]{:S(2)}) collective-permute-start(bf16[16,1536]{1,0:T(8,128)(2,1)} %get-tuple-element.94), channel_id=1, source_target_pairs={{0,4},{4,8},{8,12},{12,16},{16,20},{20,24},{24,28},{28,32},{32,36}... | collective-permute-start | bytes 147464 | tf_op jit(solution)/shard_map/ppermute | solution.py:464
  9.3 4.7 %collective-permute-start.4 = (f32[32,15]{1,0:T(8,128)}, f32[32,15]{1,0:T(8,128)S(1)}, u32[]{:S(2)}, u32[]{:S(2)}) collective-permute-start(f32[32,15]{1,0:T(8,128)} %get-tuple-element.100.r0), channel_id=1, source_target_pairs={{0,12},{4,0},{8,4},{12,8},{1,13},{5,1},{9,5},{13,9},{2,14},{6,2},{... | collective-permute-start | bytes 5768 | tf_op jit(solution)/shard_map/ppermute | solution.py:413
  15.7 1.0 copy-done
  16.7 4.7 %project.2.refs_2_ = f32[160,2880]{1,0:T(8,128)} custom-call(bf16[16,1536]{1,0:T(8,128)(2,1)S(1)} %collective-permute-done.refs_0_, bf16[16,2560]{1,0:T(8,128)(2,1)S(1)} %collective-permute-done.1.refs_1_.nexts, bf16[128,1536]{1,0:T(8,128)(2,1)S(1)} %bitcast.13, bf16[2880,1536]{1,0:T(8,128)(2,1)} %bitcast.19), custom_call_target="tpu_custom_call" | custom-call | flops 800000000 | bytes 6000000 | tf_op jit(solution)/shard_map/project/pallas_call | solution.py:472
  21.6 5.3 %collective-permute-start.6 = (f32[32,60]{1,0:T(8,128)S(1)}, f32[32,60]{1,0:T(8,128)S(1)}, u32[]{:S(2)}, u32[]{:S(2)}) collective-permute-start(f32[32,60]{1,0:T(8,128)S(1)} %join_params.2.r0), channel_id=1, source_target_pairs={{0,32},{16,48},{32,0},{48,16},{1,33},{17,49},{33,1},{49,17},{2,34}... | collective-permute-start | bytes 23048 | tf_op jit(solution)/shard_map/ppermute | solution.py:413
  26.9 2.8 %collective-permute-start.5 = (f32[32,60]{1,0:T(8,128)S(1)}, f32[32,60]{1,0:T(8,128)S(1)}, u32[]{:S(2)}, u32[]{:S(2)}) collective-permute-start(f32[32,60]{1,0:T(8,128)S(1)} %join_params.2.r0), channel_id=1, source_target_pairs={{0,16},{16,32},{32,48},{48,0},{1,17},{17,33},{33,49},{49,1},{2,18}... | collective-permute-start | bytes 23048 | tf_op jit(solution)/shard_map/ppermute | solution.py:413
  29.8 4.9 %project.3 = (f32[160,1024]{1,0:T(8,128)S(1)}, f32[160,1024]{1,0:T(8,128)S(1)}, f32[160,1024]{1,0:T(8,128)S(1)}) custom-call(bf16[16,1536]{1,0:T(8,128)(2,1)S(1)} %collective-permute-done.refs_0_, bf16[16,2560]{1,0:T(8,128)(2,1)S(1)} %collective-permute-done.1.refs_1_.nexts, f32[160,2880]{1,0:T(8,128)} %project.2.refs_2_, bf16[128,1536]{1,0:T(8,128)(2,1)S(1)} %bitcast.14, ...), custom_call_target="tpu_custom_call" | custom-call | flops 800000000 | bytes 6000000 | tf_op jit(solution)/shard_map/project/pallas_call | solution.py:472
  34.8 3.9 %collective-permute-start.10 = (f32[32,240]{1,0:T(8,128)S(1)}, f32[32,240]{1,0:T(8,128)S(1)}, u32[]{:S(2)}, u32[]{:S(2)}) collective-permute-start(f32[32,240]{1,0:T(8,128)S(1)} %join_params.3.r0), channel_id=1, source_target_pairs={{0,192},{64,0},{128,64},{192,128},{1,193},{65,1},{129,65},{193,129... | collective-permute-start | bytes 92168 | tf_op jit(solution)/shard_map/ppermute | solution.py:413
  40.1 1.4 mix_taps.1
  41.6 2.6 %collective-permute-done.9.r2 = f32[32,240]{1,0:T(8,128)S(1)} collective-permute-done((f32[32,240]{1,0:T(8,128)S(1)}, f32[32,240]{1,0:T(8,128)S(1)}, u32[]{:S(2)}, u32[]{:S(2)}) %collective-permute-start.9) | collective-permute-done | bytes 30752 | tf_op jit(solution)/shard_map/ppermute | solution.py:413
  44.5 2.2 %end_states.1 = (f32[136,1024]{1,0:T(8,128)S(1)}, f32[16,1024]{1,0:T(8,128)S(1)}, f32[16,1024]{1,0:T(8,128)S(1)}, f32[2,16,8,1024]{3,2,1,0:T(8,128)S(1)}, f32[32...) custom-call(s32[1]{0:T(128)} %bitcast.6.me.index.xi, f32[32,240]{1,0:T(8,128)S(1)} %join_params.3.r0, ...), custom_call_target="tpu_custom_call" | custom-call | flops 20000000 | bytes 3000000 | tf_op jit(solution)/shard_map/end_states/pallas_call | solution.py:522
  46.7 1.5 collective-permute-start.13
  48.2 2.3 %collective-permute-start.12 = (bf16[32,1024]{1,0:T(8,128)(2,1)S(1)}, bf16[32,1024]{1,0:T(8,128)(2,1)S(1)}, u32[]{:S(2)}, u32[]{:S(2)}) collective-permute-start(bf16[32,1024]{1,0:T(8,128)(2,1)S(1)} %get-tuple-element.123), channel_id=1, source_target_pairs={{0,8},{4,12},{8,0},{12,4},{1,9},{5,13},{9,1},{13,5},{2,10},{6,14},... | collective-permute-start | bytes 196616 | tf_op jit(solution)/shard_map/ppermute | solution.py:413
  51.0 2.9 %collective-permute-done.12.r2 = bf16[32,1024]{1,0:T(8,128)(2,1)S(1)} collective-permute-done((bf16[32,1024]{1,0:T(8,128)(2,1)S(1)}, bf16[32,1024]{1,0:T(8,128)(2,1)S(1)}, u32[]{:S(2)}, u32[]{:S(2)}) %collective-permute-start.12) | collective-permute-done | bytes 65568 | tf_op jit(solution)/shard_map/ppermute | solution.py:413
  53.9 2.0 %collective-permute-done.11.r1 = bf16[32,1024]{1,0:T(8,128)(2,1)S(1)} collective-permute-done((bf16[32,1024]{1,0:T(8,128)(2,1)S(1)}, bf16[32,1024]{1,0:T(8,128)(2,1)S(1)}, u32[]{:S(2)}, u32[]{:S(2)}) %collective-permute-start.11) | collective-permute-done | bytes 65568 | tf_op jit(solution)/shard_map/ppermute | solution.py:413
  56.3 1.5 collective-permute-start.15
  57.7 2.4 %collective-permute-start.14 = (bf16[32,1024]{1,0:T(8,128)(2,1)S(1)}, bf16[32,1024]{1,0:T(8,128)(2,1)S(1)}, u32[]{:S(2)}, u32[]{:S(2)}) collective-permute-start(bf16[32,1024]{1,0:T(8,128)(2,1)S(1)} %get-tuple-element.127), channel_id=1, source_target_pairs={{0,16},{16,32},{32,48},{48,0},{1,17},{17,33},{33,49},{49,1},{2,18}... | collective-permute-start | bytes 196616 | tf_op jit(solution)/shard_map/ppermute | solution.py:413
  60.5 1.0 collective-permute-done.15.r2
  61.5 1.2 collective-permute-done.14.r1
  62.9 1.1 collective-permute-start.18
  64.5 1.1 collective-permute-start.20
  65.6 1.4 collective-permute-start.19
  67.0 1.2 collective-permute-done.21.r3
  68.2 2.1 %collective-permute-done.20.r2 = bf16[32,1024]{1,0:T(8,128)(2,1)S(1)} collective-permute-done((bf16[32,1024]{1,0:T(8,128)(2,1)S(1)}, bf16[32,1024]{1,0:T(8,128)(2,1)S(1)}, u32[]{:S(2)}, u32[]{:S(2)}) %collective-permute-start.20) | collective-permute-done | bytes 65568 | tf_op jit(solution)/shard_map/ppermute | solution.py:413
  71.9 4.2 %collective-permute-done.18.refs_2_ = bf16[128,1536]{1,0:T(8,128)(2,1)S(1)} collective-permute-done((bf16[128,1536]{1,0:T(8,128)(2,1)S(1)}, bf16[128,1536]{1,0:T(8,128)(2,1)S(1)}, u32[]{:S(2)}, u32[]{:S(2)}) %collective-permute-start.18) | collective-permute-done | bytes 393248 | tf_op jit(solution)/shard_map/ppermute | solution.py:564
  76.3 9.6 %finish.1 = (bf16[960,128]{1,0:T(8,128)(2,1)}, bf16[3,128,1024]{2,1,0:T(8,128)(2,1)}, bf16[8,360,128]{2,1,0:T(8,128)(2,1)}, bf16[40,1024]{1,0:T(8,128)(2,1)S(1)}) custom-call(s32[1]{0:T(128)} %bitcast.2.me.index.zi, s32[1]{0:T(128)} %bitcast.3.me.index.yi, f32[160,1024]{1,0:T(8,128)S(1)} %get-tuple-element.98.zq, f32[160,1024]{1,0:T(8,128)} %copy-done.3, ...), custom_call_target="tpu_custom_call" | custom-call | flops 200000000 | bytes 10000000 | tf_op jit(solution)/shard_map/finish/pallas_call | solution.py:575
  85.9 4.3 %all-to-all-start = ((bf16[8,360,128]{2,1,0:T(8,128)(2,1)}), bf16[8,360,128]{2,1,0:T(8,128)(2,1)S(1)}, u32[]{:S(2)}, u32[]{:S(2)}) async-start(bf16[8,360,128]{2,1,0:T(8,128)(2,1)} %get-tuple-element.147), calls=%async_computation | async-start | bytes 1474560 | tf_op jit(solution)/shard_map/all_to_all | solution.py:640
  91.8 2.1 %collective-permute-done.27.refs_1_ = bf16[40,1024]{1,0:T(8,128)(2,1)S(1)} collective-permute-done((bf16[40,1024]{1,0:T(8,128)(2,1)S(1)}, bf16[40,1024]{1,0:T(8,128)(2,1)S(1)}, u32[]{:S(2)}, u32[]{:S(2)}) %collective-permute-start.27) | collective-permute-done | bytes 81952 | tf_op jit(solution)/shard_map/ppermute | solution.py:628
  94.7 2.6 %collective-permute-start.30 = (bf16[40,1024]{1,0:T(8,128)(2,1)S(1)}, bf16[40,1024]{1,0:T(8,128)(2,1)S(1)}, u32[]{:S(2)}, u32[]{:S(2)}) collective-permute-start(bf16[40,1024]{1,0:T(8,128)(2,1)S(1)} %add_parts.4.refs_0_), channel_id=1, source_target_pairs={{0,48},{16,0},{32,16},{48,32},{1,49},{17,1},{33,17},{49,33},{2,50}... | collective-permute-start | bytes 245768 | tf_op jit(solution)/shard_map/ppermute | solution.py:413
  97.6 1.7 %collective-permute-start.28 = (bf16[40,1024]{1,0:T(8,128)(2,1)S(1)}, bf16[40,1024]{1,0:T(8,128)(2,1)S(1)}, u32[]{:S(2)}, u32[]{:S(2)}) collective-permute-start(bf16[40,1024]{1,0:T(8,128)(2,1)S(1)} %add_parts.4.refs_0_), channel_id=1, source_target_pairs={{0,16},{16,32},{32,48},{48,0},{1,17},{17,33},{33,49},{49,1},{2,18}... | collective-permute-start | bytes 245768 | tf_op jit(solution)/shard_map/ppermute | solution.py:413
  99.3 6.0 %token_grads.1 = bf16[128,1536]{1,0:T(8,128)(2,1)} custom-call(bf16[3,128,1024]{2,1,0:T(8,128)(2,1)} %get-tuple-element.144.dz, bf16[2880,1536]{1,0:T(8,128)(2,1)} %bitcast.21), custom_call_target="tpu_custom_call" | custom-call | flops 1200000000 | bytes 11000000 | tf_op jit(solution)/shard_map/token_grads/pallas_call | solution.py:644
  107.4 1.7 %weight_term.1 = (bf16[360,384]{1,0:T(8,128)(2,1)S(1)}, bf16[360,384]{1,0:T(8,128)(2,1)S(1)}, bf16[360,384]{1,0:T(8,128)(2,1)S(1)}, bf16[360,384]{1,0:T(8,128)(2,1)S(1)}) custom-call(s32[1]{0:T(128)} %bitcast.6.me.index.xi, s32[1]{0:T(128)} %bitcast.3.me.index.yi, s32[1]{0:T(128)} %bitcast.10.ci, bf16[8,360,128]{2,1,0:T(8,128)(2,1)S(1)} %all-to-all-done.arrived, ...), custom_call_target="tpu_custom_call" | custom-call | flops 1200000000 | bytes 6000000 | tf_op jit(solution)/shard_map/weight_term/pallas_call | solution.py:661
  109.2 1.8 %collective-permute-start.32 = (bf16[360,384]{1,0:T(8,128)(2,1)S(1)}, bf16[360,384]{1,0:T(8,128)(2,1)S(1)}, u32[]{:S(2)}, u32[]{:S(2)}) collective-permute-start(bf16[360,384]{1,0:T(8,128)(2,1)S(1)} %get-tuple-element.159), channel_id=1, source_target_pairs={{0,128},{64,192},{128,0},{192,64},{1,129},{65,193},{129,1},{193,65... | collective-permute-start | bytes 829448 | tf_op jit(solution)/shard_map/ppermute | solution.py:413
  111.0 1.6 collective-permute-start.33
  112.6 3.1 %collective-permute-start.36 = (bf16[40,1024]{1,0:T(8,128)(2,1)S(1)}, bf16[40,1024]{1,0:T(8,128)(2,1)S(1)}, u32[]{:S(2)}, u32[]{:S(2)}) collective-permute-start(bf16[40,1024]{1,0:T(8,128)(2,1)S(1)} %add_parts.5.refs_0_), channel_id=1, source_target_pairs={{0,12},{4,0},{8,4},{12,8},{1,13},{5,1},{9,5},{13,9},{2,14},{6,2},{... | collective-permute-start | bytes 245768 | tf_op jit(solution)/shard_map/ppermute | solution.py:413
  116.5 1.3 collective-permute-done.36.refs_3_
  117.8 1.4 collective-permute-start.34
  119.2 3.0 %collective-permute-done.35.refs_2_ = bf16[40,1024]{1,0:T(8,128)(2,1)S(1)} collective-permute-done((bf16[40,1024]{1,0:T(8,128)(2,1)S(1)}, bf16[40,1024]{1,0:T(8,128)(2,1)S(1)}, u32[]{:S(2)}, u32[]{:S(2)}) %collective-permute-start.35) | collective-permute-done | bytes 81952 | tf_op jit(solution)/shard_map/ppermute | solution.py:413
  122.2 1.7 %collective-permute-done.34.refs_1_ = bf16[40,1024]{1,0:T(8,128)(2,1)S(1)} collective-permute-done((bf16[40,1024]{1,0:T(8,128)(2,1)S(1)}, bf16[40,1024]{1,0:T(8,128)(2,1)S(1)}, u32[]{:S(2)}, u32[]{:S(2)}) %collective-permute-start.34) | collective-permute-done | bytes 81952 | tf_op jit(solution)/shard_map/ppermute | solution.py:413
  125.0 1.1 split_rows.1
  126.1 10.0 %all-to-all-start.1 = ((bf16[32,24,180]{2,1,0:T(8,128)(2,1)}), bf16[32,24,180]{2,1,0:T(8,128)(2,1)S(1)}, u32[]{:S(2)}, u32[]{:S(2)}) async-start(bf16[32,24,180]{2,1,0:T(8,128)(2,1)} %split_rows.1), calls=%async_computation.1 | async-start | bytes 786432 | tf_op jit(solution)/shard_map/all_to_all | solution.py:684
  136.1 4.6 %collective-permute-start.37 = (bf16[40,1024]{1,0:T(8,128)(2,1)S(1)}, bf16[40,1024]{1,0:T(8,128)(2,1)S(1)}, u32[]{:S(2)}, u32[]{:S(2)}) collective-permute-start(bf16[40,1024]{1,0:T(8,128)(2,1)S(1)} %add_parts.6.refs_0_), channel_id=1, source_target_pairs={{0,2},{2,0},{1,3},{3,1},{4,6},{6,4},{5,7},{7,5},{8,10},{10,8},{9,1... | collective-permute-start | bytes 245768 | tf_op jit(solution)/shard_map/ppermute | solution.py:628
  140.7 11.1 %collective-permute-done.37.refs_1_ = bf16[40,1024]{1,0:T(8,128)(2,1)S(1)} collective-permute-done((bf16[40,1024]{1,0:T(8,128)(2,1)S(1)}, bf16[40,1024]{1,0:T(8,128)(2,1)S(1)}, u32[]{:S(2)}, u32[]{:S(2)}) %collective-permute-start.37) | collective-permute-done | bytes 81952 | tf_op jit(solution)/shard_map/ppermute | solution.py:628
  151.8 3.2 %collective-permute-start.40 = (bf16[40,1024]{1,0:T(8,128)(2,1)S(1)}, bf16[40,1024]{1,0:T(8,128)(2,1)S(1)}, u32[]{:S(2)}, u32[]{:S(2)}) collective-permute-start(bf16[40,1024]{1,0:T(8,128)(2,1)S(1)} %add_parts.7.refs_0_), channel_id=1, source_target_pairs={{0,192},{64,0},{128,64},{192,128},{1,193},{65,1},{129,65},{193,129... | collective-permute-start | bytes 245768 | tf_op jit(solution)/shard_map/ppermute | solution.py:413
  156.0 2.0 %collective-permute-done.40.refs_3_ = bf16[40,1024]{1,0:T(8,128)(2,1)S(1)} collective-permute-done((bf16[40,1024]{1,0:T(8,128)(2,1)S(1)}, bf16[40,1024]{1,0:T(8,128)(2,1)S(1)}, u32[]{:S(2)}, u32[]{:S(2)}) %collective-permute-start.40) | collective-permute-done | bytes 81952 | tf_op jit(solution)/shard_map/ppermute | solution.py:413
  158.0 3.1 %collective-permute-done.39.refs_2_ = bf16[40,1024]{1,0:T(8,128)(2,1)S(1)} collective-permute-done((bf16[40,1024]{1,0:T(8,128)(2,1)S(1)}, bf16[40,1024]{1,0:T(8,128)(2,1)S(1)}, u32[]{:S(2)}, u32[]{:S(2)}) %collective-permute-start.39) | collective-permute-done | bytes 81952 | tf_op jit(solution)/shard_map/ppermute | solution.py:413
  (84 shorter events, 17.6 us)
Async XLA Ops:
  0.6 29.1 %copy-start.1 = (bf16[1,128,1536]{2,1,0:T(8,128)(2,1)S(1)}, bf16[1,128,1536]{2,1,0:T(8,128)(2,1)}, u32[]{:S(2)}) copy-start(bf16[1,128,1536]{2,1,0:T(8,128)(2,1)} %param.6) | copy-start | bytes 1179652
  2.9 12.8 %collective-permute-start.1 = (bf16[16,2560]{1,0:T(8,128)(2,1)}, bf16[16,2560]{1,0:T(8,128)(2,1)S(1)}, u32[]{:S(2)}, u32[]{:S(2)}) collective-permute-start(bf16[16,2560]{1,0:T(8,128)(2,1)} %get-tuple-element.95), channel_id=1, source_target_pairs={{4,0},{8,4},{12,8},{16,12},{20,16},{24,20},{28,24},{32,28},{36,32}... | collective-permute-start | bytes 245768 | tf_op jit(solution)/shard_map/ppermute | solution.py:465
  7.4 8.3 %collective-permute-start = (bf16[16,1536]{1,0:T(8,128)(2,1)}, bf16[16,1536]{1,0:T(8,128)(2,1)S(1)}, u32[]{:S(2)}, u32[]{:S(2)}) collective-permute-start(bf16[16,1536]{1,0:T(8,128)(2,1)} %get-tuple-element.94), channel_id=1, source_target_pairs={{0,4},{4,8},{8,12},{12,16},{16,20},{20,24},{24,28},{28,32},{32,36}... | collective-permute-start | bytes 147464 | tf_op jit(solution)/shard_map/ppermute | solution.py:464
  9.3 12.1 %collective-permute-start.4 = (f32[32,15]{1,0:T(8,128)}, f32[32,15]{1,0:T(8,128)S(1)}, u32[]{:S(2)}, u32[]{:S(2)}) collective-permute-start(f32[32,15]{1,0:T(8,128)} %get-tuple-element.100.r0), channel_id=1, source_target_pairs={{0,12},{4,0},{8,4},{12,8},{1,13},{5,1},{9,5},{13,9},{2,14},{6,2},{... | collective-permute-start | bytes 5768 | tf_op jit(solution)/shard_map/ppermute | solution.py:413
  13.9 7.5 %collective-permute-start.3 = (f32[32,15]{1,0:T(8,128)}, f32[32,15]{1,0:T(8,128)S(1)}, u32[]{:S(2)}, u32[]{:S(2)}) collective-permute-start(f32[32,15]{1,0:T(8,128)} %get-tuple-element.100.r0), channel_id=1, source_target_pairs={{0,8},{4,12},{8,0},{12,4},{1,9},{5,13},{9,1},{13,5},{2,10},{6,14},... | collective-permute-start | bytes 5768 | tf_op jit(solution)/shard_map/ppermute | solution.py:413
  13.9 7.5 %collective-permute-start.2 = (f32[32,15]{1,0:T(8,128)}, f32[32,15]{1,0:T(8,128)S(1)}, u32[]{:S(2)}, u32[]{:S(2)}) collective-permute-start(f32[32,15]{1,0:T(8,128)} %get-tuple-element.100.r0), channel_id=1, source_target_pairs={{0,4},{4,8},{8,12},{12,0},{1,5},{5,9},{9,13},{13,1},{2,6},{6,10},{... | collective-permute-start | bytes 5768 | tf_op jit(solution)/shard_map/ppermute | solution.py:413
  21.5 13.2 %collective-permute-start.7 = (f32[32,60]{1,0:T(8,128)S(1)}, f32[32,60]{1,0:T(8,128)S(1)}, u32[]{:S(2)}, u32[]{:S(2)}) collective-permute-start(f32[32,60]{1,0:T(8,128)S(1)} %join_params.2.r0), channel_id=1, source_target_pairs={{0,48},{16,0},{32,16},{48,32},{1,49},{17,1},{33,17},{49,33},{2,50}... | collective-permute-start | bytes 23048 | tf_op jit(solution)/shard_map/ppermute | solution.py:413
  21.6 13.1 %collective-permute-start.6 = (f32[32,60]{1,0:T(8,128)S(1)}, f32[32,60]{1,0:T(8,128)S(1)}, u32[]{:S(2)}, u32[]{:S(2)}) collective-permute-start(f32[32,60]{1,0:T(8,128)S(1)} %join_params.2.r0), channel_id=1, source_target_pairs={{0,32},{16,48},{32,0},{48,16},{1,33},{17,49},{33,1},{49,17},{2,34}... | collective-permute-start | bytes 23048 | tf_op jit(solution)/shard_map/ppermute | solution.py:413
  26.9 7.8 %collective-permute-start.5 = (f32[32,60]{1,0:T(8,128)S(1)}, f32[32,60]{1,0:T(8,128)S(1)}, u32[]{:S(2)}, u32[]{:S(2)}) collective-permute-start(f32[32,60]{1,0:T(8,128)S(1)} %join_params.2.r0), channel_id=1, source_target_pairs={{0,16},{16,32},{32,48},{48,0},{1,17},{17,33},{33,49},{49,1},{2,18}... | collective-permute-start | bytes 23048 | tf_op jit(solution)/shard_map/ppermute | solution.py:413
  34.7 41.6 %copy-start.3 = (f32[160,1024]{1,0:T(8,128)}, f32[160,1024]{1,0:T(8,128)S(1)}, u32[]{:S(2)}) copy-start(f32[160,1024]{1,0:T(8,128)S(1)} %get-tuple-element.99.zk) | copy-start | bytes 1966084
  34.7 41.6 %copy-start.4 = (f32[160,1024]{1,0:T(8,128)}, f32[160,1024]{1,0:T(8,128)S(1)}, u32[]{:S(2)}) copy-start(f32[160,1024]{1,0:T(8,128)S(1)} %get-tuple-element.105.zv) | copy-start | bytes 1966084
  34.8 6.7 %collective-permute-start.10 = (f32[32,240]{1,0:T(8,128)S(1)}, f32[32,240]{1,0:T(8,128)S(1)}, u32[]{:S(2)}, u32[]{:S(2)}) collective-permute-start(f32[32,240]{1,0:T(8,128)S(1)} %join_params.3.r0), channel_id=1, source_target_pairs={{0,192},{64,0},{128,64},{192,128},{1,193},{65,1},{129,65},{193,129... | collective-permute-start | bytes 92168 | tf_op jit(solution)/shard_map/ppermute | solution.py:413
  38.7 5.4 %collective-permute-start.9 = (f32[32,240]{1,0:T(8,128)S(1)}, f32[32,240]{1,0:T(8,128)S(1)}, u32[]{:S(2)}, u32[]{:S(2)}) collective-permute-start(f32[32,240]{1,0:T(8,128)S(1)} %join_params.3.r0), channel_id=1, source_target_pairs={{0,128},{64,192},{128,0},{192,64},{1,129},{65,193},{129,1},{193,65... | collective-permute-start | bytes 92168 | tf_op jit(solution)/shard_map/ppermute | solution.py:413
  39.2 5.3 %collective-permute-start.8 = (f32[32,240]{1,0:T(8,128)S(1)}, f32[32,240]{1,0:T(8,128)S(1)}, u32[]{:S(2)}, u32[]{:S(2)}) collective-permute-start(f32[32,240]{1,0:T(8,128)S(1)} %join_params.3.r0), channel_id=1, source_target_pairs={{0,64},{64,128},{128,192},{192,0},{1,65},{65,129},{129,193},{193,1... | collective-permute-start | bytes 92168 | tf_op jit(solution)/shard_map/ppermute | solution.py:413
  46.7 29.4 %copy-start.2 = (f32[2,16,8,1024]{3,2,1,0:T(8,128)}, f32[2,16,8,1024]{3,2,1,0:T(8,128)S(1)}, u32[]{:S(2)}) copy-start(f32[2,16,8,1024]{3,2,1,0:T(8,128)S(1)} %get-tuple-element.121.es) | copy-start | bytes 3145732
  46.7 4.3 %collective-permute-start.13 = (bf16[32,1024]{1,0:T(8,128)(2,1)S(1)}, bf16[32,1024]{1,0:T(8,128)(2,1)S(1)}, u32[]{:S(2)}, u32[]{:S(2)}) collective-permute-start(bf16[32,1024]{1,0:T(8,128)(2,1)S(1)} %get-tuple-element.123), channel_id=1, source_target_pairs={{0,12},{4,0},{8,4},{12,8},{1,13},{5,1},{9,5},{13,9},{2,14},{6,2},{... | collective-permute-start | bytes 196616 | tf_op jit(solution)/shard_map/ppermute | solution.py:413
  48.2 5.8 %collective-permute-start.12 = (bf16[32,1024]{1,0:T(8,128)(2,1)S(1)}, bf16[32,1024]{1,0:T(8,128)(2,1)S(1)}, u32[]{:S(2)}, u32[]{:S(2)}) collective-permute-start(bf16[32,1024]{1,0:T(8,128)(2,1)S(1)} %get-tuple-element.123), channel_id=1, source_target_pairs={{0,8},{4,12},{8,0},{12,4},{1,9},{5,13},{9,1},{13,5},{2,10},{6,14},... | collective-permute-start | bytes 196616 | tf_op jit(solution)/shard_map/ppermute | solution.py:413
  50.5 5.5 %collective-permute-start.11 = (bf16[32,1024]{1,0:T(8,128)(2,1)S(1)}, bf16[32,1024]{1,0:T(8,128)(2,1)S(1)}, u32[]{:S(2)}, u32[]{:S(2)}) collective-permute-start(bf16[32,1024]{1,0:T(8,128)(2,1)S(1)} %get-tuple-element.123), channel_id=1, source_target_pairs={{0,4},{4,8},{8,12},{12,0},{1,5},{5,9},{9,13},{13,1},{2,6},{6,10},{... | collective-permute-start | bytes 196616 | tf_op jit(solution)/shard_map/ppermute | solution.py:413
  56.2 4.3 %collective-permute-start.16 = (bf16[32,1024]{1,0:T(8,128)(2,1)S(1)}, bf16[32,1024]{1,0:T(8,128)(2,1)S(1)}, u32[]{:S(2)}, u32[]{:S(2)}) collective-permute-start(bf16[32,1024]{1,0:T(8,128)(2,1)S(1)} %get-tuple-element.127), channel_id=1, source_target_pairs={{0,48},{16,0},{32,16},{48,32},{1,49},{17,1},{33,17},{49,33},{2,50}... | collective-permute-start | bytes 196616 | tf_op jit(solution)/shard_map/ppermute | solution.py:413
  56.3 5.3 %collective-permute-start.15 = (bf16[32,1024]{1,0:T(8,128)(2,1)S(1)}, bf16[32,1024]{1,0:T(8,128)(2,1)S(1)}, u32[]{:S(2)}, u32[]{:S(2)}) collective-permute-start(bf16[32,1024]{1,0:T(8,128)(2,1)S(1)} %get-tuple-element.127), channel_id=1, source_target_pairs={{0,32},{16,48},{32,0},{48,16},{1,33},{17,49},{33,1},{49,17},{2,34}... | collective-permute-start | bytes 196616 | tf_op jit(solution)/shard_map/ppermute | solution.py:413
  57.7 5.0 %collective-permute-start.14 = (bf16[32,1024]{1,0:T(8,128)(2,1)S(1)}, bf16[32,1024]{1,0:T(8,128)(2,1)S(1)}, u32[]{:S(2)}, u32[]{:S(2)}) collective-permute-start(bf16[32,1024]{1,0:T(8,128)(2,1)S(1)} %get-tuple-element.127), channel_id=1, source_target_pairs={{0,16},{16,32},{32,48},{48,0},{1,17},{17,33},{33,49},{49,1},{2,18}... | collective-permute-start | bytes 196616 | tf_op jit(solution)/shard_map/ppermute | solution.py:413
  62.9 13.2 %collective-permute-start.18 = (bf16[128,1536]{1,0:T(8,128)(2,1)S(1)}, bf16[128,1536]{1,0:T(8,128)(2,1)S(1)}, u32[]{:S(2)}, u32[]{:S(2)}) collective-permute-start(bf16[128,1536]{1,0:T(8,128)(2,1)S(1)} %bitcast.15), channel_id=1, source_target_pairs={{0,12},{4,8},{8,4},{12,0},{1,13},{5,9},{9,5},{13,1},{2,14},{6,10},... | collective-permute-start | bytes 1179656 | tf_op jit(solution)/shard_map/ppermute | solution.py:564
  63.9 12.1 %collective-permute-start.17 = (bf16[128,1536]{1,0:T(8,128)(2,1)S(1)}, bf16[128,1536]{1,0:T(8,128)(2,1)S(1)}, u32[]{:S(2)}, u32[]{:S(2)}) collective-permute-start(bf16[128,1536]{1,0:T(8,128)(2,1)S(1)} %bitcast.16), channel_id=1, source_target_pairs={{0,4},{4,0},{8,12},{12,8},{1,5},{5,1},{9,13},{13,9},{2,6},{6,2},{1... | collective-permute-start | bytes 1179656 | tf_op jit(solution)/shard_map/ppermute | solution.py:563
  63.9 4.3 %collective-permute-start.21 = (bf16[32,1024]{1,0:T(8,128)(2,1)S(1)}, bf16[32,1024]{1,0:T(8,128)(2,1)S(1)}, u32[]{:S(2)}, u32[]{:S(2)}) collective-permute-start(bf16[32,1024]{1,0:T(8,128)(2,1)S(1)} %get-tuple-element.129), channel_id=1, source_target_pairs={{0,192},{64,0},{128,64},{192,128},{1,193},{65,1},{129,65},{193,129... | collective-permute-start | bytes 196616 | tf_op jit(solution)/shard_map/ppermute | solution.py:413
  64.5 5.8 %collective-permute-start.20 = (bf16[32,1024]{1,0:T(8,128)(2,1)S(1)}, bf16[32,1024]{1,0:T(8,128)(2,1)S(1)}, u32[]{:S(2)}, u32[]{:S(2)}) collective-permute-start(bf16[32,1024]{1,0:T(8,128)(2,1)S(1)} %get-tuple-element.129), channel_id=1, source_target_pairs={{0,128},{64,192},{128,0},{192,64},{1,129},{65,193},{129,1},{193,65... | collective-permute-start | bytes 196616 | tf_op jit(solution)/shard_map/ppermute | solution.py:413
  65.6 5.5 %collective-permute-start.19 = (bf16[32,1024]{1,0:T(8,128)(2,1)S(1)}, bf16[32,1024]{1,0:T(8,128)(2,1)S(1)}, u32[]{:S(2)}, u32[]{:S(2)}) collective-permute-start(bf16[32,1024]{1,0:T(8,128)(2,1)S(1)} %get-tuple-element.129), channel_id=1, source_target_pairs={{0,64},{64,128},{128,192},{192,0},{1,65},{65,129},{129,193},{193,1... | collective-permute-start | bytes 196616 | tf_op jit(solution)/shard_map/ppermute | solution.py:413
  76.1 15.2 %collective-permute-start.25 = (bf16[128,1536]{1,0:T(8,128)(2,1)S(1)}, bf16[128,1536]{1,0:T(8,128)(2,1)S(1)}, u32[]{:S(2)}, u32[]{:S(2)}) collective-permute-start(bf16[128,1536]{1,0:T(8,128)(2,1)S(1)} %collective-permute-done.17.refs_1_), channel_id=1, source_target_pairs={{0,12},{4,8},{8,4},{12,0},{1,13},{5,9},{9,5},{13,1},{2,14},{6,10},... | collective-permute-start | bytes 1179656 | tf_op jit(solution)/shard_map/ppermute | solution.py:566
  85.9 19.4 %all-to-all-start = ((bf16[8,360,128]{2,1,0:T(8,128)(2,1)}), bf16[8,360,128]{2,1,0:T(8,128)(2,1)S(1)}, u32[]{:S(2)}, u32[]{:S(2)}) async-start(bf16[8,360,128]{2,1,0:T(8,128)(2,1)} %get-tuple-element.147), calls=%async_computation | async-start | bytes 1474560 | tf_op jit(solution)/shard_map/all_to_all | solution.py:640
  90.3 3.7 %collective-permute-start.22 = (bf16[128,1536]{1,0:T(8,128)(2,1)S(1)}, bf16[128,1536]{1,0:T(8,128)(2,1)S(1)}, u32[]{:S(2)}, u32[]{:S(2)}) collective-permute-start(bf16[128,1536]{1,0:T(8,128)(2,1)S(1)} %bitcast.17), channel_id=1, source_target_pairs={{0,1},{1,0},{2,3},{3,2},{4,5},{5,4},{6,7},{7,6},{8,9},{9,8},{10,11... | collective-permute-start | bytes 1179656 | tf_op jit(solution)/shard_map/ppermute | solution.py:569
  90.8 3.2 %collective-permute-start.23 = (bf16[128,1536]{1,0:T(8,128)(2,1)S(1)}, bf16[128,1536]{1,0:T(8,128)(2,1)S(1)}, u32[]{:S(2)}, u32[]{:S(2)}) collective-permute-start(bf16[128,1536]{1,0:T(8,128)(2,1)S(1)} %collective-permute-done.17.refs_1_), channel_id=1, source_target_pairs={{0,1},{1,0},{2,3},{3,2},{4,5},{5,4},{6,7},{7,6},{8,9},{9,8},{10,11... | collective-permute-start | bytes 1179656 | tf_op jit(solution)/shard_map/ppermute | solution.py:569
  90.8 3.2 %collective-permute-start.24 = (bf16[128,1536]{1,0:T(8,128)(2,1)S(1)}, bf16[128,1536]{1,0:T(8,128)(2,1)S(1)}, u32[]{:S(2)}, u32[]{:S(2)}) collective-permute-start(bf16[128,1536]{1,0:T(8,128)(2,1)S(1)} %collective-permute-done.18.refs_2_), channel_id=1, source_target_pairs={{0,1},{1,0},{2,3},{3,2},{4,5},{5,4},{6,7},{7,6},{8,9},{9,8},{10,11... | collective-permute-start | bytes 1179656 | tf_op jit(solution)/shard_map/ppermute | solution.py:569
  91.3 3.5 %collective-permute-start.26 = (bf16[128,1536]{1,0:T(8,128)(2,1)S(1)}, bf16[128,1536]{1,0:T(8,128)(2,1)S(1)}, u32[]{:S(2)}, u32[]{:S(2)}) collective-permute-start(bf16[128,1536]{1,0:T(8,128)(2,1)S(1)} %collective-permute-done.25.refs_3_), channel_id=1, source_target_pairs={{0,1},{1,0},{2,3},{3,2},{4,5},{5,4},{6,7},{7,6},{8,9},{9,8},{10,11... | collective-permute-start | bytes 1179656 | tf_op jit(solution)/shard_map/ppermute | solution.py:569
  91.3 2.6 %collective-permute-start.27 = (bf16[40,1024]{1,0:T(8,128)(2,1)S(1)}, bf16[40,1024]{1,0:T(8,128)(2,1)S(1)}, u32[]{:S(2)}, u32[]{:S(2)}) collective-permute-start(bf16[40,1024]{1,0:T(8,128)(2,1)S(1)} %get-tuple-element.139.refs_0_), channel_id=1, source_target_pairs={{0,1},{1,0},{2,3},{3,2},{4,5},{5,4},{6,7},{7,6},{8,9},{9,8},{10,11... | collective-permute-start | bytes 245768 | tf_op jit(solution)/shard_map/ppermute | solution.py:628
  94.7 10.5 %collective-permute-start.30 = (bf16[40,1024]{1,0:T(8,128)(2,1)S(1)}, bf16[40,1024]{1,0:T(8,128)(2,1)S(1)}, u32[]{:S(2)}, u32[]{:S(2)}) collective-permute-start(bf16[40,1024]{1,0:T(8,128)(2,1)S(1)} %add_parts.4.refs_0_), channel_id=1, source_target_pairs={{0,48},{16,0},{32,16},{48,32},{1,49},{17,1},{33,17},{49,33},{2,50}... | collective-permute-start | bytes 245768 | tf_op jit(solution)/shard_map/ppermute | solution.py:413
  97.3 8.0 %collective-permute-start.29 = (bf16[40,1024]{1,0:T(8,128)(2,1)S(1)}, bf16[40,1024]{1,0:T(8,128)(2,1)S(1)}, u32[]{:S(2)}, u32[]{:S(2)}) collective-permute-start(bf16[40,1024]{1,0:T(8,128)(2,1)S(1)} %add_parts.4.refs_0_), channel_id=1, source_target_pairs={{0,32},{16,48},{32,0},{48,16},{1,33},{17,49},{33,1},{49,17},{2,34}... | collective-permute-start | bytes 245768 | tf_op jit(solution)/shard_map/ppermute | solution.py:413
  97.6 7.7 %collective-permute-start.28 = (bf16[40,1024]{1,0:T(8,128)(2,1)S(1)}, bf16[40,1024]{1,0:T(8,128)(2,1)S(1)}, u32[]{:S(2)}, u32[]{:S(2)}) collective-permute-start(bf16[40,1024]{1,0:T(8,128)(2,1)S(1)} %add_parts.4.refs_0_), channel_id=1, source_target_pairs={{0,16},{16,32},{32,48},{48,0},{1,17},{17,33},{33,49},{49,1},{2,18}... | collective-permute-start | bytes 245768 | tf_op jit(solution)/shard_map/ppermute | solution.py:413
  99.3 62.6 %copy-start.8 = (f32[15,16]{1,0:T(8,128)S(1)}, f32[15,16]{1,0:T(8,128)}, u32[]{:S(2)}) copy-start(f32[15,16]{1,0:T(8,128)} %get-tuple-element.167.amp) | copy-start | bytes 2884
  109.1 15.3 %collective-permute-start.31 = (bf16[360,384]{1,0:T(8,128)(2,1)S(1)}, bf16[360,384]{1,0:T(8,128)(2,1)S(1)}, u32[]{:S(2)}, u32[]{:S(2)}) collective-permute-start(bf16[360,384]{1,0:T(8,128)(2,1)S(1)} %get-tuple-element.158), channel_id=1, source_target_pairs={{0,64},{64,128},{128,192},{192,0},{1,65},{65,129},{129,193},{193,1... | collective-permute-start | bytes 829448 | tf_op jit(solution)/shard_map/ppermute | solution.py:413
  109.2 15.2 %collective-permute-start.32 = (bf16[360,384]{1,0:T(8,128)(2,1)S(1)}, bf16[360,384]{1,0:T(8,128)(2,1)S(1)}, u32[]{:S(2)}, u32[]{:S(2)}) collective-permute-start(bf16[360,384]{1,0:T(8,128)(2,1)S(1)} %get-tuple-element.159), channel_id=1, source_target_pairs={{0,128},{64,192},{128,0},{192,64},{1,129},{65,193},{129,1},{193,65... | collective-permute-start | bytes 829448 | tf_op jit(solution)/shard_map/ppermute | solution.py:413
  111.0 14.0 %collective-permute-start.33 = (bf16[360,384]{1,0:T(8,128)(2,1)S(1)}, bf16[360,384]{1,0:T(8,128)(2,1)S(1)}, u32[]{:S(2)}, u32[]{:S(2)}) collective-permute-start(bf16[360,384]{1,0:T(8,128)(2,1)S(1)} %get-tuple-element.160), channel_id=1, source_target_pairs={{0,192},{64,0},{128,64},{192,128},{1,193},{65,1},{129,65},{193,129... | collective-permute-start | bytes 829448 | tf_op jit(solution)/shard_map/ppermute | solution.py:413
  112.6 5.2 %collective-permute-start.36 = (bf16[40,1024]{1,0:T(8,128)(2,1)S(1)}, bf16[40,1024]{1,0:T(8,128)(2,1)S(1)}, u32[]{:S(2)}, u32[]{:S(2)}) collective-permute-start(bf16[40,1024]{1,0:T(8,128)(2,1)S(1)} %add_parts.5.refs_0_), channel_id=1, source_target_pairs={{0,12},{4,0},{8,4},{12,8},{1,13},{5,1},{9,5},{13,9},{2,14},{6,2},{... | collective-permute-start | bytes 245768 | tf_op jit(solution)/shard_map/ppermute | solution.py:413
  115.7 6.5 %collective-permute-start.35 = (bf16[40,1024]{1,0:T(8,128)(2,1)S(1)}, bf16[40,1024]{1,0:T(8,128)(2,1)S(1)}, u32[]{:S(2)}, u32[]{:S(2)}) collective-permute-start(bf16[40,1024]{1,0:T(8,128)(2,1)S(1)} %add_parts.5.refs_0_), channel_id=1, source_target_pairs={{0,8},{4,12},{8,0},{12,4},{1,9},{5,13},{9,1},{13,5},{2,10},{6,14},... | collective-permute-start | bytes 245768 | tf_op jit(solution)/shard_map/ppermute | solution.py:413
  117.8 6.1 %collective-permute-start.34 = (bf16[40,1024]{1,0:T(8,128)(2,1)S(1)}, bf16[40,1024]{1,0:T(8,128)(2,1)S(1)}, u32[]{:S(2)}, u32[]{:S(2)}) collective-permute-start(bf16[40,1024]{1,0:T(8,128)(2,1)S(1)} %add_parts.5.refs_0_), channel_id=1, source_target_pairs={{0,4},{4,8},{8,12},{12,0},{1,5},{5,9},{9,13},{13,1},{2,6},{6,10},{... | collective-permute-start | bytes 245768 | tf_op jit(solution)/shard_map/ppermute | solution.py:413
  126.1 36.5 %all-to-all-start.1 = ((bf16[32,24,180]{2,1,0:T(8,128)(2,1)}), bf16[32,24,180]{2,1,0:T(8,128)(2,1)S(1)}, u32[]{:S(2)}, u32[]{:S(2)}) async-start(bf16[32,24,180]{2,1,0:T(8,128)(2,1)} %split_rows.1), calls=%async_computation.1 | async-start | bytes 786432 | tf_op jit(solution)/shard_map/all_to_all | solution.py:684
  136.1 15.7 %collective-permute-start.37 = (bf16[40,1024]{1,0:T(8,128)(2,1)S(1)}, bf16[40,1024]{1,0:T(8,128)(2,1)S(1)}, u32[]{:S(2)}, u32[]{:S(2)}) collective-permute-start(bf16[40,1024]{1,0:T(8,128)(2,1)S(1)} %add_parts.6.refs_0_), channel_id=1, source_target_pairs={{0,2},{2,0},{1,3},{3,1},{4,6},{6,4},{5,7},{7,5},{8,10},{10,8},{9,1... | collective-permute-start | bytes 245768 | tf_op jit(solution)/shard_map/ppermute | solution.py:628
  151.8 6.2 %collective-permute-start.40 = (bf16[40,1024]{1,0:T(8,128)(2,1)S(1)}, bf16[40,1024]{1,0:T(8,128)(2,1)S(1)}, u32[]{:S(2)}, u32[]{:S(2)}) collective-permute-start(bf16[40,1024]{1,0:T(8,128)(2,1)S(1)} %add_parts.7.refs_0_), channel_id=1, source_target_pairs={{0,192},{64,0},{128,64},{192,128},{1,193},{65,1},{129,65},{193,129... | collective-permute-start | bytes 245768 | tf_op jit(solution)/shard_map/ppermute | solution.py:413
  155.0 6.0 %collective-permute-start.39 = (bf16[40,1024]{1,0:T(8,128)(2,1)S(1)}, bf16[40,1024]{1,0:T(8,128)(2,1)S(1)}, u32[]{:S(2)}, u32[]{:S(2)}) collective-permute-start(bf16[40,1024]{1,0:T(8,128)(2,1)S(1)} %add_parts.7.refs_0_), channel_id=1, source_target_pairs={{0,128},{64,192},{128,0},{192,64},{1,129},{65,193},{129,1},{193,65... | collective-permute-start | bytes 245768 | tf_op jit(solution)/shard_map/ppermute | solution.py:413
  155.3 6.5 %collective-permute-start.38 = (bf16[40,1024]{1,0:T(8,128)(2,1)S(1)}, bf16[40,1024]{1,0:T(8,128)(2,1)S(1)}, u32[]{:S(2)}, u32[]{:S(2)}) collective-permute-start(bf16[40,1024]{1,0:T(8,128)(2,1)S(1)} %add_parts.7.refs_0_), channel_id=1, source_target_pairs={{0,64},{64,128},{128,192},{192,0},{1,65},{65,129},{129,193},{193,1... | collective-permute-start | bytes 245768 | tf_op jit(solution)/shard_map/ppermute | solution.py:413
  (8 other events, 65.6 us)
